TPU v7x, 32 devices: a whole 2x2x4 slice. The times are simulated.
32 devices in a mesh: dp: 8 (over z, core), tensor: 4 (over y, x).
Axes of the slice: x: 2, y: 2, z: 4, core: 2. Of those that a mesh axis runs over, the one named last changes fastest.
Arguments:
- hidden_in: bfloat16 [16384, 1024], P(('dp', 'tensor')), may hold values from -6 to 6
- norm_gain: bfloat16 [1024], P('dp'), may hold values from 0.5 to 1.5
- proj_gate: bfloat16 [1024, 2048], P('dp', 'tensor'), may hold values from -0.1875 to 0.1875
- proj_conv: bfloat16 [1024, 2048], P('dp', 'tensor'), may hold values from -0.1875 to 0.1875
- proj_state: bfloat16 [1024, 288], P('dp'), may hold values from -0.1875 to 0.1875
- conv_kernel: bfloat16 [4, 32, 64], P(None, 'tensor', 'dp'), may hold values from -3 to 3
- conv_offset: bfloat16 [32, 64], P('tensor', 'dp'), may hold values from -0.5 to 0.5
- state_kernel: bfloat16 [4, 256], P(None, 'dp'), may hold values from -3 to 3
- state_offset: bfloat16 [256], P('dp'), may hold values from -0.5 to 0.5
- step_bias: bfloat16 [32], P('dp'), may hold values from -6 to -2.5
- decay_log: bfloat16 [32], P('dp'), may hold values from -1 to 2.5
- skip_gain: bfloat16 [32], P('dp'), may hold values from 0.5 to 2
- gate_gain: bfloat16 [32, 64], P('tensor', 'dp'), may hold values from 0.5 to 1.5
- proj_out: bfloat16 [2048, 1024], P('tensor', 'dp'), may hold values from -0.125 to 0.125
- out_cotangent: bfloat16 [16384, 1024], P(('dp', 'tensor')), may hold values from -6 to 6
- seq_lengths: int32 [8, 1], P('dp'), may hold values from 1024 to 2048, as said below
Outputs:
- block_out: bfloat16 [16384, 1024], P(('dp', 'tensor'))
- grad_hidden: float32 [16384, 1024], P(('dp', 'tensor'))
- grad_norm_gain: float32 [1024], P(('dp', 'tensor'))
- grad_proj_gate: float32 [1024, 2048], P('dp', 'tensor')
- grad_proj_conv: float32 [1024, 2048], P('dp', 'tensor')
- grad_proj_state: float32 [1024, 288], P(('dp', 'tensor'))
- grad_proj_out: float32 [2048, 1024], P('tensor', 'dp')
- grad_conv_kernel: float32 [4, 32, 64], P(None, 'tensor', 'dp')
- grad_conv_offset: float32 [32, 64], P('tensor', 'dp')
- grad_state_kernel: float32 [4, 256], P(None, 'dp')
- grad_state_offset: float32 [256], P('dp')
- grad_step_bias: float32 [32], P('dp')
- grad_decay_log: float32 [32], P('dp')
- grad_skip_gain: float32 [32], P('dp')
- grad_gate_gain: float32 [32, 64], P('tensor', 'dp')
Inputs may be any that keep to these rules, and one draw needn't show every extreme that they name: `seq_lengths`: some group's lengths are all 2048 and some length is 1024; in every group the lengths sum to at most 2048.
All inputs are finite; a program needn't handle non-finite values.
Results may differ from a plain program's by a relative error of at most 0.018.
Values may be sent and summed in bfloat16 or wider, within the bound.
No kernel may reach another device: no remote copies, remote signals or barrier semaphores. Data moves between devices by JAX's collectives and lax.ppermute only.
A program may use at most 384 MiB of HBM per device.

v0:
```python
import jax
import jax.numpy as jnp
from jax import lax
from jax.sharding import PartitionSpec as P

HEADDIM = 64
STATE = 128
BLOCK = 256
INNER = 2048


epsilon = 1e-05
highest = lax.Precision.HIGHEST


def against_rows(left_matrix, right_matrix):
    return lax.dot_general(
        left_matrix, right_matrix, (((1,), (1,)), ((), ())), preferred_element_type=jnp.float32
    )


def along_rows(left_matrix, right_matrix):
    return lax.dot_general(
        left_matrix, right_matrix, (((0,), (0,)), ((), ())), preferred_element_type=jnp.float32
    )


def segments(lengths, tokens):
    seq_ends = jnp.cumsum(lengths)
    places = jnp.arange(tokens, dtype=jnp.int32)
    passed = places[:, None] >= seq_ends[None, :]
    segment = jnp.sum(passed.astype(jnp.int32), axis=1)
    starts = jnp.max(
        jnp.where(passed, seq_ends[None, :], jnp.zeros_like(seq_ends)[None, :]), axis=1
    )
    return (places, starts, segment)


def conv_silu(values, kernel, offset, places, starts):
    taps = kernel.shape[0]
    result = offset[None, :] + kernel[taps - 1][None, :] * values
    for lag_steps in range(1, taps):
        shifted = jnp.concatenate(
            [jnp.zeros((lag_steps, values.shape[1]), values.dtype), values[:-lag_steps]], axis=0
        )
        usable = (places - lag_steps >= starts)[:, None]
        result = result + kernel[taps - 1 - lag_steps][None, :] * jnp.where(
            usable, shifted, jnp.zeros_like(shifted)
        )
    return jax.nn.silu(result)


def block_scan(inputs_x, b_rows, c_rows, log_decay, step_size, skip_head, segment, block_size):
    tokens, head_count, head_width = inputs_x.shape
    block_count = tokens // block_size
    states = b_rows.shape[1]
    stacked = (
        inputs_x.reshape(block_count, block_size, head_count, head_width),
        b_rows.reshape(block_count, block_size, states),
        c_rows.reshape(block_count, block_size, states),
        log_decay.reshape(block_count, block_size, head_count),
        step_size.reshape(block_count, block_size, head_count),
        segment.reshape(block_count, block_size),
    )
    lower_mask = jnp.arange(block_size)[:, None] >= jnp.arange(block_size)[None, :]

    def advance(carry_in, block_inputs):
        carry_state, last_segment = carry_in
        block_x, block_b, block_c, block_decay, block_step, block_segment = block_inputs
        cumulative = jnp.cumsum(block_decay, axis=0).T
        pair_mask = ((block_segment[:, None] == block_segment[None, :]) & lower_mask)[None, :, :]
        spread = cumulative[:, :, None] - cumulative[:, None, :]
        kernel = jnp.where(pair_mask, jnp.exp(jnp.where(pair_mask, spread, 0.0)), 0.0)
        gram_matrix = jnp.dot(block_c, block_b.T, precision=highest)
        mixing = kernel * gram_matrix[None, :, :] * block_step.T[:, None, :]
        inner_y = jnp.einsum("hij,jhp->ihp", mixing, block_x, precision=highest)
        follows = (block_segment == last_segment).astype(carry_state.dtype)
        carried = follows[:, None] * jnp.exp(cumulative.T)
        outer_y = (
            jnp.einsum("is,hps->ihp", block_c, carry_state, precision=highest) * carried[:, :, None]
        )
        result = inner_y + outer_y + skip_head[None, :, None] * block_x
        tail_segment = block_segment[-1]
        ending = cumulative[:, -1]
        keep_weight = (
            (block_segment == tail_segment).astype(carry_state.dtype)[:, None]
            * jnp.exp(ending[None, :] - cumulative.T)
            * block_step
        )
        fresh_state = jnp.einsum(
            "jhp,js->hps", keep_weight[:, :, None] * block_x, block_b, precision=highest
        )
        survive = jnp.where(tail_segment == last_segment, jnp.exp(ending), jnp.zeros_like(ending))
        carry_state = carry_state * survive[:, None, None] + fresh_state
        return ((carry_state, tail_segment), result)

    start_state = jnp.zeros((head_count, head_width, states), inputs_x.dtype)
    final_carry, outputs = lax.scan(advance, (start_state, jnp.array(-1, jnp.int32)), stacked)
    return outputs.reshape(tokens, head_count * head_width)


def state_mixer(
    conv_in,
    state_in,
    step_in,
    conv_kernel,
    conv_offset,
    state_kernel,
    state_offset,
    step_bias,
    decay_log,
    skip_gain,
    head_start,
    places,
    starts,
    segment,
):
    channels = conv_in.shape[1]
    heads_here = channels // HEADDIM
    conv_out = conv_silu(conv_in, conv_kernel, conv_offset, places, starts)
    state_out = conv_silu(state_in, state_kernel, state_offset, places, starts)
    raw_step = (
        lax.dynamic_slice_in_dim(step_in, head_start, heads_here, 1)
        + lax.dynamic_slice_in_dim(step_bias, head_start, heads_here, 0)[None, :]
    )
    step_size = jax.nn.softplus(raw_step)
    decay_rates = jnp.exp(lax.dynamic_slice_in_dim(decay_log, head_start, heads_here, 0))
    skip_head = lax.dynamic_slice_in_dim(skip_gain, head_start, heads_here, 0)
    return block_scan(
        conv_out.reshape(conv_out.shape[0], heads_here, HEADDIM),
        state_out[:, :STATE],
        state_out[:, STATE:],
        -decay_rates[None, :] * step_size,
        step_size,
        skip_head,
        segment,
        BLOCK,
    )


def per_device(
    hidden_in,
    norm_gain,
    proj_gate,
    proj_conv,
    proj_state,
    conv_kernel,
    conv_offset,
    state_kernel,
    state_offset,
    step_bias,
    decay_log,
    skip_gain,
    gate_gain,
    proj_out,
    out_cotangent,
    seq_lengths,
):
    tensor_count = lax.axis_size("tensor")
    tensor_place = lax.axis_index("tensor")
    gathered = (
        lax.all_gather(norm_gain, "dp", axis=0, tiled=True),
        lax.all_gather(proj_gate, "dp", axis=0, tiled=True),
        lax.all_gather(proj_conv, "dp", axis=0, tiled=True),
        lax.all_gather(proj_state, "dp", axis=0, tiled=True),
        lax.all_gather(conv_kernel, "dp", axis=2, tiled=True),
        lax.all_gather(conv_offset, "dp", axis=1, tiled=True),
        lax.all_gather(state_kernel, "dp", axis=1, tiled=True),
        lax.all_gather(state_offset, "dp", axis=0, tiled=True),
        lax.all_gather(step_bias, "dp", axis=0, tiled=True),
        lax.all_gather(decay_log, "dp", axis=0, tiled=True),
        lax.all_gather(skip_gain, "dp", axis=0, tiled=True),
        lax.all_gather(gate_gain, "dp", axis=1, tiled=True),
        lax.all_gather(proj_out, "dp", axis=1, tiled=True),
    )
    (
        gain_full,
        gate_cols,
        conv_cols,
        state_cols,
        kernel_part,
        offset_part,
        kernel_state,
        offset_state,
        bias_step,
        rate_log,
        skip_full,
        gain_part,
        out_weight,
    ) = gathered
    row_count = hidden_in.shape[0]
    group_rows = row_count * tensor_count
    channels = gate_cols.shape[1]
    heads_here = channels // HEADDIM
    head_start = tensor_place * heads_here
    places, starts, segment = segments(seq_lengths[0], group_rows)
    values = hidden_in.astype(jnp.float32)
    inverse_in = lax.rsqrt(jnp.mean(values * values, axis=1, keepdims=True) + epsilon)
    scaled = values * inverse_in
    gain_in = gain_full.astype(jnp.float32)
    normed = (scaled * gain_in[None, :]).astype(jnp.bfloat16)
    normed_all = lax.all_gather(normed, "tensor", axis=0, tiled=True)
    weights_in = jnp.concatenate([gate_cols, conv_cols, state_cols], axis=1)
    projected = jnp.dot(normed_all, weights_in, preferred_element_type=jnp.float32)
    gate_pre = projected[:, :channels]
    conv_pre = projected[:, channels : 2 * channels]
    state_pre = projected[:, 2 * channels : 2 * channels + 2 * STATE]
    step_pre = projected[:, 2 * channels + 2 * STATE :]
    kernel_count = kernel_part.shape[0]

    def local_mixer(
        conv_in,
        state_in,
        step_in,
        kernel_conv,
        offset_conv,
        kernel_maps,
        offset_maps,
        step_offset,
        log_rates,
        skip_heads,
    ):
        return state_mixer(
            conv_in,
            state_in,
            step_in,
            kernel_conv,
            offset_conv,
            kernel_maps,
            offset_maps,
            step_offset,
            log_rates,
            skip_heads,
            head_start,
            places,
            starts,
            segment,
        )

    mixed_out, mixer_back = jax.vjp(
        local_mixer,
        conv_pre,
        state_pre,
        step_pre,
        kernel_part.astype(jnp.float32).reshape(kernel_count, channels),
        offset_part.astype(jnp.float32).reshape(channels),
        kernel_state.astype(jnp.float32),
        offset_state.astype(jnp.float32),
        bias_step.astype(jnp.float32),
        rate_log.astype(jnp.float32),
        skip_full.astype(jnp.float32),
    )
    gate_act = jax.nn.silu(gate_pre)
    gated_in = mixed_out * gate_act
    square_sum = lax.psum(jnp.sum(gated_in * gated_in, axis=1), "tensor")
    inverse_gate = lax.rsqrt(square_sum / INNER + epsilon)[:, None]
    gate_hat = gated_in * inverse_gate
    gain_gate = gain_part.astype(jnp.float32).reshape(channels)
    gated_out = (gate_hat * gain_gate[None, :]).astype(jnp.bfloat16)
    branch_out = lax.psum_scatter(
        jnp.dot(gated_out, out_weight, preferred_element_type=jnp.float32).astype(jnp.bfloat16),
        "tensor",
        scatter_dimension=0,
        tiled=True,
    ).astype(jnp.float32)
    block_out = (values + branch_out).astype(jnp.bfloat16)
    cotangent_all = lax.all_gather(out_cotangent, "tensor", axis=0, tiled=True)
    grad_gated = against_rows(cotangent_all, out_weight)
    grad_out_proj = along_rows(gated_out, cotangent_all)
    grad_gain_gate = jnp.sum(grad_gated * gate_hat, axis=0).reshape(heads_here, HEADDIM)
    grad_hat = grad_gated * gain_gate[None, :]
    inner_sum = lax.psum(jnp.sum(grad_hat * gate_hat, axis=1), "tensor")
    grad_inner = inverse_gate * (grad_hat - gate_hat * (inner_sum / INNER)[:, None])
    grad_mixed = grad_inner * gate_act
    sigmoid_gate = jax.nn.sigmoid(gate_pre)
    grad_gate_pre = grad_inner * mixed_out * sigmoid_gate * (1.0 + gate_pre * (1.0 - sigmoid_gate))
    mixer_grads = mixer_back(grad_mixed)
    state_part = jnp.concatenate([mixer_grads[1], mixer_grads[2]], axis=1)
    own_state = lax.psum_scatter(
        state_part.astype(jnp.bfloat16), "tensor", scatter_dimension=0, tiled=True
    )
    shared = lax.psum(
        (mixer_grads[5], mixer_grads[6], mixer_grads[7], mixer_grads[8], mixer_grads[9]), "tensor"
    )
    gate_bf = grad_gate_pre.astype(jnp.bfloat16)
    conv_bf = mixer_grads[0].astype(jnp.bfloat16)
    grad_normed = lax.psum_scatter(
        (against_rows(gate_bf, gate_cols) + against_rows(conv_bf, conv_cols)).astype(jnp.bfloat16),
        "tensor",
        scatter_dimension=0,
        tiled=True,
    ).astype(jnp.float32)
    grad_normed = grad_normed + against_rows(own_state, state_cols)
    grad_gain_in = jnp.sum(grad_normed * scaled, axis=0)
    grad_scaled = grad_normed * gain_in[None, :]
    grad_hidden = out_cotangent.astype(jnp.float32) + inverse_in * (
        grad_scaled - scaled * jnp.mean(grad_scaled * scaled, axis=1, keepdims=True)
    )
    row_terms = (
        lax.psum_scatter(grad_gain_in, ("dp", "tensor"), scatter_dimension=0, tiled=True),
        lax.psum_scatter(
            along_rows(normed, own_state), ("dp", "tensor"), scatter_dimension=0, tiled=True
        ),
    )
    weight_terms = (
        lax.psum_scatter(
            along_rows(normed_all, gate_bf).astype(jnp.bfloat16),
            "dp",
            scatter_dimension=0,
            tiled=True,
        ).astype(jnp.float32),
        lax.psum_scatter(
            along_rows(normed_all, conv_bf).astype(jnp.bfloat16),
            "dp",
            scatter_dimension=0,
            tiled=True,
        ).astype(jnp.float32),
        lax.psum_scatter(
            grad_out_proj.astype(jnp.bfloat16), "dp", scatter_dimension=1, tiled=True
        ).astype(jnp.float32),
        lax.psum_scatter(
            mixer_grads[3].reshape(kernel_count, heads_here, HEADDIM).astype(jnp.bfloat16),
            "dp",
            scatter_dimension=2,
            tiled=True,
        ).astype(jnp.float32),
        lax.psum_scatter(
            mixer_grads[4].reshape(heads_here, HEADDIM).astype(jnp.bfloat16),
            "dp",
            scatter_dimension=1,
            tiled=True,
        ).astype(jnp.float32),
        lax.psum_scatter(
            shared[0].astype(jnp.bfloat16), "dp", scatter_dimension=1, tiled=True
        ).astype(jnp.float32),
        lax.psum_scatter(
            shared[1].astype(jnp.bfloat16), "dp", scatter_dimension=0, tiled=True
        ).astype(jnp.float32),
        lax.psum_scatter(
            shared[2].astype(jnp.bfloat16), "dp", scatter_dimension=0, tiled=True
        ).astype(jnp.float32),
        lax.psum_scatter(
            shared[3].astype(jnp.bfloat16), "dp", scatter_dimension=0, tiled=True
        ).astype(jnp.float32),
        lax.psum_scatter(
            shared[4].astype(jnp.bfloat16), "dp", scatter_dimension=0, tiled=True
        ).astype(jnp.float32),
        lax.psum_scatter(
            grad_gain_gate.astype(jnp.bfloat16), "dp", scatter_dimension=1, tiled=True
        ).astype(jnp.float32),
    )
    return (
        block_out,
        grad_hidden,
        row_terms[0],
        weight_terms[0],
        weight_terms[1],
        row_terms[1],
        weight_terms[2],
        weight_terms[3],
        weight_terms[4],
        weight_terms[5],
        weight_terms[6],
        weight_terms[7],
        weight_terms[8],
        weight_terms[9],
        weight_terms[10],
    )


def solution(mesh):
    placed = (
        P(("dp", "tensor"), None),
        P("dp"),
        P("dp", "tensor"),
        P("dp", "tensor"),
        P("dp", None),
        P(None, "tensor", "dp"),
        P("tensor", "dp"),
        P(None, "dp"),
        P("dp"),
        P("dp"),
        P("dp"),
        P("dp"),
        P("tensor", "dp"),
        P("tensor", "dp"),
        P(("dp", "tensor"), None),
        P("dp", None),
    )
    return jax.shard_map(
        per_device,
        mesh=mesh,
        in_specs=placed,
        out_specs=(
            P(("dp", "tensor"), None),
            P(("dp", "tensor"), None),
            P(("dp", "tensor")),
            P("dp", "tensor"),
            P("dp", "tensor"),
            P(("dp", "tensor"), None),
            P("tensor", "dp"),
            P(None, "tensor", "dp"),
            P("tensor", "dp"),
            P(None, "dp"),
            P("dp"),
            P("dp"),
            P("dp"),
            P("dp"),
            P("tensor", "dp"),
        ),
        check_vma=False,
    )
```

profile of v0, /device:TPU:0, one launch (start us, length us, event | category | flops | bytes accessed | tf_op | source)
XLA Modules:
  0.0 1230.4 jit_solution(1454590304400421335)
XLA Ops:
  8.8 13.5 %all-gather = bf16[8,1,128]{2,1,0:T(2,128)(2,1)S(1)} all-gather(bf16[1,1,128]{2,1,0:T(2,128)(2,1)} %bitcast.553), channel_id=1, replica_groups=mesh['dp'=8,'tensor'=4] {'dp'}, dimensions={0}, use_global_device_ids=true | all-gather | bytes 2304 | tf_op jit(solution)/shard_map/all_gather | solution.py:162
  30.8 13.9 %all-reduce.37 = (bf16[32]{0:T(256)(128)(2,1)S(1)}, bf16[32]{0:T(256)(128)(2,1)S(1)}, bf16[256]{0:T(256)(128)(2,1)S(1)}, bf16[32]{0:T(256)(128)(2,1)S(1)}) all-reduce(bf16[32]{0:T(256)(128)(2,1)S(1)} %dynamic-update-slice.1, bf16[32]{0:T(256)(128)(2,1)S(1)} %dynamic-update-slice, ...), channel_id=1, replica_groups=mesh['dp'=8,'tensor'=4] {'dp'}, use_global_device_ids=true, to_apply=%add.24 | all-reduce | flops 352 | bytes 1408
  44.7 16.9 %all_gather.50 = bf16[1024,288]{0,1:T(8,128)(2,1)S(1)} all-gather(bf16[128,288]{0,1:T(8,128)(2,1)S(1)} %copy-done.19), channel_id=1, replica_groups=mesh['dp'=8,'tensor'=4] {'dp'}, dimensions={0}, use_global_device_ids=true | all-gather | bytes 663552 | tf_op jit(solution)/shard_map/all_gather | solution.py:165
  62.7 9.0 all-gather.1
  72.1 14.0 %all_gather.53 = bf16[4,8,64]{1,0,2:T(4,128)(2,1)S(1)} all-gather(bf16[4,8,8]{1,0,2:T(4,128)(2,1)S(1)} %copy.167), channel_id=1, replica_groups=mesh['dp'=8,'tensor'=4] {'dp'}, dimensions={2}, use_global_device_ids=true | all-gather | bytes 4608 | tf_op jit(solution)/shard_map/all_gather | solution.py:166
  86.8 12.7 %all_gather.52 = bf16[8,64]{0,1:T(8,128)(2,1)S(1)} all-gather(bf16[8,8]{0,1:T(8,128)(2,1)S(1)} %copy.165), channel_id=1, replica_groups=mesh['dp'=8,'tensor'=4] {'dp'}, dimensions={1}, use_global_device_ids=true | all-gather | bytes 1152 | tf_op jit(solution)/shard_map/all_gather | solution.py:167
  99.9 12.7 %all_gather.57 = bf16[8,64]{0,1:T(8,128)(2,1)S(1)} all-gather(bf16[8,8]{0,1:T(8,128)(2,1)S(1)} %copy.177), channel_id=1, replica_groups=mesh['dp'=8,'tensor'=4] {'dp'}, dimensions={1}, use_global_device_ids=true | all-gather | bytes 1152 | tf_op jit(solution)/shard_map/all_gather | solution.py:173
  115.7 8.4 fusion.150
  139.4 9.2 fusion.145
  156.2 290.3 %while.89 = (s32[]{:T(128)}, f32[8,64,128]{2,1,0:T(8,128)S(1)}, s32[]{:T(128)}, f32[8,256,8,64]{1,0,3,2:T(8,128)}, pred[8,8,256,256]{3,2,1,0:T(32,128)(4,1)}, /*...) while((s32[]{:T(128)}, f32[8,64,128]{2,1,0:T(8,128)S(1)}, ...), condition=%wide.region_4.5_spmd.clone, body=%wide.region_1.0_spmd.clone.sunk | while | flops 912799808 | bytes 19398264 | solution.py:98
  161.6 4.1 multiply_dynamic-update-slice_fusion.5
  171.4 12.7 %dynamic_update_slice.325 = f32[8,256,8,64]{1,0,3,2:T(8,128)} dynamic-update-slice(f32[8,256,8,64]{1,0,3,2:T(8,128)} %get-tuple-element.2612, f32[1,256,8,64]{1,0,3,2:T(1,128)S(1)} %copy.284, s32[]{:T(128)} %get-tuple-element.2609, s32[]{:T(128)} %constant.240.clone.1..sunk, s32[]{:T(128)} %constant.240.clone.1..sunk, s32[]{:T(128)} %constant.240.clone.1..sunk) | dynamic-update-slice | bytes 1048580 | tf_op jit(solution)/shard_map/jvp()/while/body/jit(dynamic_update_index_in_dim)/dynamic_update_slice | solution.py:98
  197.8 4.2 multiply_dynamic-update-slice_fusion.5
  207.7 12.7 %dynamic_update_slice.325 = f32[8,256,8,64]{1,0,3,2:T(8,128)} dynamic-update-slice(f32[8,256,8,64]{1,0,3,2:T(8,128)} %get-tuple-element.2612, f32[1,256,8,64]{1,0,3,2:T(1,128)S(1)} %copy.284, s32[]{:T(128)} %get-tuple-element.2609, s32[]{:T(128)} %constant.240.clone.1..sunk, s32[]{:T(128)} %constant.240.clone.1..sunk, s32[]{:T(128)} %constant.240.clone.1..sunk) | dynamic-update-slice | bytes 1048580 | tf_op jit(solution)/shard_map/jvp()/while/body/jit(dynamic_update_index_in_dim)/dynamic_update_slice | solution.py:98
  234.0 4.1 multiply_dynamic-update-slice_fusion.5
  243.9 12.7 %dynamic_update_slice.325 = f32[8,256,8,64]{1,0,3,2:T(8,128)} dynamic-update-slice(f32[8,256,8,64]{1,0,3,2:T(8,128)} %get-tuple-element.2612, f32[1,256,8,64]{1,0,3,2:T(1,128)S(1)} %copy.284, s32[]{:T(128)} %get-tuple-element.2609, s32[]{:T(128)} %constant.240.clone.1..sunk, s32[]{:T(128)} %constant.240.clone.1..sunk, s32[]{:T(128)} %constant.240.clone.1..sunk) | dynamic-update-slice | bytes 1048580 | tf_op jit(solution)/shard_map/jvp()/while/body/jit(dynamic_update_index_in_dim)/dynamic_update_slice | solution.py:98
  270.3 4.1 multiply_dynamic-update-slice_fusion.5
  280.0 12.7 %dynamic_update_slice.325 = f32[8,256,8,64]{1,0,3,2:T(8,128)} dynamic-update-slice(f32[8,256,8,64]{1,0,3,2:T(8,128)} %get-tuple-element.2612, f32[1,256,8,64]{1,0,3,2:T(1,128)S(1)} %copy.284, s32[]{:T(128)} %get-tuple-element.2609, s32[]{:T(128)} %constant.240.clone.1..sunk, s32[]{:T(128)} %constant.240.clone.1..sunk, s32[]{:T(128)} %constant.240.clone.1..sunk) | dynamic-update-slice | bytes 1048580 | tf_op jit(solution)/shard_map/jvp()/while/body/jit(dynamic_update_index_in_dim)/dynamic_update_slice | solution.py:98
  306.3 4.3 multiply_dynamic-update-slice_fusion.5
  316.3 12.7 %dynamic_update_slice.325 = f32[8,256,8,64]{1,0,3,2:T(8,128)} dynamic-update-slice(f32[8,256,8,64]{1,0,3,2:T(8,128)} %get-tuple-element.2612, f32[1,256,8,64]{1,0,3,2:T(1,128)S(1)} %copy.284, s32[]{:T(128)} %get-tuple-element.2609, s32[]{:T(128)} %constant.240.clone.1..sunk, s32[]{:T(128)} %constant.240.clone.1..sunk, s32[]{:T(128)} %constant.240.clone.1..sunk) | dynamic-update-slice | bytes 1048580 | tf_op jit(solution)/shard_map/jvp()/while/body/jit(dynamic_update_index_in_dim)/dynamic_update_slice | solution.py:98
  352.5 12.7 %dynamic_update_slice.325 = f32[8,256,8,64]{1,0,3,2:T(8,128)} dynamic-update-slice(f32[8,256,8,64]{1,0,3,2:T(8,128)} %get-tuple-element.2612, f32[1,256,8,64]{1,0,3,2:T(1,128)S(1)} %copy.284, s32[]{:T(128)} %get-tuple-element.2609, s32[]{:T(128)} %constant.240.clone.1..sunk, s32[]{:T(128)} %constant.240.clone.1..sunk, s32[]{:T(128)} %constant.240.clone.1..sunk) | dynamic-update-slice | bytes 1048580 | tf_op jit(solution)/shard_map/jvp()/while/body/jit(dynamic_update_index_in_dim)/dynamic_update_slice | solution.py:98
  378.9 4.3 multiply_dynamic-update-slice_fusion.5
  389.0 12.7 %dynamic_update_slice.325 = f32[8,256,8,64]{1,0,3,2:T(8,128)} dynamic-update-slice(f32[8,256,8,64]{1,0,3,2:T(8,128)} %get-tuple-element.2612, f32[1,256,8,64]{1,0,3,2:T(1,128)S(1)} %copy.284, s32[]{:T(128)} %get-tuple-element.2609, s32[]{:T(128)} %constant.240.clone.1..sunk, s32[]{:T(128)} %constant.240.clone.1..sunk, s32[]{:T(128)} %constant.240.clone.1..sunk) | dynamic-update-slice | bytes 1048580 | tf_op jit(solution)/shard_map/jvp()/while/body/jit(dynamic_update_index_in_dim)/dynamic_update_slice | solution.py:98
  415.4 4.0 multiply_dynamic-update-slice_fusion.5
  425.1 12.7 %dynamic_update_slice.325 = f32[8,256,8,64]{1,0,3,2:T(8,128)} dynamic-update-slice(f32[8,256,8,64]{1,0,3,2:T(8,128)} %get-tuple-element.2612, f32[1,256,8,64]{1,0,3,2:T(1,128)S(1)} %copy.284, s32[]{:T(128)} %get-tuple-element.2609, s32[]{:T(128)} %constant.240.clone.1..sunk, s32[]{:T(128)} %constant.240.clone.1..sunk, s32[]{:T(128)} %constant.240.clone.1..sunk) | dynamic-update-slice | bytes 1048580 | tf_op jit(solution)/shard_map/jvp()/while/body/jit(dynamic_update_index_in_dim)/dynamic_update_slice | solution.py:98
  446.5 4.1 copy.251
  450.7 7.0 multiply_reduce_fusion.6
  457.7 9.1 psum.49
  466.8 9.1 multiply_reduce_fusion
  475.9 8.9 psum.50
  484.9 8.3 fusion.169
  501.7 330.7 %while.90 = (s32[]{:T(128)}, f32[8]{0:T(128)S(1)}, f32[8,64,128]{2,1,0:T(8,128)S(1)}, f32[8,256,8,64]{1,0,3,2:T(8,128)}, f32[8,256,128]{2,1,0:T(8,128)}, /*index...) while((s32[]{:T(128)}, f32[8]{0:T(128)S(1)}, ...), condition=%wide.region_22.23_spmd.clone, body=%wide.region_10.22_spmd.clone.sunk | while | flops 1820084224 | bytes 23877688 | solution.py:98
  510.1 6.1 fusion.263
  522.6 12.7 %dynamic_update_slice.331 = f32[8,256,8,64]{1,0,3,2:T(8,128)} dynamic-update-slice(f32[8,256,8,64]{1,0,3,2:T(8,128)} %get-tuple-element.2723, f32[1,256,8,64]{1,0,3,2:T(1,128)S(1)} %copy.289, s32[]{:T(128)S(6)} %sub.252, s32[]{:T(128)} %constant.240.clone.1..sunk.1, s32[]{:T(128)} %constant.240.clone.1..sunk.1, s32[]{:T(128)} %constant.240.clone.1..sunk.1) | dynamic-update-slice | bytes 1048580 | tf_op jit(solution)/shard_map/transpose(jvp())/while/body/jit(dynamic_update_index_in_dim)/dynamic_update_slice | solution.py:98
  551.4 6.1 fusion.263
  563.9 12.7 %dynamic_update_slice.331 = f32[8,256,8,64]{1,0,3,2:T(8,128)} dynamic-update-slice(f32[8,256,8,64]{1,0,3,2:T(8,128)} %get-tuple-element.2723, f32[1,256,8,64]{1,0,3,2:T(1,128)S(1)} %copy.289, s32[]{:T(128)S(6)} %sub.252, s32[]{:T(128)} %constant.240.clone.1..sunk.1, s32[]{:T(128)} %constant.240.clone.1..sunk.1, s32[]{:T(128)} %constant.240.clone.1..sunk.1) | dynamic-update-slice | bytes 1048580 | tf_op jit(solution)/shard_map/transpose(jvp())/while/body/jit(dynamic_update_index_in_dim)/dynamic_update_slice | solution.py:98
  592.7 6.1 fusion.263
  605.2 12.7 %dynamic_update_slice.331 = f32[8,256,8,64]{1,0,3,2:T(8,128)} dynamic-update-slice(f32[8,256,8,64]{1,0,3,2:T(8,128)} %get-tuple-element.2723, f32[1,256,8,64]{1,0,3,2:T(1,128)S(1)} %copy.289, s32[]{:T(128)S(6)} %sub.252, s32[]{:T(128)} %constant.240.clone.1..sunk.1, s32[]{:T(128)} %constant.240.clone.1..sunk.1, s32[]{:T(128)} %constant.240.clone.1..sunk.1) | dynamic-update-slice | bytes 1048580 | tf_op jit(solution)/shard_map/transpose(jvp())/while/body/jit(dynamic_update_index_in_dim)/dynamic_update_slice | solution.py:98
  634.0 6.1 fusion.263
  646.5 12.7 %dynamic_update_slice.331 = f32[8,256,8,64]{1,0,3,2:T(8,128)} dynamic-update-slice(f32[8,256,8,64]{1,0,3,2:T(8,128)} %get-tuple-element.2723, f32[1,256,8,64]{1,0,3,2:T(1,128)S(1)} %copy.289, s32[]{:T(128)S(6)} %sub.252, s32[]{:T(128)} %constant.240.clone.1..sunk.1, s32[]{:T(128)} %constant.240.clone.1..sunk.1, s32[]{:T(128)} %constant.240.clone.1..sunk.1) | dynamic-update-slice | bytes 1048580 | tf_op jit(solution)/shard_map/transpose(jvp())/while/body/jit(dynamic_update_index_in_dim)/dynamic_update_slice | solution.py:98
  675.3 6.1 fusion.263
  687.8 12.7 %dynamic_update_slice.331 = f32[8,256,8,64]{1,0,3,2:T(8,128)} dynamic-update-slice(f32[8,256,8,64]{1,0,3,2:T(8,128)} %get-tuple-element.2723, f32[1,256,8,64]{1,0,3,2:T(1,128)S(1)} %copy.289, s32[]{:T(128)S(6)} %sub.252, s32[]{:T(128)} %constant.240.clone.1..sunk.1, s32[]{:T(128)} %constant.240.clone.1..sunk.1, s32[]{:T(128)} %constant.240.clone.1..sunk.1) | dynamic-update-slice | bytes 1048580 | tf_op jit(solution)/shard_map/transpose(jvp())/while/body/jit(dynamic_update_index_in_dim)/dynamic_update_slice | solution.py:98
  716.7 6.1 fusion.263
  729.2 12.7 %dynamic_update_slice.331 = f32[8,256,8,64]{1,0,3,2:T(8,128)} dynamic-update-slice(f32[8,256,8,64]{1,0,3,2:T(8,128)} %get-tuple-element.2723, f32[1,256,8,64]{1,0,3,2:T(1,128)S(1)} %copy.289, s32[]{:T(128)S(6)} %sub.252, s32[]{:T(128)} %constant.240.clone.1..sunk.1, s32[]{:T(128)} %constant.240.clone.1..sunk.1, s32[]{:T(128)} %constant.240.clone.1..sunk.1) | dynamic-update-slice | bytes 1048580 | tf_op jit(solution)/shard_map/transpose(jvp())/while/body/jit(dynamic_update_index_in_dim)/dynamic_update_slice | solution.py:98
  758.0 6.1 fusion.263
  770.5 12.7 %dynamic_update_slice.331 = f32[8,256,8,64]{1,0,3,2:T(8,128)} dynamic-update-slice(f32[8,256,8,64]{1,0,3,2:T(8,128)} %get-tuple-element.2723, f32[1,256,8,64]{1,0,3,2:T(1,128)S(1)} %copy.289, s32[]{:T(128)S(6)} %sub.252, s32[]{:T(128)} %constant.240.clone.1..sunk.1, s32[]{:T(128)} %constant.240.clone.1..sunk.1, s32[]{:T(128)} %constant.240.clone.1..sunk.1) | dynamic-update-slice | bytes 1048580 | tf_op jit(solution)/shard_map/transpose(jvp())/while/body/jit(dynamic_update_index_in_dim)/dynamic_update_slice | solution.py:98
  799.3 6.1 fusion.263
  811.8 12.7 %dynamic_update_slice.331 = f32[8,256,8,64]{1,0,3,2:T(8,128)} dynamic-update-slice(f32[8,256,8,64]{1,0,3,2:T(8,128)} %get-tuple-element.2723, f32[1,256,8,64]{1,0,3,2:T(1,128)S(1)} %copy.289, s32[]{:T(128)S(6)} %sub.252, s32[]{:T(128)} %constant.240.clone.1..sunk.1, s32[]{:T(128)} %constant.240.clone.1..sunk.1, s32[]{:T(128)} %constant.240.clone.1..sunk.1) | dynamic-update-slice | bytes 1048580 | tf_op jit(solution)/shard_map/transpose(jvp())/while/body/jit(dynamic_update_index_in_dim)/dynamic_update_slice | solution.py:98
  837.2 5.4 fusion.179
  848.9 15.5 %all-reduce.35 = (bf16[4,256]{1,0:T(4,128)(2,1)S(1)}, bf16[256]{0:T(256)(128)(2,1)S(1)}, bf16[32]{0:T(256)(128)(2,1)S(1)}, bf16[32]{0:T(256)(128)(2,1)S(1)}, bf16[32]{0:T(256)(128)(2,1)S(1)}) all-reduce(f32[4,256]{1,0:T(4,128)S(1)} %pad_add_fusion, f32[256]{0:T(256)S(1)} %get-tuple-element.1877, ...), channel_id=1, replica_groups=mesh['dp'=8,'tensor'=4] {'tensor'}, use_global_device_ids=true, to_apply=%region_43.44 | all-reduce | flops 1376 | bytes 8256 | tf_op jit(solution)/shard_map/psum | solution.py:282
  865.1 6.1 copy.253
  871.3 11.4 fusion.178
  901.6 6.3 convolution_convert_fusion.3
  908.0 4.1 fusion.190
  912.2 4.6 add_convert_fusion
  918.0 6.6 convolution_convert_fusion
  927.0 26.3 %all-reduce.36 = (bf16[4,8,64]{2,1,0:T(8,128)(2,1)S(1)}, bf16[8,64]{1,0:T(8,128)(2,1)S(1)}, bf16[256]{0:T(256)(128)(2,1)S(1)}, bf16[32]{0:T(256)(128)(2,1)S(1)},...) all-reduce(bf16[4,8,64]{2,1,0:T(8,128)(2,1)S(1)} %convert_element_t, ...), channel_id=10, replica_groups=mesh['dp'=8,'tensor'=4] {'dp'}, use_global_device_ids=true, to_apply=%region_36.37.clone | all-reduce | flops 3424 | bytes 13696
  963.9 11.9 reduce-scatter.24.cloned.1.call-done
  977.4 31.9 %reduce-scatter.22.cloned.1.call-done = bf16[128,512]{1,0:T(8,128)(2,1)} async-done(((bf16[1024,512]{1,0:T(8,128)(2,1)}), bf16[128,512]{1,0:T(8,128)(2,1)}) %reduce-scatter.22.cloned.1.call-update) | async-done | bytes 131088 | tf_op jit(solution)/shard_map/reduce_scatter | solution.py:306
  1010.9 52.8 %reduce-scatter.18.cloned.1.call-done = bf16[512,1024]{1,0:T(8,128)(2,1)} async-done(((bf16[2048,1024]{1,0:T(8,128)(2,1)}), bf16[512,1024]{1,0:T(8,128)(2,1)}) %reduce-scatter.18.cloned.1.call-update) | async-done | bytes 1048592 | tf_op jit(solution)/shard_map/reduce_scatter | solution.py:287
  1067.3 39.5 %all-reduce.27 = f32[1024]{0:T(1024)S(1)} all-reduce(f32[1024]{0:T(1024)S(1)} %get-tuple-element.1875), channel_id=5, replica_groups=mesh['dp'=8,'tensor'=4] {'dp','tensor'}, use_global_device_ids=true, to_apply=%region_27.28.clone | all-reduce | flops 1024 | bytes 8192
  1107.4 12.3 reduce-scatter.16.cloned.1.call-done
  1119.7 4.3 fusion.160
  1124.0 99.6 %reduce-scatter.26.cloned.1.call-done = f32[32,288]{1,0:T(8,128)} async-done(((f32[1024,288]{1,0:T(8,128)}), f32[32,288]{1,0:T(8,128)}) %reduce-scatter.26.cloned.1.call-update) | async-done | bytes 36880 | tf_op jit(solution)/shard_map/reduce_scatter | solution.py:301
  (791 shorter events, 421.3 us)
Async XLA Ops:
  7.2 20.7 %copy-start.53 = (u32[32]{0:T(128)S(1)}, u32[32]{0:T(128)}, u32[]{:S(2)}) copy-start(u32[32]{0:T(128)} %constant.307) | copy-start | bytes 388
  7.2 22.6 %copy-start.65 = (bf16[4]{0:T(256)(128)(2,1)S(1)}, bf16[4]{0:T(256)(128)(2,1)}, u32[]{:S(2)}) copy-start(bf16[4]{0:T(256)(128)(2,1)} %param.30) | copy-start | bytes 28
  7.2 22.9 %copy-start.66 = (bf16[4]{0:T(256)(128)(2,1)S(1)}, bf16[4]{0:T(256)(128)(2,1)}, u32[]{:S(2)}) copy-start(bf16[4]{0:T(256)(128)(2,1)} %param.29) | copy-start | bytes 28
  7.2 23.1 %copy-start.67 = (bf16[4]{0:T(256)(128)(2,1)S(1)}, bf16[4]{0:T(256)(128)(2,1)}, u32[]{:S(2)}) copy-start(bf16[4]{0:T(256)(128)(2,1)} %param.31) | copy-start | bytes 28
  7.2 23.3 %copy-start.68 = (bf16[32]{0:T(256)(128)(2,1)S(1)}, bf16[32]{0:T(256)(128)(2,1)}, u32[]{:S(2)}) copy-start(bf16[32]{0:T(256)(128)(2,1)} %param.28) | copy-start | bytes 196
  7.2 37.5 %copy-start.19 = (bf16[128,288]{0,1:T(8,128)(2,1)S(1)}, bf16[128,288]{0,1:T(8,128)(2,1)}, u32[]{:S(2)}) copy-start(bf16[128,288]{0,1:T(8,128)(2,1)} %param.24) | copy-start | bytes 221188
  7.2 55.4 %copy-start.56 = (bf16[4,32]{1,0:T(4,128)(2,1)S(1)}, bf16[4,32]{1,0:T(4,128)(2,1)}, u32[]{:S(2)}) copy-start(bf16[4,32]{1,0:T(4,128)(2,1)} %param.27) | copy-start | bytes 772
  7.3 64.7 %copy-start.46 = (bf16[4,8,8]{2,1,0:T(8,128)(2,1)S(1)}, bf16[4,8,8]{2,1,0:T(8,128)(2,1)}, u32[]{:S(2)}) copy-start(bf16[4,8,8]{2,1,0:T(8,128)(2,1)} %param.25) | copy-start | bytes 1540
  7.3 79.5 %copy-start.54 = (bf16[8,8]{1,0:T(8,128)(2,1)S(1)}, bf16[8,8]{1,0:T(8,128)(2,1)}, u32[]{:S(2)}) copy-start(bf16[8,8]{1,0:T(8,128)(2,1)} %param.26) | copy-start | bytes 388
  7.3 106.9 %all-gather.10.cloned.1.call-start = ((), (), s32[]{:S(2)}) async-start(), calls=%async_computation.9 | async-start | bytes 1179648 | tf_op jit(solution)/shard_map/all_gather | solution.py:163
  8.0 91.8 %copy-start.55 = (bf16[8,8]{1,0:T(8,128)(2,1)S(1)}, bf16[8,8]{1,0:T(8,128)(2,1)}, u32[]{:S(2)}) copy-start(bf16[8,8]{1,0:T(8,128)(2,1)} %param.32) | copy-start | bytes 388
  8.0 106.1 %all-gather.12.cloned.1.call-start = ((), (), s32[]{:S(2)}) async-start(), calls=%async_computation.10 | async-start | bytes 1179648 | tf_op jit(solution)/shard_map/all_gather | solution.py:164
  8.8 106.9 %all-gather.8.cloned.1.call-start = ((), (), s32[]{:S(2)}) async-start(), calls=%async_computation.8 | async-start | bytes 5242880 | tf_op jit(solution)/shard_map/all_gather | solution.py:202
  22.4 5.5 copy-start.20
  23.9 4.0 copy-start.24
  26.4 440.4 %all-gather.14.cloned.1.call-start = ((), (), s32[]{:S(2)}) async-start(), calls=%async_computation.11 | async-start | bytes 1179648 | tf_op jit(solution)/shard_map/all_gather | solution.py:174
  27.0 439.8 %all-gather.16.cloned.1.call-start = ((), (), s32[]{:S(2)}) async-start(), calls=%async_computation.13 | async-start | bytes 5242880 | tf_op jit(solution)/shard_map/all_gather | solution.py:267
  27.6 926.9 %reduce-scatter.20.cloned.1.call-start = ((), (), s32[]{:S(2)}) async-start(), calls=%async_computation.15 | async-start | bytes 1474560 | tf_op jit(solution)/shard_map/reduce_scatter | solution.py:279
  61.6 62.5 %copy-start.13 = (bf16[1024,288]{0,1:T(8,128)(2,1)}, bf16[1024,288]{0,1:T(8,128)(2,1)S(1)}, u32[]{:S(2)}) copy-start(bf16[1024,288]{0,1:T(8,128)(2,1)S(1)} %all_gather.50) | copy-start | bytes 1769476
  71.8 62.4 %copy-start.38 = (f32[1,256]{1,0:T(1,128)}, f32[1,256]{1,0:T(1,128)S(1)}, u32[]{:S(2)}) copy-start(f32[1,256]{1,0:T(1,128)S(1)} %get-tuple-element.2082) | copy-start | bytes 3076
  71.8 62.4 %copy-start.40 = (f32[1,256]{1,0:T(1,128)}, f32[1,256]{1,0:T(1,128)S(1)}, u32[]{:S(2)}) copy-start(f32[1,256]{1,0:T(1,128)S(1)} %get-tuple-element.2085) | copy-start | bytes 3076
  71.8 62.4 %copy-start.42 = (f32[1,256]{1,0:T(1,128)}, f32[1,256]{1,0:T(1,128)S(1)}, u32[]{:S(2)}) copy-start(f32[1,256]{1,0:T(1,128)S(1)} %get-tuple-element.2083) | copy-start | bytes 3076
  71.8 62.4 %copy-start.44 = (f32[1,256]{1,0:T(1,128)}, f32[1,256]{1,0:T(1,128)S(1)}, u32[]{:S(2)}) copy-start(f32[1,256]{1,0:T(1,128)S(1)} %get-tuple-element.2084) | copy-start | bytes 3076
  71.8 14.8 %copy-start.58 = (f32[32]{0:T(128)}, f32[32]{0:T(128)S(1)}, u32[]{:S(2)}) copy-start(f32[32]{0:T(128)S(1)} %convert_element_type.192) | copy-start | bytes 388
  71.9 81.8 %copy-start.49 = (f32[8]{0:T(128)}, f32[8]{0:T(128)S(1)}, u32[]{:S(2)}) copy-start(f32[8]{0:T(128)S(1)} %fusion.176) | copy-start | bytes 100
  72.0 81.7 %copy-start.51 = (f32[8]{0:T(128)}, f32[8]{0:T(128)S(1)}, u32[]{:S(2)}) copy-start(f32[8]{0:T(128)S(1)} %dynamic_slice.335) | copy-start | bytes 100
  86.3 53.0 %copy-start.28 = (f32[512]{0:T(512)}, f32[512]{0:T(512)S(1)}, u32[]{:S(2)}) copy-start(f32[512]{0:T(512)S(1)} %mul.917) | copy-start | bytes 6148
  86.5 52.9 %copy-start.30 = (f32[512]{0:T(512)}, f32[512]{0:T(512)S(1)}, u32[]{:S(2)}) copy-start(f32[512]{0:T(512)S(1)} %mul.920) | copy-start | bytes 6148
  86.6 52.8 %copy-start.34 = (f32[512]{0:T(512)}, f32[512]{0:T(512)S(1)}, u32[]{:S(2)}) copy-start(f32[512]{0:T(512)S(1)} %mul.923) | copy-start | bytes 6148
  86.7 52.6 %copy-start.32 = (f32[512]{0:T(512)}, f32[512]{0:T(512)S(1)}, u32[]{:S(2)}) copy-start(f32[512]{0:T(512)S(1)} %mul.926) | copy-start | bytes 6148
  112.7 372.1 %copy-start.47 = (f32[512]{0:T(512)}, f32[512]{0:T(512)S(1)}, u32[]{:S(2)}) copy-start(f32[512]{0:T(512)S(1)} %reshape.613) | copy-start | bytes 6148
  124.1 10.1 copy-start
  124.3 9.9 copy-start.4
  124.5 9.7 copy-start.6
  124.8 9.4 copy-start.7
  124.8 28.9 %copy-start.15 = (f32[2048,32]{0,1:T(8,128)}, f32[2048,32]{0,1:T(8,128)S(1)}, u32[]{:S(2)}) copy-start(f32[2048,32]{0,1:T(8,128)S(1)} %slice.146) | copy-start | bytes 786436
  450.7 7.0 copy-start.3
  466.8 18.1 %copy-start.22 = (f32[2048]{0:T(1024)}, f32[2048]{0:T(1024)S(1)}, u32[]{:S(2)}) copy-start(f32[2048]{0:T(1024)S(1)} %add_rsqrt_fusion) | copy-start | bytes 24580
  832.4 4.8 copy-start.5
  837.2 5.4 copy-start.27
  837.2 5.5 copy-start.45
  848.2 112.6 %reduce-scatter.30.cloned.1.call-start = ((), (), s32[]{:S(2)}) async-start(), calls=%async_computation.20 | async-start | bytes 73728
  871.3 90.9 %reduce-scatter.28.cloned.1.call-start = ((), (), s32[]{:S(2)}) async-start(), calls=%async_computation.19 | async-start | bytes 1179648
  871.3 11.5 copy-start.9
  871.3 11.5 copy-start.23
  871.3 11.5 copy-start.48
  871.3 11.5 copy-start.61
  885.2 4.7 copy-start.33
  889.9 3.7 copy-start.31
  889.9 85.8 %reduce-scatter.24.cloned.1.call-start = ((), (), s32[]{:S(2)}) async-start(), calls=%async_computation.17 | async-start | bytes 1179648 | tf_op jit(solution)/shard_map/reduce_scatter | solution.py:312
  890.0 3.6 copy-start.2
  901.4 107.9 %reduce-scatter.22.cloned.1.call-start = ((), (), s32[]{:S(2)}) async-start(), calls=%async_computation.16 | async-start | bytes 1179648 | tf_op jit(solution)/shard_map/reduce_scatter | solution.py:306
  901.6 6.4 copy-start.62
  908.0 155.8 %reduce-scatter.18.cloned.1.call-start = ((), (), s32[]{:S(2)}) async-start(), calls=%async_computation.14 | async-start | bytes 5242880 | tf_op jit(solution)/shard_map/reduce_scatter | solution.py:287
  908.0 4.1 copy-start.63
  916.8 202.9 %reduce-scatter.16.cloned.1.call-start = ((), (), s32[]{:S(2)}) async-start(), calls=%async_computation.12 | async-start | bytes 5242880 | tf_op jit(solution)/shard_map/reduce_scatter | solution.py:260
  924.6 30.0 %copy-start.11 = (bf16[512,1024]{1,0:T(8,128)(2,1)S(1)}, bf16[512,1024]{1,0:T(8,128)(2,1)}, u32[]{:S(2)}) copy-start(bf16[512,1024]{1,0:T(8,128)(2,1)} %fusion.156) | copy-start | bytes 3145732
  924.6 139.2 %copy-start.10 = (bf16[512,1024]{1,0:T(8,128)(2,1)S(1)}, bf16[512,1024]{1,0:T(8,128)(2,1)}, u32[]{:S(2)}) copy-start(bf16[512,1024]{1,0:T(8,128)(2,1)} %param.20) | copy-start | bytes 3145732
  924.6 139.2 %copy-start.14 = (bf16[1024,288]{0,1:T(8,128)(2,1)S(1)}, bf16[1024,288]{0,1:T(8,128)(2,1)}, u32[]{:S(2)}) copy-start(bf16[1024,288]{0,1:T(8,128)(2,1)} %copy-done.13) | copy-start | bytes 1769476
  924.6 139.2 %copy-start.21 = (f32[8,1,128]{2,1,0:T(1,128)S(1)}, f32[8,1,128]{2,1,0:T(1,128)}, u32[]{:S(2)}) copy-start(f32[8,1,128]{2,1,0:T(1,128)} %copy-done.20) | copy-start | bytes 12292
  924.6 139.1 %copy-start.25 = (f32[512]{0:T(512)S(1)}, f32[512]{0:T(512)}, u32[]{:S(2)}) copy-start(f32[512]{0:T(512)} %copy-done.24) | copy-start | bytes 6148
  924.6 299.0 %reduce-scatter.26.cloned.1.call-start = ((), (), s32[]{:S(2)}) async-start(), calls=%async_computation.18 | async-start | bytes 1622016 | tf_op jit(solution)/shard_map/reduce_scatter | solution.py:301
  954.5 109.2 %copy-start.16 = (bf16[512,288]{0,1:T(8,128)(2,1)S(1)}, bf16[512,288]{0,1:T(8,128)(2,1)}, u32[]{:S(2)}) copy-start(bf16[512,288]{0,1:T(8,128)(2,1)} %reduce-scatter.20.cloned.1.call-done) | copy-start | bytes 884740
  957.6 162.1 %copy-start.12 = (bf16[512,1024]{1,0:T(8,128)(2,1)S(1)}, bf16[512,1024]{1,0:T(8,128)(2,1)}, u32[]{:S(2)}) copy-start(bf16[512,1024]{1,0:T(8,128)(2,1)} %param.34) | copy-start | bytes 3145732
  (18 other events, 31.3 us)
Sparse Core Ops, SparseCore 0:
  9.7 24.7 all-gather.9
  36.1 25.5 all-gather.11
  63.6 52.0 all-gather.7
  117.1 23.9 all-gather.13
  142.8 51.3 all-gather.15
  848.3 28.7 reduce-scatter.19
  879.9 30.0 reduce-scatter.29
  912.3 30.6 reduce-scatter.27
  945.4 30.3 reduce-scatter.23
  978.6 30.6 reduce-scatter.21
  1012.5 51.1 reduce-scatter.17
  1066.5 53.1 reduce-scatter.15
  1126.4 97.1 reduce-scatter.25
where the time goes:
time: 1240 us; the launch traced here: 1230 us
  local copies, waits for them, and re-layouts  331 us (27%)
  matrix products  274 us (22%)
  waiting for transfers between devices  213 us (17%)
  blocking collectives  192 us (15%)
  other arithmetic  189 us (15%)
  between operations  19.5 us (2%)
  loops' own time  12.4 us (1%)
    dynamic_update_slice x80, local copies, waits for them, and re-layouts, block_scan(): lax.scan(advance, (start_state, jnp.array(-1, jnp.int32)), stacked)  233 us
    dot_general x24, matrix products, advance(): inner_y = jnp.einsum('hij,jhp->ihp', mixing, block_x, precision=highest)  103 us
    reduce_scatter x1, waiting for transfers between devices, per_device(): lax.psum_scatter(along_rows(normed, own_state), ('dp', 'tensor'), scatter...  99.6 us
    unnamed x3, blocking collectives  79.7 us
    dynamic_update_slice x72, other arithmetic, block_scan(): lax.scan(advance, (start_state, jnp.array(-1, jnp.int32)), stacked)  62.1 us
    reduce_scatter x1, waiting for transfers between devices, per_device(): lax.psum_scatter((against_rows(gate_bf, gate_cols) + against_rows(conv_bf...  52.8 us
    dot_general x24, matrix products, advance(): jnp.einsum('jhp,js->hps', keep_weight[:, :, None] * block_x, block_b, pre...  45.1 us
    dot_general x24, matrix products, advance(): gram_matrix = jnp.dot(block_c, block_b.T, precision=highest)  41.5 us
  transfers between devices with their start and end apart: 13, of which 6 were waited for; matrix products, arithmetic and copies ran while one was open for 34% of the time, Pallas kernels for 0%

commit v1 on v0

v1 whole, which is shorter than its diff:
```python
import functools

import jax
import jax.numpy as jnp
import numpy as np
from jax import lax
from jax.experimental import pallas as pl
from jax.experimental.pallas import tpu as pltpu
from jax.sharding import PartitionSpec as P

HEADDIM = 64
STATE = 128
INNER = 2048
LANES = 128
ROWS = 256
WIDE_ROWS = 512
SUB = 128
EPS = 1e-05
LOG2E = 1.4426950408889634

f32 = jnp.float32
bf16 = jnp.bfloat16


def nn(a, b):
    return lax.dot_general(a, b, (((1,), (0,)), ((), ())), preferred_element_type=f32)


def nt(a, b):
    return lax.dot_general(a, b, (((1,), (1,)), ((), ())), preferred_element_type=f32)


def tn(a, b):
    return lax.dot_general(a, b, (((0,), (0,)), ((), ())), preferred_element_type=f32)


def pieces(z, count):
    parts = []
    for _ in range(count - 1):
        part = z.astype(bf16)
        parts.append(part)
        z = z - part.astype(f32)
    parts.append(z.astype(bf16))
    return parts


def head_matrix(channels):
    lane = lax.broadcasted_iota(jnp.int32, (LANES, channels), 1)
    row = lax.broadcasted_iota(jnp.int32, (LANES, channels), 0)
    inside = (lane >= row * HEADDIM) & (lane < row * HEADDIM + HEADDIM)
    return jnp.where(inside, 1.0, 0.0).astype(bf16)


def spread_heads(z, heads):
    return sum(nn(part, heads) for part in pieces(z, 2))


def gather_heads(z, heads):
    return sum(nt(part, heads) for part in pieces(z, 2))


def triangle_sum(triangle, z):
    return sum(nn(triangle, part) for part in pieces(z, 3))


def ends_of(len_ref, count):
    ends, total = [], 0
    for s in range(count):
        total = total + len_ref[0, s]
        ends.append(total)
    return ends


def segment_of(places, ends):
    return sum((places >= end).astype(jnp.int32) for end in ends)


def start_of(places, ends):
    start = jnp.zeros_like(places)
    for end in ends:
        start = jnp.where(places >= end, end, start)
    return start


def scan_terms(raw, decay, base, ends, heads):
    sub = raw.shape[0]
    row = lax.broadcasted_iota(jnp.int32, (sub, sub), 0)
    col = lax.broadcasted_iota(jnp.int32, (sub, sub), 1)
    lower = jnp.where(row >= col, 1.0, 0.0).astype(bf16)
    step = jnp.maximum(raw, 0.0) + jnp.log1p(jnp.exp(-jnp.abs(raw)))
    log_decay = -decay * step
    cum = triangle_sum(lower, log_decay)
    places = base + lax.broadcasted_iota(jnp.int32, (sub, 1), 0)
    segment = segment_of(places, ends)
    before = segment_of(base - 1, ends)
    tail = segment_of(base + sub - 1, ends)
    last = cum[sub - 1 : sub, :]
    carried = jnp.where(segment == before, jnp.exp(cum), 0.0)
    keep = jnp.where(segment == tail, jnp.exp(last - cum), 0.0)
    survive = jnp.where(tail == before, jnp.exp(last), 0.0)
    wide = spread_heads(
        jnp.concatenate([step, carried, keep, jnp.broadcast_to(survive, (8, LANES))], axis=0), heads
    )
    return (
        step,
        log_decay,
        cum * LOG2E,
        wide[:sub],
        wide[sub : 2 * sub],
        wide[2 * sub : 3 * sub],
        wide[3 * sub : 3 * sub + 1],
    )


def pair_stack(z):
    lane = lax.broadcasted_iota(jnp.int32, z.shape, 1)
    zero = jnp.zeros_like(z)
    return jnp.concatenate(
        [jnp.where(lane < HEADDIM, z, zero), jnp.where(lane >= HEADDIM, z, zero)], axis=0
    )


def silu(u):
    return u * jax.nn.sigmoid(u)


def own_lanes(z, shift, count):
    moved = pltpu.roll(z, (z.shape[1] - shift) % z.shape[1], 1)
    lane = lax.broadcasted_iota(jnp.int32, z.shape, 1)
    return jnp.where(lane < count, moved, 0.0)


def nn3(a, b):
    a, a_low = pieces(a, 2)
    b, b_low = pieces(b, 2)
    return nn(jnp.concatenate([a, a_low, a], axis=1), jnp.concatenate([b, b, b_low], axis=0))


def nt3(a, b):
    a, a_low = pieces(a, 2)
    b, b_low = pieces(b, 2)
    return nt(jnp.concatenate([a, a_low, a], axis=1), jnp.concatenate([b, b, b_low], axis=1))


def pair_product(mixing, z):
    high, low = pieces(z, 2)
    both = nn(
        jnp.concatenate(mixing, axis=1),
        jnp.concatenate([pair_stack(high), pair_stack(low)], axis=1),
    )
    return both[:, :LANES] + both[:, LANES:]


def take_rows(refs, which, buffer):
    if len(refs) == 1:
        return refs[0][...]
    half = refs[3].shape[1]
    for k in range(3):

        @pl.when(which == k)
        def _(k=k):
            buffer[...] = refs[k][...]

    @pl.when(which == 3)
    def _():
        buffer[:, :half] = refs[3][...]
        buffer[:, half:] = refs[4][...]

    return buffer[...]


def put_halves(refs, which, product):
    half = product.shape[1] // 2
    left, right = product[:, :half], product[:, half:]
    if len(refs) == 2:
        refs[0][...] = left
        refs[1][...] = right
        return
    left_sent, left_kept, right_sent, right_kept = refs

    @pl.when(which % 2 == 1)
    def _():
        left_sent[...] = left

    @pl.when(which % 2 == 0)
    def _():
        left_kept[...] = left

    @pl.when(which >= 2)
    def _():
        right_sent[...] = right

    @pl.when(which < 2)
    def _():
        right_kept[...] = right


def scan_kernel(len_ref, first_ref, place_ref, *refs, parts, seqs, taps, head_count):
    part_refs, refs = refs[:parts], refs[parts:]
    (
        w_ref,
        gain_ref,
        prm_ref,
        prs_ref,
        prh_ref,
        normed_ref,
        v_ref,
        u_ref,
        vs_ref,
        us_ref,
        raw_ref,
        y_ref,
        st_ref,
        hid_buf,
        vbuf,
        sbuf,
        carry,
    ) = refs
    rows, channels = v_ref.shape
    step_id = pl.program_id(0)
    base = step_id * rows
    ends = ends_of(len_ref, seqs)

    @pl.when(step_id == 0)
    def _():
        vbuf[0:8, :] = jnp.zeros((8, channels), f32)
        sbuf[0:8, :] = jnp.zeros((8, 2 * STATE), f32)
        carry[...] = jnp.zeros_like(carry)

    values = take_rows(part_refs, place_ref[0, step_id], hid_buf).astype(f32)
    inverse = lax.rsqrt(jnp.mean(values * values, axis=1, keepdims=True) + EPS)
    normed = (values * inverse * gain_ref[...]).astype(bf16)
    normed_ref[...] = normed
    conv_pre = nn(normed, w_ref[:, :channels])
    state_all = nn(normed, w_ref[:, channels:])
    v_ref[...] = conv_pre.astype(bf16)
    vs_ref[...] = state_all[:, : 2 * STATE].astype(bf16)
    vbuf[8 : 8 + rows, :] = conv_pre
    sbuf[8 : 8 + rows, :] = state_all[:, : 2 * STATE]
    places = base + lax.broadcasted_iota(jnp.int32, (rows, 1), 0)
    start = start_of(places, ends)
    u = prm_ref[taps : taps + 1, :] + prm_ref[taps - 1 : taps, :] * conv_pre
    us = prs_ref[taps : taps + 1, :] + prs_ref[taps - 1 : taps, :] * state_all[:, : 2 * STATE]
    for lag in range(1, taps):
        usable = places - lag >= start
        tap = taps - 1 - lag
        u = u + prm_ref[tap : tap + 1, :] * jnp.where(usable, vbuf[8 - lag : 8 - lag + rows, :], 0.0)
        us = us + prs_ref[tap : tap + 1, :] * jnp.where(usable, sbuf[8 - lag : 8 - lag + rows, :], 0.0)
    vbuf[0:8, :] = vbuf[rows : rows + 8, :]
    sbuf[0:8, :] = sbuf[rows : rows + 8, :]
    u_ref[...] = u
    us_ref[...] = us
    raw = own_lanes(state_all[:, 2 * STATE :], first_ref[0], head_count) + prh_ref[0:1, :]
    raw_ref[...] = raw

    heads = head_matrix(channels)
    x = silu(u)
    maps_f = silu(us)
    maps = maps_f.astype(bf16)
    decay = prh_ref[1:2, :]
    row = lax.broadcasted_iota(jnp.int32, (SUB, SUB), 0)
    col = lax.broadcasted_iota(jnp.int32, (SUB, SUB), 1)
    for q in range(rows // SUB):
        at = slice(q * SUB, (q + 1) * SUB)
        low = base + q * SUB
        step, log_decay, cum, step_w, carried_w, keep_w, survive_w = scan_terms(
            raw[at], decay, low, ends, heads
        )
        cum_row = cum.T
        mask = (row >= col) & (segment_of(low + row, ends) == segment_of(low + col, ends))
        b_map, c_map = maps[at, :STATE], maps[at, STATE:]
        gram = jnp.where(mask, nt3(maps_f[at, STATE:], maps_f[at, :STATE]), 0.0)
        stepped = step_w * x[at]
        stepped_b = stepped.astype(bf16)
        state = carry[...]
        st_ref[q] = state
        outer = carried_w * nn3(maps_f[at, STATE:], state)
        for pair in range(channels // LANES):
            lanes = slice(pair * LANES, (pair + 1) * LANES)
            mixing = []
            for h in (2 * pair, 2 * pair + 1):
                spread = cum[:, h : h + 1] - cum_row[h : h + 1, :]
                mixing.append((jnp.exp2(jnp.minimum(spread, 0.0)) * gram).astype(bf16))
            inner = pair_product(mixing, stepped[:, lanes])
            y_ref[at, lanes] = inner + outer[:, lanes]
        carry[...] = survive_w * state + nn3(maps_f[at, :STATE].T, keep_w * stepped)


def value_kernel(place_ref, normed_ref, u_ref, y_ref, prm_ref, w_ref, gate_ref, ga_ref, square_ref, *refs, taps):
    rows, channels = gate_ref.shape
    gate_pre = nn(normed_ref[...], w_ref[:, :channels])
    gate_ref[...] = gate_pre
    y = y_ref[...] + prm_ref[taps + 1 : taps + 2, :] * silu(u_ref[...])
    g = y * silu(gate_pre)
    ga = (g * prm_ref[taps + 2 : taps + 3, :]).astype(bf16)
    ga_ref[...] = ga
    square = jnp.sum(g * g, axis=1, keepdims=True)
    square_ref[...] = jnp.broadcast_to(square, (rows, LANES)).T[:8, :]
    product = nt(ga, w_ref[:, channels:]).astype(bf16)
    put_halves(refs, place_ref[0, pl.program_id(0)], product)


def cotangent_kernel(place_ref, *refs, parts):
    part_refs, refs = refs[:parts], refs[parts:]
    w_ref, ga_ref, square_ref, gg_ref, sums_ref, cot_buf = refs
    rows = gg_ref.shape[0]
    cotangent = take_rows(part_refs, place_ref[0, pl.program_id(0)], cot_buf)
    grad_gated = nn(cotangent, w_ref[...])
    gg_ref[...] = grad_gated
    inner = jnp.sum(grad_gated * ga_ref[...].astype(f32), axis=1, keepdims=True)
    inner_row = jnp.broadcast_to(inner, (rows, LANES)).T[:8, :]
    sublane = lax.broadcasted_iota(jnp.int32, (8, rows), 0)
    sums_ref[...] = jnp.where(sublane == 0, square_ref[...], inner_row)


def gate_kernel(sums_ref, prm_ref, gate_ref, u_ref, y_ref, gg_ref, gated_ref, dgate_ref, dy_ref, dprm_ref, *, taps):
    rows = gate_ref.shape[0]

    @pl.when(pl.program_id(0) == 0)
    def _():
        dprm_ref[...] = jnp.zeros_like(dprm_ref)

    sums = jnp.concatenate([sums_ref[...], jnp.zeros((LANES - 8, rows), f32)], axis=0).T
    inverse = lax.rsqrt(sums[:, 0:1] * (1.0 / INNER) + EPS)
    inner_mean = sums[:, 1:2] * inverse * (1.0 / INNER)
    skip = prm_ref[taps + 1 : taps + 2, :]
    gain = prm_ref[taps + 2 : taps + 3, :]
    gate_pre = gate_ref[...]
    sig_gate = jax.nn.sigmoid(gate_pre)
    act = gate_pre * sig_gate
    x = silu(u_ref[...])
    y = y_ref[...] + skip * x
    hat = y * act * inverse
    gated_ref[...] = (hat * gain).astype(bf16)
    grad_gated = gg_ref[...]
    dprm_ref[taps + 2 : taps + 3, :] += jnp.sum(grad_gated * hat, axis=0, keepdims=True)
    grad_inner = inverse * (grad_gated * gain - hat * inner_mean)
    dy = grad_inner * act
    dgate_ref[...] = (grad_inner * y * sig_gate * (1.0 + gate_pre * (1.0 - sig_gate))).astype(bf16)
    dprm_ref[taps + 1 : taps + 2, :] += jnp.sum(dy * x, axis=0, keepdims=True)
    dy_ref[...] = dy


def gain_row(weights, grads):
    terms = jnp.sum(weights.astype(f32) * grads, axis=1, keepdims=True)
    return jnp.broadcast_to(terms, (terms.shape[0], LANES)).T[:8, :]


def first_weights_kernel(place_ref, *refs, parts):
    part_refs, refs = refs[:parts], refs[parts:]
    normed_ref, dgate_ref, gated_ref, w_ref, out_ref, gain_ref, cot_buf, total = refs
    channels = dgate_ref.shape[1]
    step_id = pl.program_id(0)

    @pl.when(step_id == 0)
    def _():
        total[...] = jnp.zeros_like(total)

    total[:, :channels] += tn(normed_ref[...], dgate_ref[...])
    cotangent = take_rows(part_refs, place_ref[0, step_id], cot_buf)
    total[:, channels:] += tn(cotangent, gated_ref[...])

    @pl.when(step_id == pl.num_programs(0) - 1)
    def _():
        out_ref[...] = total[...].astype(bf16)
        gain_ref[...] = gain_row(w_ref[...], total[:, :channels])


def last_weights_kernel(
    first_ref,
    normed_ref,
    gb_ref,
    w_ref,
    gain_ref,
    terms_ref,
    dprm_gate_ref,
    dprm_ref,
    dprs_ref,
    dprh_ref,
    out_ref,
    small_ref,
    total,
    *,
    taps,
):
    step_id = pl.program_id(0)
    channels = dprm_ref.shape[1]

    @pl.when(step_id == 0)
    def _():
        total[...] = jnp.zeros_like(total)

    total[...] += tn(normed_ref[...], gb_ref[...])

    @pl.when(step_id == pl.num_programs(0) - 1)
    def _():
        grads = total[...]
        out_ref[...] = grads.astype(bf16)
        terms = (gain_row(w_ref[...], grads) + terms_ref[...]) / gain_ref[...]
        row = lax.broadcasted_iota(jnp.int32, (8, 1), 0)
        both = jnp.where(row > taps, dprm_gate_ref[...], dprm_ref[...])
        skip = gather_heads(dprm_gate_ref[...], head_matrix(channels))
        by_head = jnp.where(row == 2, pltpu.roll(skip, 8 - (taps - 1), 0), dprh_ref[...])
        small_ref[...] = jnp.zeros_like(small_ref)
        small_ref[0:8, :channels] = both
        small_ref[0:8, channels : channels + 2 * STATE] = dprs_ref[...]
        small_ref[0:8, channels + 2 * STATE : channels + 2 * STATE + LANES] = pltpu.roll(
            by_head, first_ref[0], 1
        )
        small_ref[8:16, :] = terms


def backward_kernel(len_ref, first_ref, place_ref, *refs, seqs, taps, halves):
    (
        wg_ref,
        w_ref,
        prm_ref,
        prs_ref,
        prh_ref,
        dgate_ref,
        dy_ref,
        v_ref,
        u_ref,
        vs_ref,
        us_ref,
        raw_ref,
        y_ref,
        st_ref,
        gb_ref,
    ) = refs[:15]
    half_refs = refs[15 : 15 + halves]
    dprm_ref, dprs_ref, dprh_ref, dbuf, dsbuf, carry, ending = refs[15 + halves :]
    rows, channels = dgate_ref.shape
    step_id = pl.program_id(0)
    base = (pl.num_programs(0) - 1 - step_id) * rows
    ends = ends_of(len_ref, seqs)

    @pl.when(step_id == 0)
    def _():
        dbuf[rows : rows + 8, :] = jnp.zeros((8, channels), f32)
        dsbuf[rows : rows + 8, :] = jnp.zeros((8, 2 * STATE), f32)
        carry[...] = jnp.zeros_like(carry)
        ending[...] = jnp.zeros_like(ending)
        dprm_ref[...] = jnp.zeros_like(dprm_ref)
        dprs_ref[...] = jnp.zeros_like(dprs_ref)
        dprh_ref[...] = jnp.zeros_like(dprh_ref)

    def add_row(ref, at, z):
        ref[at : at + 1, :] += jnp.sum(z, axis=0, keepdims=True)

    skip = prm_ref[taps + 1 : taps + 2, :]
    u = u_ref[...]
    sig_u = jax.nn.sigmoid(u)
    x = u * sig_u
    y_scan = y_ref[...]
    dy_f = dy_ref[...]
    dy_b = dy_f.astype(bf16)

    heads = head_matrix(channels)
    us = us_ref[...]
    sig_us = jax.nn.sigmoid(us)
    maps_f = us * sig_us
    maps = maps_f.astype(bf16)
    raw = raw_ref[...]
    decay = prh_ref[1:2, :]
    row = lax.broadcasted_iota(jnp.int32, (SUB, SUB), 0)
    col = lax.broadcasted_iota(jnp.int32, (SUB, SUB), 1)
    upper = jnp.where(row <= col, 1.0, 0.0).astype(bf16)
    dxs, dmaps, draws = [], [], []
    for q in reversed(range(rows // SUB)):
        at = slice(q * SUB, (q + 1) * SUB)
        low = base + q * SUB
        step, log_decay, cum, step_w, carried_w, keep_w, survive_w = scan_terms(
            raw[at], decay, low, ends, heads
        )
        cum_row = cum.T
        mask = (row <= col) & (segment_of(low + row, ends) == segment_of(low + col, ends))
        b_map, c_map = maps[at, :STATE], maps[at, STATE:]
        gram = jnp.where(mask, nt3(maps_f[at, :STATE], maps_f[at, STATE:]), 0.0)
        stepped = step_w * x[at]
        stepped_b = stepped.astype(bf16)
        state = st_ref[q]
        dstate = carry[...]
        dstate_b = dstate.astype(bf16)
        dgram = jnp.zeros((SUB, SUB), f32)
        inner = []
        for pair in range(channels // LANES):
            lanes = slice(pair * LANES, (pair + 1) * LANES)
            dy_pair = dy_b[at, lanes]
            dmix = nt(pair_stack(stepped_b[:, lanes]), dy_pair)
            mixing = []
            for i, h in enumerate((2 * pair, 2 * pair + 1)):
                spread = cum_row[h : h + 1, :] - cum[:, h : h + 1]
                weight = jnp.exp2(jnp.minimum(spread, 0.0))
                mixing.append((weight * gram).astype(bf16))
                dgram = dgram + dmix[i * SUB : (i + 1) * SUB] * weight
            inner.append(pair_product(mixing, dy_f[at, lanes]))
        dstepped = jnp.concatenate(inner, axis=1) + keep_w * nn3(maps_f[at, :STATE], dstate)
        dgram = jnp.where(mask, dgram, 0.0).astype(bf16)
        dy_q = dy_f[at]
        dy_carried = (carried_w * dy_q).astype(bf16)
        db = nn(dgram, c_map) + nt((keep_w * stepped).astype(bf16), dstate_b)
        dc = tn(dgram, b_map) + nt(dy_carried, state.astype(bf16))
        dprev = survive_w * dstate + nn3(maps_f[at, STATE:].T, carried_w * dy_q)
        carry[...] = dprev
        balance = dy_q * y_scan[at] - stepped * dstepped
        state_end = ending[0:1, :]
        ending[0:1, :] = jnp.sum(state * dprev, axis=0, keepdims=True)
        by_head = gather_heads(
            jnp.concatenate(
                [balance, x[at] * dstepped, jnp.broadcast_to(state_end, (8, channels))], axis=0
            ),
            heads,
        )
        dlog = triangle_sum(upper, by_head[:SUB]) + by_head[2 * SUB : 2 * SUB + 1]
        dstep = by_head[SUB : 2 * SUB] - decay * dlog
        draw = dstep * jax.nn.sigmoid(raw[at])
        add_row(dprh_ref, 0, draw)
        add_row(dprh_ref, 1, dlog * log_decay)
        dxs.append(step_w * dstepped + skip * dy_q)
        dmaps.append(jnp.concatenate([db, dc], axis=1))
        draws.append(draw)
    dx = jnp.concatenate(dxs[::-1], axis=0)
    dmap = jnp.concatenate(dmaps[::-1], axis=0)
    draw = jnp.concatenate(draws[::-1], axis=0)
    du = dx * sig_u * (1.0 + u * (1.0 - sig_u))
    dus = dmap * sig_us * (1.0 + us * (1.0 - sig_us))
    dbuf[0:rows, :] = du
    dsbuf[0:rows, :] = dus
    v = v_ref[...].astype(f32)
    vs = vs_ref[...].astype(f32)
    places = base + lax.broadcasted_iota(jnp.int32, (rows, 1), 0)
    segment = segment_of(places, ends)
    dv = prm_ref[taps - 1 : taps, :] * du
    dvs = prs_ref[taps - 1 : taps, :] * dus
    add_row(dprm_ref, taps - 1, du * v)
    add_row(dprs_ref, taps - 1, dus * vs)
    add_row(dprm_ref, taps, du)
    add_row(dprs_ref, taps, dus)
    for lag in range(1, taps):
        usable = segment_of(places + lag, ends) == segment
        tap = taps - 1 - lag
        later = jnp.where(usable, dbuf[lag : lag + rows, :], 0.0)
        later_s = jnp.where(usable, dsbuf[lag : lag + rows, :], 0.0)
        dv = dv + prm_ref[tap : tap + 1, :] * later
        dvs = dvs + prs_ref[tap : tap + 1, :] * later_s
        add_row(dprm_ref, tap, later * v)
        add_row(dprs_ref, tap, later_s * vs)
    dbuf[rows : rows + 8, :] = dbuf[0:8, :]
    dsbuf[rows : rows + 8, :] = dsbuf[0:8, :]
    gb_ref[:, :channels] = dv.astype(bf16)
    gb_ref[:, channels : channels + 2 * STATE] = dvs.astype(bf16)
    gb_ref[:, channels + 2 * STATE :] = pltpu.roll(draw, first_ref[0], 1).astype(bf16)
    product = nt(dgate_ref[...], wg_ref[...]) + nt(gb_ref[...], w_ref[...])
    put_halves(half_refs, place_ref[0, step_id], product.astype(bf16))


def held(places):
    last = next(p for p in places if p is not None)
    filled = []
    for p in places:
        last = last if p is None else p
        filled.append(last)
    return filled


def place_table(tensor_place, quarter_blocks, order):
    relative = [(b // quarter_blocks) ^ tensor_place for b in order]
    inside = [b % quarter_blocks for b in order]

    def places(slots):
        return held(
            [slots.index(r) * quarter_blocks + w if r in slots else None for r, w in zip(relative, inside)]
        )

    return [
        relative,
        places([0]),
        places([1]),
        places([2]),
        places([3]),
        places([1, 3]),
        places([0, 2]),
        places([2, 3]),
        places([0, 1]),
    ]


def over_x(z):
    return lax.ppermute(z, "tensor", [(0, 1), (1, 0), (2, 3), (3, 2)])


def over_y(z):
    return lax.ppermute(z, "tensor", [(0, 2), (2, 0), (1, 3), (3, 1)])


def gather_start(z):
    return over_x(z), over_y(z)


def gather_end(z, from_x, from_y):
    half = z.shape[1] // 2
    return [z, from_x, from_y, over_y(from_x[:, :half]), over_x(from_y[:, half:])]


def scatter_start(halves):
    return over_x(halves[0]), over_y(halves[2])


def scatter_middle(halves, from_x, from_y, after=()):
    rows = from_x.shape[0] // 2
    left, right = halves[1], halves[3]
    left_far = left[rows:].astype(f32) + from_x[rows:].astype(f32)
    right_far = right[rows:].astype(f32) + from_y[rows:].astype(f32)
    far = (left_far.astype(bf16), right_far.astype(bf16))
    far, after = lax.optimization_barrier((far, after))
    return (over_y(far[0]), over_x(far[1])), after


def scatter_end(halves, from_x, from_y, far_left, far_right):
    rows = from_x.shape[0] // 2
    left, right = halves[1][:rows].astype(f32), halves[3][:rows].astype(f32)
    left = left + from_x[:rows].astype(f32) + far_left.astype(f32)
    right = right + from_y[:rows].astype(f32) + far_right.astype(f32)
    return jnp.concatenate([left, right], axis=1)


def sum_over_tensor(z):
    z = (z.astype(f32) + over_x(z).astype(f32)).astype(z.dtype)
    return z.astype(f32) + over_y(z).astype(f32)


def sum_over_dp(z):
    count = lax.axis_size("dp")
    bit = 1
    while bit < count:
        z = z + lax.ppermute(z, "dp", [(i, i ^ bit) for i in range(count)])
        bit *= 2
    return z


class Kernels:
    def __init__(self, lengths, first, tensor_place, tensor_count, group_rows, width, channels, taps, head_count):
        self.lengths, self.first = lengths, first
        self.tensor_place, self.tensor_count = tensor_place, tensor_count
        self.square = tensor_count == 4
        self.group_rows, self.width, self.channels = group_rows, width, channels
        self.taps, self.head_count = taps, head_count
        self.seqs = lengths.shape[1]

    def table(self, block, backwards=False):
        order = list(range(self.group_rows // block))
        if backwards:
            order = order[::-1]
        if not self.square:
            return jnp.asarray([order], jnp.int32)
        each = len(order) // 4
        tables = np.array([place_table(t, each, order) for t in range(4)], np.int32)
        return lax.dynamic_index_in_dim(jnp.asarray(tables), self.tensor_place, 0, keepdims=False)

    def call(self, kernel, scalars, block, ins, outs, scratch, flops, transcendentals=0):
        steps = self.group_rows // block
        specs, arrays = zip(*ins)
        out_specs, out_shapes = zip(*outs)
        return pl.pallas_call(
            kernel,
            grid_spec=pltpu.PrefetchScalarGridSpec(
                num_scalar_prefetch=len(scalars),
                grid=(steps,),
                in_specs=list(specs),
                out_specs=list(out_specs),
                scratch_shapes=scratch,
            ),
            out_shape=list(out_shapes),
            compiler_params=pltpu.CompilerParams(vmem_limit_bytes=56 * 2**20),
            cost_estimate=pl.CostEstimate(flops=1000, bytes_accessed=1000, transcendentals=0),
            name=getattr(kernel, "func", kernel).__name__,
        )(*scalars, *arrays)

    def whole(self, array):
        return pl.BlockSpec(array.shape, lambda i, *s: (0,) * len(array.shape)), array

    def columns(self, array, width, place):
        return pl.BlockSpec((array.shape[0], width), lambda i, *s: (0, place)), array

    def rows(self, array, block, backwards=False):
        last = self.group_rows // block - 1

        def at(i, *s):
            return (last - i if backwards else i,) + (0,) * (len(array.shape) - 1)

        size = array.shape[0] * block // self.group_rows
        return pl.BlockSpec((size,) + array.shape[1:], at), array

    def across(self, array, block):
        return pl.BlockSpec((8, block), lambda i, *s: (0, i)), array

    def out(self, columns, dtype):
        return jax.ShapeDtypeStruct((self.group_rows, columns), dtype)

    def parts(self, arrays, block):
        if not self.square:
            return [self.rows(arrays[0], block)]
        return [
            (pl.BlockSpec((block, z.shape[1]), lambda i, *s, k=k: (s[-1][k, i], 0)), z)
            for k, z in zip((1, 2, 3, 4, 4), arrays)
        ]

    def halves(self, block):
        half = self.width // 2
        if not self.square:
            return [
                (pl.BlockSpec((block, half), lambda i, *s: (s[-1][0, i], 0)), self.out(half, bf16))
                for _ in range(2)
            ]
        shape = jax.ShapeDtypeStruct((self.group_rows // 2, half), bf16)
        return [
            (pl.BlockSpec((block, half), lambda i, *s, k=k: (s[-1][k, i], 0)), shape) for k in (5, 6, 7, 8)
        ]

    def scan(self, hidden, weights, gain, prm, prs, prh):
        channels, count = self.channels, self.group_rows
        parts = self.parts(hidden, ROWS)
        outs = [
            self.out(self.width, bf16),
            self.out(channels, bf16),
            self.out(channels, f32),
            self.out(2 * STATE, bf16),
            self.out(2 * STATE, f32),
            self.out(LANES, f32),
            self.out(channels, f32),
            jax.ShapeDtypeStruct((count // SUB, STATE, channels), f32),
        ]
        return self.call(
            functools.partial(
                scan_kernel, parts=len(parts), seqs=self.seqs, taps=self.taps, head_count=self.head_count
            ),
            (self.lengths, self.first, self.table(ROWS)),
            ROWS,
            parts + [self.whole(z) for z in (weights, gain, prm, prs, prh)],
            [self.rows(z, ROWS) for z in outs],
            [
                pltpu.VMEM((ROWS, self.width), bf16),
                pltpu.VMEM((ROWS + 8, channels), f32),
                pltpu.VMEM((ROWS + 8, 2 * STATE), f32),
                pltpu.VMEM((STATE, channels), f32),
            ],
            count * self.width * channels * 8,
            count * channels * 8,
        )

    def value(self, normed, u, y, prm, weights):
        channels, count = self.channels, self.group_rows
        outs = [self.rows(self.out(channels, f32), WIDE_ROWS), self.rows(self.out(channels, bf16), WIDE_ROWS)]
        outs += [self.across(jax.ShapeDtypeStruct((8, count), f32), WIDE_ROWS)]
        result = self.call(
            functools.partial(value_kernel, taps=self.taps),
            (self.table(WIDE_ROWS),),
            WIDE_ROWS,
            [self.rows(z, WIDE_ROWS) for z in (normed, u, y)] + [self.whole(prm), self.whole(weights)],
            outs + self.halves(WIDE_ROWS),
            [],
            4 * count * self.width * channels,
        )
        return result[:3], result[3:]

    def cotangent(self, cotangent, weights, ga, square):
        channels, count = self.channels, self.group_rows
        parts = self.parts(cotangent, WIDE_ROWS)
        return self.call(
            functools.partial(cotangent_kernel, parts=len(parts)),
            (self.table(WIDE_ROWS),),
            WIDE_ROWS,
            parts
            + [
                self.columns(weights, channels, 1),
                self.rows(ga, WIDE_ROWS),
                self.across(square, WIDE_ROWS),
            ],
            [
                self.rows(self.out(channels, f32), WIDE_ROWS),
                self.across(jax.ShapeDtypeStruct((8, count), f32), WIDE_ROWS),
            ],
            [pltpu.VMEM((WIDE_ROWS, self.width), bf16)],
            2 * count * self.width * channels,
        )

    def gate(self, sums, prm, gate, u, y, gg):
        channels = self.channels
        return self.call(
            functools.partial(gate_kernel, taps=self.taps),
            (),
            WIDE_ROWS,
            [self.across(sums, WIDE_ROWS), self.whole(prm)] + [self.rows(z, WIDE_ROWS) for z in (gate, u, y, gg)],
            [self.rows(self.out(channels, bf16), WIDE_ROWS)] * 2
            + [self.rows(self.out(channels, f32), WIDE_ROWS)]
            + [self.whole(jax.ShapeDtypeStruct(prm.shape, f32))],
            [],
            self.group_rows * channels * 60,
        )

    def first_weights(self, cotangent, normed, dgate, gated, weights):
        channels = self.channels
        parts = self.parts(cotangent, WIDE_ROWS)
        return self.call(
            functools.partial(first_weights_kernel, parts=len(parts)),
            (self.table(WIDE_ROWS),),
            WIDE_ROWS,
            parts
            + [self.rows(z, WIDE_ROWS) for z in (normed, dgate, gated)]
            + [self.columns(weights, channels, 0)],
            [
                self.whole(jax.ShapeDtypeStruct((self.width, 2 * channels), bf16)),
                self.whole(jax.ShapeDtypeStruct((8, self.width), f32)),
            ],
            [pltpu.VMEM((WIDE_ROWS, self.width), bf16), pltpu.VMEM((self.width, 2 * channels), f32)],
            4 * self.group_rows * self.width * channels,
        )

    def last_weights(self, normed, gb, weights, gain, terms, dprm_gate, dprm, dprs, dprh):
        gradients = gb.shape[1]
        return self.call(
            functools.partial(last_weights_kernel, taps=self.taps),
            (self.first,),
            WIDE_ROWS,
            [self.rows(normed, WIDE_ROWS), self.rows(gb, WIDE_ROWS)]
            + [self.whole(z) for z in (weights, gain, terms, dprm_gate, dprm, dprs, dprh)],
            [
                self.whole(jax.ShapeDtypeStruct((self.width, gradients), bf16)),
                self.whole(jax.ShapeDtypeStruct((16, self.width), f32)),
            ],
            [pltpu.VMEM((self.width, gradients), f32)],
            2 * self.group_rows * self.width * gradients,
        )

    def backward(self, first_weights, weights, prm, prs, prh, saved):
        channels, count = self.channels, self.group_rows
        halves = self.halves(ROWS)
        result = self.call(
            functools.partial(backward_kernel, seqs=self.seqs, taps=self.taps, halves=len(halves)),
            (self.lengths, self.first, self.table(ROWS, True)),
            ROWS,
            [self.columns(first_weights, channels, 0)]
            + [self.whole(z) for z in (weights, prm, prs, prh)]
            + [self.rows(z, ROWS, True) for z in saved],
            [self.rows(self.out(channels + 3 * STATE, bf16), ROWS, True)]
            + halves
            + [self.whole(jax.ShapeDtypeStruct(z.shape, f32)) for z in (prm, prs, prh)],
            [
                pltpu.VMEM((ROWS + 8, channels), f32),
                pltpu.VMEM((ROWS + 8, 2 * STATE), f32),
                pltpu.VMEM((STATE, channels), f32),
                pltpu.VMEM((8, channels), f32),
            ],
            count * self.width * channels * 14,
            count * channels * 8,
        )
        return result[0], result[1 : 1 + len(halves)], result[1 + len(halves) :]


def per_device(
    hidden_in,
    norm_gain,
    proj_gate,
    proj_conv,
    proj_state,
    conv_kernel,
    conv_offset,
    state_kernel,
    state_offset,
    step_bias,
    decay_log,
    skip_gain,
    gate_gain,
    proj_out,
    out_cotangent,
    seq_lengths,
):
    tensor_count = lax.axis_size("tensor")
    tensor_place = lax.axis_index("tensor")
    dp_count = lax.axis_size("dp")
    dp_place = lax.axis_index("dp")
    square_mesh = tensor_count == 4
    own_rows, width = hidden_in.shape
    depth, channels = proj_gate.shape
    taps, heads_here, cut = conv_kernel.shape
    head_cut = step_bias.shape[0]
    state_cut = state_kernel.shape[1]
    state_width = proj_state.shape[1]
    group_rows = own_rows * tensor_count
    first_head = (tensor_place * heads_here).astype(jnp.int32)

    if square_mesh:
        hidden_all = gather_end(hidden_in, *gather_start(hidden_in))
    else:
        hidden_all = [lax.all_gather(hidden_in, "tensor", axis=0, tiled=True)]
    state_part = jnp.pad(proj_state, ((0, 0), (0, 3 * STATE - state_width)))
    weights = lax.all_gather(
        jnp.concatenate([proj_conv, state_part], axis=1), "dp", axis=0, tiled=True
    )
    first_weights = lax.all_gather(
        jnp.concatenate([proj_gate, proj_out.T], axis=1), "dp", axis=0, tiled=True
    )

    small = [
        norm_gain,
        conv_kernel,
        conv_offset,
        state_kernel,
        state_offset,
        step_bias,
        decay_log,
        skip_gain,
        gate_gain,
    ]
    flat = jnp.concatenate([z.reshape(-1) for z in small])
    flat = jnp.pad(flat, (0, -flat.shape[0] % 1024)).reshape(-1, LANES)
    small_all = lax.all_gather(flat, "dp", axis=0).reshape(dp_count, -1).astype(f32)
    shares, at = [], 0
    for z in small:
        shares.append(small_all[:, at : at + z.size].reshape((dp_count,) + z.shape))
        at += z.size
    gain_in = shares[0].reshape(1, width)
    taps_conv = shares[1].transpose(1, 2, 0, 3).reshape(taps, channels)
    off_conv = shares[2].transpose(1, 0, 2).reshape(1, channels)
    taps_state = shares[3].transpose(1, 0, 2).reshape(taps, 2 * STATE)
    off_state = shares[4].reshape(1, 2 * STATE)
    gain_gate = shares[8].transpose(1, 0, 2).reshape(1, channels)

    def own_heads(z):
        return lax.dynamic_slice_in_dim(z.reshape(-1), first_head, heads_here, 0)

    skip = jnp.repeat(own_heads(shares[7]), HEADDIM).reshape(1, channels)
    prm = jnp.concatenate([taps_conv, off_conv, skip, gain_gate], axis=0)
    prm = jnp.pad(prm, ((0, -prm.shape[0] % 8), (0, 0)))
    prs = jnp.concatenate([taps_state, off_state], axis=0)
    prs = jnp.pad(prs, ((0, -prs.shape[0] % 8), (0, 0)))
    prh = jnp.stack([own_heads(shares[5]), jnp.exp(own_heads(shares[6]))])
    prh = jnp.pad(prh, ((0, 6), (0, LANES - heads_here)))

    kernels = Kernels(
        seq_lengths,
        first_head.reshape(1),
        tensor_place,
        tensor_count,
        group_rows,
        width,
        channels,
        taps,
        heads_here,
    )

    hidden_all, cot = lax.optimization_barrier((hidden_all, out_cotangent))
    if square_mesh:
        moving = gather_start(cot)
    else:
        cotangent_all = [lax.all_gather(cot, "tensor", axis=0, tiled=True)]
    saved = kernels.scan(hidden_all, weights, gain_in, prm, prs, prh)
    if square_mesh:
        saved, moving = lax.optimization_barrier((saved, moving))
        cotangent_all = gather_end(cot, *moving)
    normed, v, u, vs, us, raw, y_scan, states = saved
    (gate_pre, ga, square), out_halves = kernels.value(normed, u, y_scan, prm, first_weights)
    if square_mesh:
        out_halves, cotangent_all = lax.optimization_barrier((out_halves, cotangent_all))
        moving = scatter_start(out_halves)
    gg, sums = kernels.cotangent(cotangent_all, first_weights, ga, square)
    if square_mesh:
        sums = sum_over_tensor(sums)
    else:
        sums = lax.psum(sums, "tensor")
    gated, dgate, dy, dprm_gate = kernels.gate(sums, prm, gate_pre, u, y_scan, gg)

    if square_mesh:
        gated, moving = lax.optimization_barrier((gated, moving))
        far, _ = scatter_middle(out_halves, *moving)
    grad_first, terms = kernels.first_weights(cotangent_all, normed, dgate, gated, first_weights)
    if square_mesh:
        grad_first, dy, far = lax.optimization_barrier((grad_first, dy, far))
        out_moving = moving + far
    own_first = lax.psum_scatter(grad_first, "dp", scatter_dimension=0, tiled=True)
    gb, gn_halves, small_grads = kernels.backward(
        first_weights, weights, prm, prs, prh, [dgate, dy, v, u, vs, us, raw, y_scan, states]
    )

    def own_sum(halves):
        return lax.psum_scatter(
            jnp.concatenate(halves, axis=1), "tensor", scatter_dimension=0, tiled=True
        ).astype(f32)

    if square_mesh:
        moving = scatter_start(gn_halves)
    grad_last, small_sum = kernels.last_weights(
        normed, gb, weights, gain_in, terms, dprm_gate, *small_grads
    )
    grad_last, own_first = lax.optimization_barrier((grad_last, own_first))
    own_last = lax.psum_scatter(grad_last, "dp", scatter_dimension=0, tiled=True)
    if square_mesh:
        small_sum, moving = lax.optimization_barrier((small_sum, moving))
        far, small_sum = scatter_middle(gn_halves, *moving, small_sum)
    small_sum = sum_over_dp(small_sum)
    small_shared = sum_over_tensor(small_sum) if square_mesh else lax.psum(small_sum, "tensor")

    if square_mesh:
        grad_normed = scatter_end(gn_halves, *moving, *far)
        branch = scatter_end(out_halves, *out_moving)
    else:
        grad_normed = own_sum(gn_halves)
        branch = own_sum(out_halves)

    own_square = lax.dynamic_slice_in_dim(sums[0], tensor_place * own_rows, own_rows, 0)
    inverse_gate = lax.rsqrt(own_square * (1.0 / INNER) + EPS)[:, None]
    values = hidden_in.astype(f32)
    block_out = (values + branch * inverse_gate).astype(bf16)

    inverse_in = lax.rsqrt(jnp.mean(values * values, axis=1, keepdims=True) + EPS)
    scaled = values * inverse_in
    grad_scaled = grad_normed * gain_in
    grad_hidden = out_cotangent.astype(f32) + inverse_in * (
        grad_scaled - scaled * jnp.mean(grad_scaled * scaled, axis=1, keepdims=True)
    )

    own_state = own_last[:, channels:]
    own_state = sum_over_tensor(own_state) if square_mesh else lax.psum(own_state.astype(f32), "tensor")
    own_part = depth // tensor_count
    own_state = lax.dynamic_slice_in_dim(own_state, tensor_place * own_part, own_part, 0)[:, :state_width]

    def own_cut(z, size, axis):
        return lax.dynamic_slice_in_dim(z, dp_place * size, size, axis)

    by_channel = small_sum[: taps + 3, :channels].reshape(taps + 3, heads_here, HEADDIM)
    by_channel = own_cut(by_channel, cut, 2)
    by_map = own_cut(small_shared[: taps + 1, channels : channels + 2 * STATE], state_cut, 1)
    heads_at = channels + 2 * STATE
    by_head = own_cut(small_shared[:3, heads_at : heads_at + LANES], head_cut, 1)
    gain_grad = lax.dynamic_slice_in_dim(
        small_shared[8], (dp_place * tensor_count + tensor_place) * own_part, own_part, 0
    )
    own_first = own_first.astype(f32)
    return (
        block_out,
        grad_hidden,
        gain_grad,
        own_first[:, :channels],
        own_last[:, :channels].astype(f32),
        own_state,
        own_first[:, channels:].T,
        by_channel[:taps],
        by_channel[taps],
        by_map[:taps],
        by_map[taps],
        by_head[0],
        by_head[1],
        by_head[2],
        by_channel[taps + 2],
    )


def solution(mesh):
    placed = (
        P(("dp", "tensor"), None),
        P("dp"),
        P("dp", "tensor"),
        P("dp", "tensor"),
        P("dp", None),
        P(None, "tensor", "dp"),
        P("tensor", "dp"),
        P(None, "dp"),
        P("dp"),
        P("dp"),
        P("dp"),
        P("dp"),
        P("tensor", "dp"),
        P("tensor", "dp"),
        P(("dp", "tensor"), None),
        P("dp", None),
    )
    return jax.shard_map(
        per_device,
        mesh=mesh,
        in_specs=placed,
        out_specs=(
            P(("dp", "tensor"), None),
            P(("dp", "tensor"), None),
            P(("dp", "tensor")),
            P("dp", "tensor"),
            P("dp", "tensor"),
            P(("dp", "tensor"), None),
            P("tensor", "dp"),
            P(None, "tensor", "dp"),
            P("tensor", "dp"),
            P(None, "dp"),
            P("dp"),
            P("dp"),
            P("dp"),
            P("dp"),
            P("tensor", "dp"),
        ),
        check_vma=False,
    )
```

time: 1240 us -> 302 us (0.24)
  local copies, waits for them, and re-layouts: 331 us -> 21.4 us
  matrix products: 274 us -> 0 us
  blocking collectives: 192 us -> 13 us
  other arithmetic: 189 us -> 21.8 us
  waiting for transfers between devices: 213 us -> 76.6 us
  Pallas kernels: 0 us -> 127 us
  starting transfers between devices: 0.7 us -> 26.2 us
  loops' own time: 12.4 us -> 0 us
    dot_general x106 -> x0, matrix products: 274 us -> none  [the longest x24 103 us: advance(): inner_y = jnp.einsum('hij,jhp->ihp', mixing, block_x, precision=highest)]
    dynamic_update_slice x83 -> x0, local copies, waits for them, and re-layouts: 234 us -> none  [the longest x80 233 us: block_scan(): lax.scan(advance, (start_state, jnp.array(-1, jnp.int32)), stacked)]
    reduce_scatter x6 -> x2, waiting for transfers between devices: 208 us -> 0.04 us  [the longest x1 0.02 us: per_device(): lax.psum_scatter(grad_last, 'dp', scatter_dimension=0, tiled=True)]
    pallas_call x0 -> x7, Pallas kernels: none -> 127 us  [call(): pl.pallas_call(kernel, grid_spec=pltpu.PrefetchScalarGridSpec(num_scalar_...]
    unnamed x3 -> x0, blocking collectives: 79.7 us -> none
    ppermute x0 -> x25, waiting for transfers between devices: none -> 76.5 us  [the longest x11 55.8 us: over_x(): return lax.ppermute(z, 'tensor', [(0, 1), (1, 0), (2, 3), (3, 2)])]
    all_gather x6 -> x1, blocking collectives: 78.8 us -> 13 us  [per_device(): lax.all_gather(flat, 'dp', axis=0).reshape(dp_count, -1).astype(f32)]
    dynamic_update_slice x73 -> x0, other arithmetic: 62.2 us -> none  [the longest x72 62.1 us: block_scan(): lax.scan(advance, (start_state, jnp.array(-1, jnp.int32)), stacked)]
  transfers between devices with their start and end apart: 13 -> 29, of which waited for: 6 -> 12; matrix products, arithmetic and copies ran while one was open for 34% -> 11% of each run, Pallas kernels for 0% -> 42%
where the time goes in v1:
time: 302 us; the launch traced here: 301 us
  Pallas kernels  127 us (42%)
  waiting for transfers between devices  76.6 us (25%)
  starting transfers between devices  26.2 us (9%)
  other arithmetic  21.8 us (7%)
  local copies, waits for them, and re-layouts  21.4 us (7%)
  between operations  15.1 us (5%)
  blocking collectives  13 us (4%)
    pallas_call x7, Pallas kernels, call(): pl.pallas_call(kernel, grid_spec=pltpu.PrefetchScalarGridSpec(num_scalar_...  127 us
    ppermute x11, waiting for transfers between devices, over_x(): return lax.ppermute(z, 'tensor', [(0, 1), (1, 0), (2, 3), (3, 2)])  55.8 us
    all_gather x1, blocking collectives, per_device(): lax.all_gather(flat, 'dp', axis=0).reshape(dp_count, -1).astype(f32)  13 us
    ppermute x11, starting transfers between devices, over_x(): return lax.ppermute(z, 'tensor', [(0, 1), (1, 0), (2, 3), (3, 2)])  12.2 us
    ppermute x11, waiting for transfers between devices, over_y(): return lax.ppermute(z, 'tensor', [(0, 2), (2, 0), (1, 3), (3, 1)])  11.5 us
    ppermute x11, starting transfers between devices, over_y(): return lax.ppermute(z, 'tensor', [(0, 2), (2, 0), (1, 3), (3, 1)])  11.2 us
    ppermute x3, waiting for transfers between devices, sum_over_dp(): z = z + lax.ppermute(z, 'dp', [(i, i ^ bit) for i in range(count)])  9.15 us
    unnamed x68, local copies, waits for them, and re-layouts  7.3 us
  transfers between devices with their start and end apart: 29, of which 12 were waited for; matrix products, arithmetic and copies ran while one was open for 11% of the time, Pallas kernels for 42%

profile of v1, /device:TPU:0, one launch (start us, length us, event | category | flops | bytes accessed | tf_op | source)
XLA Modules:
  0.0 301.0 jit_solution(12263175840447416381)
XLA Ops:
  7.3 1.1 copy.60
  8.4 1.6 fusion.9
  10.1 1.0 copy.66
  11.1 1.6 pad_maximum_fusion
  12.8 3.0 collective-permute-start
  15.8 1.5 collective-permute-start.1
  17.4 21.9 %collective-permute-done.refs_1_ = bf16[512,1024]{1,0:T(8,128)(2,1)S(1)} collective-permute-done((bf16[512,1024]{1,0:T(8,128)(2,1)}, bf16[512,1024]{1,0:T(8,128)(2,1)S(1)}, u32[]{:S(2)}, u32[]{:S(2)}) %collective-permute-start) | collective-permute-done | bytes 1048608 | tf_op jit(solution)/shard_map/ppermute | solution.py:590
  39.2 1.0 copy-done.5
  40.2 1.8 collective-permute-start.2
  42.1 1.0 copy-done.6
  43.1 1.6 collective-permute-start.3
  45.1 13.0 %all_gather.10 = bf16[8,8,128]{2,1,0:T(8,128)(2,1)S(1)} all-gather(bf16[1,8,128]{2,1,0:T(8,128)(2,1)S(1)} %pad_bitcast_fusion), channel_id=1, replica_groups=mesh['dp'=8,'tensor'=4] {'dp'}, dimensions={0}, use_global_device_ids=true | all-gather | bytes 18432 | tf_op jit(solution)/shard_map/all_gather | solution.py:918
  58.2 0.8 copy-done.20
  61.4 0.7 dynamic-slice_bitcast_fusion.3
  62.1 0.7 copy.65.place_ref
  66.1 26.8 %scan_kernel.1 = (bf16[2048,1024]{1,0:T(8,128)(2,1)}, bf16[2048,512]{1,0:T(8,128)(2,1)}, f32[2048,512]{1,0:T(8,128)}, bf16[2048,256]{1,0:T(8,128)(2,1)}, f32[204...) custom-call(s32[1,1]{1,0:T(1,128)S(6)} %copy.83.len_ref, ...), custom_call_target="tpu_custom_call" | custom-call | flops 1000 | bytes 1000 | tf_op jit(solution)/shard_map/scan_kernel/pallas_call | solution.py:665
  93.0 0.9 slice.152
  93.9 1.6 collective-permute-start.6
  95.4 0.8 slice.153
  96.2 1.6 collective-permute-start.7
  97.8 0.7 fusion.10
  98.5 0.7 copy.67.place_ref
  99.2 13.7 %value_kernel.1 = (f32[2048,512]{1,0:T(8,128)}, bf16[2048,512]{1,0:T(8,128)(2,1)}, f32[8,2048]{1,0:T(8,128)}, bf16[1024,512]{1,0:T(8,128)(2,1)}, bf16[1024,512]{...) custom-call(s32[9,4]{1,0:T(8,128)} %copy.67.place_ref, ...), custom_call_target="tpu_custom_call" | custom-call | flops 1000 | bytes 1000 | tf_op jit(solution)/shard_map/value_kernel/pallas_call | solution.py:665
  113.9 8.8 %cotangent_kernel.1 = (f32[2048,512]{1,0:T(8,128)}, f32[8,2048]{1,0:T(8,128)}) custom-call(s32[9,4]{1,0:T(8,128)} %copy.67.place_ref, bf16[512,1024]{1,0:T(8,128)(2,1)} %refs_0_.2, bf16[512,1024]{1,0:T(8,128)(2,1)} %copy-done.3, bf16[512,1024]{1,0:T(8,128)(2,1)} %copy-done.4, bf16[512,512]{1,0:T(8,128)(2,1)} %copy-done.7, bf16[512,512]{1,0:T(8,128)(2,1)} %copy-done.8, ...), custom_call_target="tpu_custom_call" | custom-call | flops 1000 | bytes 1000 | tf_op jit(solution)/shard_map/cotangent_kernel/pallas_call | solution.py:665
  122.7 1.7 collective-permute-start.8
  124.4 14.4 %collective-permute-done.8 = f32[8,2048]{1,0:T(8,128)S(1)} collective-permute-done((f32[8,2048]{1,0:T(8,128)}, f32[8,2048]{1,0:T(8,128)S(1)}, u32[]{:S(2)}, u32[]{:S(2)}) %collective-permute-start.8) | collective-permute-done | bytes 65568 | tf_op jit(solution)/shard_map/ppermute | solution.py:590
  138.8 0.9 add.142
  140.3 3.7 %collective-permute-done.9 = f32[8,2048]{1,0:T(8,128)S(1)} collective-permute-done((f32[8,2048]{1,0:T(8,128)S(1)}, f32[8,2048]{1,0:T(8,128)S(1)}, u32[]{:S(2)}, u32[]{:S(2)}) %collective-permute-start.9) | collective-permute-done | bytes 65568 | tf_op jit(solution)/shard_map/ppermute | solution.py:594
  144.7 11.7 %gate_kernel.1 = (bf16[2048,512]{1,0:T(8,128)(2,1)}, bf16[2048,512]{1,0:T(8,128)(2,1)}, f32[2048,512]{1,0:T(8,128)}, f32[8,512]{1,0:T(8,128)}) custom-call(f32[8,2048]{1,0:T(8,128)} %add.143.sums_ref, f32[8,512]{1,0:T(8,128)} %select_maximum_fusion.refs_7_.prm_ref.refs_2_, f32[2048,512]{1,0:T(8,128)} %get-tuple-element.122.gate_ref, ...), custom_call_target="tpu_custom_call" | custom-call | flops 1000 | bytes 1000 | tf_op jit(solution)/shard_map/gate_kernel/pallas_call | solution.py:665
  157.7 13.1 %first_weights_kernel.1 = (bf16[1024,1024]{1,0:T(8,128)(2,1)}, f32[8,1024]{1,0:T(8,128)}) custom-call(s32[9,4]{1,0:T(8,128)} %copy.67.place_ref, bf16[512,1024]{1,0:T(8,128)(2,1)} %refs_0_.2, bf16[512,1024]{1,0:T(8,128)(2,1)} %copy-done.3, bf16[512,1024]{1,0:T(8,128)(2,1)} %copy-done.4, bf16[512,512]{1,0:T(8,128)(2,1)} %copy-done.7, ...), custom_call_target="tpu_custom_call" | custom-call | flops 1000 | bytes 1000 | tf_op jit(solution)/shard_map/first_weights_kernel/pallas_call | solution.py:665
  170.8 0.8 copy-done.18
  171.8 0.7 dynamic-slice_bitcast_fusion.2
  172.5 0.7 copy.70.place_ref
  173.2 43.1 %backward_kernel.1 = (bf16[2048,896]{1,0:T(8,128)(2,1)}, bf16[1024,512]{1,0:T(8,128)(2,1)}, bf16[1024,512]{1,0:T(8,128)(2,1)}, bf16[1024,512]{1,0:T(8,128)(2,1)}...) custom-call(s32[1,1]{1,0:T(1,128)S(6)} %copy.83.len_ref, ...), custom_call_target="tpu_custom_call" | custom-call | flops 1000 | bytes 1000 | tf_op jit(solution)/shard_map/backward_kernel/pallas_call | solution.py:665
  216.3 1.7 collective-permute-start.14
  218.0 1.4 collective-permute-start.15
  219.7 9.8 %last_weights_kernel.1 = (bf16[1024,896]{1,0:T(8,128)(2,1)}, f32[16,1024]{1,0:T(8,128)}) custom-call(s32[1]{0:T(128)} %bitcast.1.first_ref, bf16[2048,1024]{1,0:T(8,128)(2,1)} %get-tuple-element.104.normed_ref.refs_5_, bf16[2048,896]{1,0:T(8,128)(2,1)} %get-tuple-element.145.gb_ref, bf16[1024,896]{1,0:T(8,128)(2,1)} %all-gather.3.cloned.1.call-done.refs_5_.refs_1_.w_ref, ...), custom_call_target="tpu_custom_call" | custom-call | flops 1000 | bytes 1000 | tf_op jit(solution)/shard_map/last_weights_kernel/pallas_call | solution.py:665
  229.7 8.6 %collective-permute-done.14 = bf16[1024,512]{1,0:T(8,128)(2,1)} collective-permute-done((bf16[1024,512]{1,0:T(8,128)(2,1)}, bf16[1024,512]{1,0:T(8,128)(2,1)}, u32[]{:S(2)}, u32[]{:S(2)}) %collective-permute-start.14) | collective-permute-done | bytes 1048608 | tf_op jit(solution)/shard_map/ppermute | solution.py:590
  238.3 1.4 collective-permute-done.15
  239.7 2.0 add_convert_fusion
  241.7 2.3 add_convert_fusion.1
  244.0 1.2 collective-permute-done.18
  245.2 1.6 collective-permute-start.19
  246.8 1.2 convert_add_fusion.4
  248.1 3.2 %collective-permute-done.19 = f32[16,1024]{1,0:T(8,128)S(1)} collective-permute-done((f32[16,1024]{1,0:T(8,128)S(1)}, f32[16,1024]{1,0:T(8,128)S(1)}, u32[]{:S(2)}, u32[]{:S(2)}) %collective-permute-start.19) | collective-permute-done | bytes 65568 | tf_op jit(solution)/shard_map/ppermute | solution.py:637
  251.2 0.9 collective-permute-start.20
  252.1 1.2 convert_add_fusion.3
  253.4 1.4 collective-permute-start.16
  254.8 0.7 collective-permute-start.17
  255.5 4.8 %collective-permute-done.20 = f32[16,1024]{1,0:T(8,128)S(1)} collective-permute-done((f32[16,1024]{1,0:T(8,128)S(1)}, f32[16,1024]{1,0:T(8,128)S(1)}, u32[]{:S(2)}, u32[]{:S(2)}) %collective-permute-start.20) | collective-permute-done | bytes 65568 | tf_op jit(solution)/shard_map/ppermute | solution.py:637
  260.4 0.7 constant_dynamic-slice_fusion
  261.1 8.3 %collective-permute-done.21 = f32[16,1024]{1,0:T(8,128)S(1)} collective-permute-done((f32[16,1024]{1,0:T(8,128)S(1)}, f32[16,1024]{1,0:T(8,128)S(1)}, u32[]{:S(2)}, u32[]{:S(2)}) %collective-permute-start.21) | collective-permute-done | bytes 65568 | tf_op jit(solution)/shard_map/ppermute | solution.py:590
  270.7 3.1 %collective-permute-done.22 = f32[16,1024]{1,0:T(8,128)S(1)} collective-permute-done((f32[16,1024]{1,0:T(8,128)S(1)}, f32[16,1024]{1,0:T(8,128)S(1)}, u32[]{:S(2)}, u32[]{:S(2)}) %collective-permute-start.22) | collective-permute-done | bytes 65568 | tf_op jit(solution)/shard_map/ppermute | solution.py:594
  276.1 1.5 convert_add_fusion.2
  277.7 1.4 convert_add_fusion.1
  279.7 0.7 copy-done.2
  280.4 2.1 fusion.5
  282.6 1.0 slice.203
  284.2 0.7 slice.201
  284.9 0.8 copy.71
  285.7 2.5 collective-permute-done.23
  288.3 0.9 add_convert_fusion.4
  289.8 0.7 slice_convert_fusion
  290.5 3.4 %collective-permute-done.24 = bf16[128,384]{1,0:T(8,128)(2,1)S(1)} collective-permute-done((bf16[128,384]{1,0:T(8,128)(2,1)S(1)}, bf16[128,384]{1,0:T(8,128)(2,1)S(1)}, u32[]{:S(2)}, u32[]{:S(2)}) %collective-permute-start.24) | collective-permute-done | bytes 98336 | tf_op jit(solution)/shard_map/ppermute | solution.py:594
  (164 shorter events, 16.2 us)
Async XLA Ops:
  7.2 37.4 %copy-start.23 = (bf16[4,8,8]{2,1,0:T(8,128)(2,1)S(1)}, bf16[4,8,8]{2,1,0:T(8,128)(2,1)}, u32[]{:S(2)}) copy-start(bf16[4,8,8]{2,1,0:T(8,128)(2,1)} %param.26) | copy-start | bytes 1540
  7.2 37.5 %copy-start.24 = (bf16[8,8]{1,0:T(8,128)(2,1)S(1)}, bf16[8,8]{1,0:T(8,128)(2,1)}, u32[]{:S(2)}) copy-start(bf16[8,8]{1,0:T(8,128)(2,1)} %param.27) | copy-start | bytes 388
  7.2 37.6 %copy-start.31 = (bf16[4,32]{1,0:T(4,128)(2,1)S(1)}, bf16[4,32]{1,0:T(4,128)(2,1)}, u32[]{:S(2)}) copy-start(bf16[4,32]{1,0:T(4,128)(2,1)} %param.28) | copy-start | bytes 772
  7.2 37.7 %copy-start.25 = (bf16[8,8]{1,0:T(8,128)(2,1)S(1)}, bf16[8,8]{1,0:T(8,128)(2,1)}, u32[]{:S(2)}) copy-start(bf16[8,8]{1,0:T(8,128)(2,1)} %param.33) | copy-start | bytes 388
  7.2 37.8 %copy-start.26 = (bf16[128]{0:T(256)(128)(2,1)S(1)}, bf16[128]{0:T(256)(128)(2,1)}, u32[]{:S(2)}) copy-start(bf16[128]{0:T(256)(128)(2,1)} %param.22) | copy-start | bytes 772
  7.2 37.8 %copy-start.27 = (bf16[32]{0:T(256)(128)(2,1)S(1)}, bf16[32]{0:T(256)(128)(2,1)}, u32[]{:S(2)}) copy-start(bf16[32]{0:T(256)(128)(2,1)} %param.29) | copy-start | bytes 196
  7.2 37.8 %copy-start.28 = (bf16[4]{0:T(256)(128)(2,1)S(1)}, bf16[4]{0:T(256)(128)(2,1)}, u32[]{:S(2)}) copy-start(bf16[4]{0:T(256)(128)(2,1)} %param.30) | copy-start | bytes 28
  7.3 37.8 %copy-start.29 = (bf16[4]{0:T(256)(128)(2,1)S(1)}, bf16[4]{0:T(256)(128)(2,1)}, u32[]{:S(2)}) copy-start(bf16[4]{0:T(256)(128)(2,1)} %param.31) | copy-start | bytes 28
  7.3 37.8 %copy-start.30 = (bf16[4]{0:T(256)(128)(2,1)S(1)}, bf16[4]{0:T(256)(128)(2,1)}, u32[]{:S(2)}) copy-start(bf16[4]{0:T(256)(128)(2,1)} %param.32) | copy-start | bytes 28
  7.3 51.8 %copy-start.1 = (bf16[512,1024]{1,0:T(8,128)(2,1)S(1)}, bf16[512,1024]{1,0:T(8,128)(2,1)}, u32[]{:S(2)}) copy-start(bf16[512,1024]{1,0:T(8,128)(2,1)} %refs_0_.2) | copy-start | bytes 3145732
  7.3 58.9 %all-gather.3.cloned.1.call-start = ((), (), s32[]{:S(2)}) async-start(), calls=%async_computation.2 | async-start | bytes 2064384 | tf_op jit(solution)/shard_map/all_gather | solution.py:898
  10.1 89.1 %all-gather.5.cloned.1.call-start = ((), (), s32[]{:S(2)}) async-start(), calls=%async_computation.3 | async-start | bytes 2359296 | tf_op jit(solution)/shard_map/all_gather | solution.py:901
  12.8 216.8 %reduce-scatter.3.cloned.1.call-start = ((), (), s32[]{:S(2)}) async-start(), calls=%async_computation.4 | async-start | bytes 2359296 | tf_op jit(solution)/shard_map/reduce_scatter | solution.py:981
  12.8 26.4 %collective-permute-start = (bf16[512,1024]{1,0:T(8,128)(2,1)}, bf16[512,1024]{1,0:T(8,128)(2,1)S(1)}, u32[]{:S(2)}, u32[]{:S(2)}) collective-permute-start(bf16[512,1024]{1,0:T(8,128)(2,1)} %refs_0_), channel_id=1, source_target_pairs={{0,1},{1,0},{2,3},{3,2},{4,5},{5,4},{6,7},{7,6},{8,9},{9,8},{10,11... | collective-permute-start | bytes 3145736 | tf_op jit(solution)/shard_map/ppermute | solution.py:590
  15.8 26.2 %collective-permute-start.1 = (bf16[512,1024]{1,0:T(8,128)(2,1)}, bf16[512,1024]{1,0:T(8,128)(2,1)S(1)}, u32[]{:S(2)}, u32[]{:S(2)}) collective-permute-start(bf16[512,1024]{1,0:T(8,128)(2,1)} %refs_0_), channel_id=1, source_target_pairs={{0,2},{2,0},{1,3},{3,1},{4,6},{6,4},{5,7},{7,5},{8,10},{10,8},{9,1... | collective-permute-start | bytes 3145736 | tf_op jit(solution)/shard_map/ppermute | solution.py:594
  39.2 1.0 copy-start.5
  40.2 18.0 %collective-permute-start.2 = (bf16[512,512]{1,0:T(8,128)(2,1)S(1)}, bf16[512,512]{1,0:T(8,128)(2,1)S(1)}, u32[]{:S(2)}, u32[]{:S(2)}) collective-permute-start(bf16[512,512]{1,0:T(8,128)(2,1)S(1)} %slice.188), channel_id=1, source_target_pairs={{0,2},{2,0},{1,3},{3,1},{4,6},{6,4},{5,7},{7,5},{8,10},{10,8},{9,1... | collective-permute-start | bytes 1572872 | tf_op jit(solution)/shard_map/ppermute | solution.py:594
  42.1 1.0 copy-start.6
  43.1 16.0 %collective-permute-start.3 = (bf16[512,512]{1,0:T(8,128)(2,1)S(1)}, bf16[512,512]{1,0:T(8,128)(2,1)}, u32[]{:S(2)}, u32[]{:S(2)}) collective-permute-start(bf16[512,512]{1,0:T(8,128)(2,1)S(1)} %slice.189), channel_id=1, source_target_pairs={{0,1},{1,0},{2,3},{3,2},{4,5},{5,4},{6,7},{7,6},{8,9},{9,8},{10,11... | collective-permute-start | bytes 1572872 | tf_op jit(solution)/shard_map/ppermute | solution.py:590
  58.2 0.8 copy-start.20
  59.1 33.9 %collective-permute-start.4 = (bf16[512,1024]{1,0:T(8,128)(2,1)S(1)}, bf16[512,1024]{1,0:T(8,128)(2,1)S(1)}, u32[]{:S(2)}, u32[]{:S(2)}) collective-permute-start(bf16[512,1024]{1,0:T(8,128)(2,1)S(1)} %copy-done.1), channel_id=1, source_target_pairs={{0,1},{1,0},{2,3},{3,2},{4,5},{5,4},{6,7},{7,6},{8,9},{9,8},{10,11... | collective-permute-start | bytes 3145736 | tf_op jit(solution)/shard_map/ppermute | solution.py:590
  59.5 33.5 %collective-permute-start.5 = (bf16[512,1024]{1,0:T(8,128)(2,1)S(1)}, bf16[512,1024]{1,0:T(8,128)(2,1)S(1)}, u32[]{:S(2)}, u32[]{:S(2)}) collective-permute-start(bf16[512,1024]{1,0:T(8,128)(2,1)S(1)} %copy-done.1), channel_id=1, source_target_pairs={{0,2},{2,0},{1,3},{3,1},{4,6},{6,4},{5,7},{7,5},{8,10},{10,8},{9,1... | collective-permute-start | bytes 3145736 | tf_op jit(solution)/shard_map/ppermute | solution.py:594
  92.9 19.9 %copy-start.3 = (bf16[512,1024]{1,0:T(8,128)(2,1)}, bf16[512,1024]{1,0:T(8,128)(2,1)S(1)}, u32[]{:S(2)}) copy-start(bf16[512,1024]{1,0:T(8,128)(2,1)S(1)} %collective-permute-done.4.refs_1_) | copy-start | bytes 3145732
  93.0 19.9 %copy-start.4 = (bf16[512,1024]{1,0:T(8,128)(2,1)}, bf16[512,1024]{1,0:T(8,128)(2,1)S(1)}, u32[]{:S(2)}) copy-start(bf16[512,1024]{1,0:T(8,128)(2,1)S(1)} %collective-permute-done.5.refs_2_) | copy-start | bytes 3145732
  93.9 19.0 %collective-permute-start.6 = (bf16[512,512]{1,0:T(8,128)(2,1)}, bf16[512,512]{1,0:T(8,128)(2,1)S(1)}, u32[]{:S(2)}, u32[]{:S(2)}) collective-permute-start(bf16[512,512]{1,0:T(8,128)(2,1)} %slice.152), channel_id=1, source_target_pairs={{0,2},{2,0},{1,3},{3,1},{4,6},{6,4},{5,7},{7,5},{8,10},{10,8},{9,1... | collective-permute-start | bytes 1572872 | tf_op jit(solution)/shard_map/ppermute | solution.py:594
  96.2 16.7 %collective-permute-start.7 = (bf16[512,512]{1,0:T(8,128)(2,1)}, bf16[512,512]{1,0:T(8,128)(2,1)S(1)}, u32[]{:S(2)}, u32[]{:S(2)}) collective-permute-start(bf16[512,512]{1,0:T(8,128)(2,1)} %slice.153), channel_id=1, source_target_pairs={{0,1},{1,0},{2,3},{3,2},{4,5},{5,4},{6,7},{7,6},{8,9},{9,8},{10,11... | collective-permute-start | bytes 1572872 | tf_op jit(solution)/shard_map/ppermute | solution.py:590
  112.9 1.0 copy-start.7
  112.9 1.0 copy-start.8
  112.9 43.4 %collective-permute-start.10 = (bf16[1024,512]{1,0:T(8,128)(2,1)}, bf16[1024,512]{1,0:T(8,128)(2,1)S(1)}, u32[]{:S(2)}, u32[]{:S(2)}) collective-permute-start(bf16[1024,512]{1,0:T(8,128)(2,1)} %get-tuple-element.125), channel_id=1, source_target_pairs={{0,1},{1,0},{2,3},{3,2},{4,5},{5,4},{6,7},{7,6},{8,9},{9,8},{10,11... | collective-permute-start | bytes 3145736 | tf_op jit(solution)/shard_map/ppermute | solution.py:590
  113.4 42.9 %collective-permute-start.11 = (bf16[1024,512]{1,0:T(8,128)(2,1)}, bf16[1024,512]{1,0:T(8,128)(2,1)S(1)}, u32[]{:S(2)}, u32[]{:S(2)}) collective-permute-start(bf16[1024,512]{1,0:T(8,128)(2,1)} %get-tuple-element.126), channel_id=1, source_target_pairs={{0,2},{2,0},{1,3},{3,1},{4,6},{6,4},{5,7},{7,5},{8,10},{10,8},{9,1... | collective-permute-start | bytes 3145736 | tf_op jit(solution)/shard_map/ppermute | solution.py:594
  122.7 16.1 %collective-permute-start.8 = (f32[8,2048]{1,0:T(8,128)}, f32[8,2048]{1,0:T(8,128)S(1)}, u32[]{:S(2)}, u32[]{:S(2)}) collective-permute-start(f32[8,2048]{1,0:T(8,128)} %get-tuple-element.121), channel_id=1, source_target_pairs={{0,1},{1,0},{2,3},{3,2},{4,5},{5,4},{6,7},{7,6},{8,9},{9,8},{10,11... | collective-permute-start | bytes 196616 | tf_op jit(solution)/shard_map/ppermute | solution.py:590
  139.7 4.3 %collective-permute-start.9 = (f32[8,2048]{1,0:T(8,128)S(1)}, f32[8,2048]{1,0:T(8,128)S(1)}, u32[]{:S(2)}, u32[]{:S(2)}) collective-permute-start(f32[8,2048]{1,0:T(8,128)S(1)} %add.142), channel_id=1, source_target_pairs={{0,2},{2,0},{1,3},{3,1},{4,6},{6,4},{5,7},{7,5},{8,10},{10,8},{9,1... | collective-permute-start | bytes 196616 | tf_op jit(solution)/shard_map/ppermute | solution.py:594
  144.7 11.7 %copy-start.9 = (bf16[1024,512]{1,0:T(8,128)(2,1)S(1)}, bf16[1024,512]{1,0:T(8,128)(2,1)}, u32[]{:S(2)}) copy-start(bf16[1024,512]{1,0:T(8,128)(2,1)} %get-tuple-element.132) | copy-start | bytes 3145732
  144.7 11.9 %copy-start.11 = (bf16[1024,512]{1,0:T(8,128)(2,1)S(1)}, bf16[1024,512]{1,0:T(8,128)(2,1)}, u32[]{:S(2)}) copy-start(bf16[1024,512]{1,0:T(8,128)(2,1)} %get-tuple-element.113) | copy-start | bytes 3145732
  156.3 14.4 %copy-start.14 = (bf16[1024,512]{1,0:T(8,128)(2,1)}, bf16[1024,512]{1,0:T(8,128)(2,1)S(1)}, u32[]{:S(2)}) copy-start(bf16[1024,512]{1,0:T(8,128)(2,1)S(1)} %collective-permute-done.10) | copy-start | bytes 3145732
  156.3 14.4 %copy-start.12 = (bf16[1024,512]{1,0:T(8,128)(2,1)}, bf16[1024,512]{1,0:T(8,128)(2,1)S(1)}, u32[]{:S(2)}) copy-start(bf16[1024,512]{1,0:T(8,128)(2,1)S(1)} %collective-permute-done.11) | copy-start | bytes 3145732
  156.7 14.1 %collective-permute-start.12 = (bf16[512,512]{1,0:T(8,128)(2,1)S(1)}, bf16[512,512]{1,0:T(8,128)(2,1)S(1)}, u32[]{:S(2)}, u32[]{:S(2)}) collective-permute-start(bf16[512,512]{1,0:T(8,128)(2,1)S(1)} %add_convert_fusion.3), channel_id=1, source_target_pairs={{0,2},{2,0},{1,3},{3,1},{4,6},{6,4},{5,7},{7,5},{8,10},{10,8},{9,1... | collective-permute-start | bytes 1572872 | tf_op jit(solution)/shard_map/ppermute | solution.py:594
  157.3 14.3 %collective-permute-start.13 = (bf16[512,512]{1,0:T(8,128)(2,1)S(1)}, bf16[512,512]{1,0:T(8,128)(2,1)}, u32[]{:S(2)}, u32[]{:S(2)}) collective-permute-start(bf16[512,512]{1,0:T(8,128)(2,1)S(1)} %add_convert_fusion.2), channel_id=1, source_target_pairs={{0,1},{1,0},{2,3},{3,2},{4,5},{5,4},{6,7},{7,6},{8,9},{9,8},{10,11... | collective-permute-start | bytes 1572872 | tf_op jit(solution)/shard_map/ppermute | solution.py:590
  170.8 0.8 copy-start.18
  171.6 111.0 %reduce-scatter.5.cloned.1.call-start = ((), (), s32[]{:S(2)}) async-start(), calls=%async_computation.5 | async-start | bytes 2064384 | tf_op jit(solution)/shard_map/reduce_scatter | solution.py:997
  173.2 46.2 %copy-start = (bf16[512,1024]{1,0:T(8,128)(2,1)S(1)}, bf16[512,1024]{1,0:T(8,128)(2,1)}, u32[]{:S(2)}) copy-start(bf16[512,1024]{1,0:T(8,128)(2,1)} %refs_0_) | copy-start | bytes 3145732
  216.3 22.0 %collective-permute-start.14 = (bf16[1024,512]{1,0:T(8,128)(2,1)}, bf16[1024,512]{1,0:T(8,128)(2,1)}, u32[]{:S(2)}, u32[]{:S(2)}) collective-permute-start(bf16[1024,512]{1,0:T(8,128)(2,1)} %get-tuple-element.152), channel_id=1, source_target_pairs={{0,1},{1,0},{2,3},{3,2},{4,5},{5,4},{6,7},{7,6},{8,9},{9,8},{10,11... | collective-permute-start | bytes 3145736 | tf_op jit(solution)/shard_map/ppermute | solution.py:590
  218.0 21.7 %collective-permute-start.15 = (bf16[1024,512]{1,0:T(8,128)(2,1)}, bf16[1024,512]{1,0:T(8,128)(2,1)}, u32[]{:S(2)}, u32[]{:S(2)}) collective-permute-start(bf16[1024,512]{1,0:T(8,128)(2,1)} %get-tuple-element.153), channel_id=1, source_target_pairs={{0,2},{2,0},{1,3},{3,1},{4,6},{6,4},{5,7},{7,5},{8,10},{10,8},{9,1... | collective-permute-start | bytes 3145736 | tf_op jit(solution)/shard_map/ppermute | solution.py:594
  229.6 10.1 %copy-start.15 = (bf16[1024,512]{1,0:T(8,128)(2,1)S(1)}, bf16[1024,512]{1,0:T(8,128)(2,1)}, u32[]{:S(2)}) copy-start(bf16[1024,512]{1,0:T(8,128)(2,1)} %get-tuple-element.155) | copy-start | bytes 3145732
  229.6 14.4 %copy-start.22 = (f32[16,1024]{1,0:T(8,128)S(1)}, f32[16,1024]{1,0:T(8,128)}, u32[]{:S(2)}) copy-start(f32[16,1024]{1,0:T(8,128)} %get-tuple-element.160) | copy-start | bytes 196612
  229.6 14.3 %slice-start = ((f32[8,2048]{1,0:T(8,128)}), f32[1,2048]{1,0:T(1,128)S(1)}, s32[]{:S(2)}) async-start(f32[8,2048]{1,0:T(8,128)} %add.143.sums_ref), calls=%async_computation.6 | async-start | bytes 16384 | tf_op jit(solution)/shard_map/slice | solution.py:1011
  229.7 17.2 %copy-start.19 = (bf16[512,512]{1,0:T(8,128)(2,1)S(1)}, bf16[512,512]{1,0:T(8,128)(2,1)}, u32[]{:S(2)}) copy-start(bf16[512,512]{1,0:T(8,128)(2,1)} %copy-done.18) | copy-start | bytes 1572868
  241.6 10.5 %copy-start.10 = (bf16[1024,512]{1,0:T(8,128)(2,1)S(1)}, bf16[1024,512]{1,0:T(8,128)(2,1)}, u32[]{:S(2)}) copy-start(bf16[1024,512]{1,0:T(8,128)(2,1)} %get-tuple-element.132) | copy-start | bytes 3145732
  241.7 10.5 %copy-start.13 = (bf16[1024,512]{1,0:T(8,128)(2,1)S(1)}, bf16[1024,512]{1,0:T(8,128)(2,1)}, u32[]{:S(2)}) copy-start(bf16[1024,512]{1,0:T(8,128)(2,1)} %copy-done.12) | copy-start | bytes 3145732
  243.9 1.3 collective-permute-start.18
  245.2 6.0 %collective-permute-start.19 = (f32[16,1024]{1,0:T(8,128)S(1)}, f32[16,1024]{1,0:T(8,128)S(1)}, u32[]{:S(2)}, u32[]{:S(2)}) collective-permute-start(f32[16,1024]{1,0:T(8,128)S(1)} %add.163), channel_id=1, source_target_pairs={{0,8},{4,12},{8,0},{12,4},{16,24},{20,28},{24,16},{28,20},{1,9},{5... | collective-permute-start | bytes 196616 | tf_op jit(solution)/shard_map/ppermute | solution.py:637
  251.2 9.0 %collective-permute-start.20 = (f32[16,1024]{1,0:T(8,128)S(1)}, f32[16,1024]{1,0:T(8,128)S(1)}, u32[]{:S(2)}, u32[]{:S(2)}) collective-permute-start(f32[16,1024]{1,0:T(8,128)S(1)} %add.164), channel_id=1, source_target_pairs={{0,16},{4,20},{8,24},{12,28},{16,0},{20,4},{24,8},{28,12},{1,17},{... | collective-permute-start | bytes 196616 | tf_op jit(solution)/shard_map/ppermute | solution.py:637
  253.4 22.8 %collective-permute-start.16 = (bf16[512,512]{1,0:T(8,128)(2,1)}, bf16[512,512]{1,0:T(8,128)(2,1)}, u32[]{:S(2)}, u32[]{:S(2)}) collective-permute-start(bf16[512,512]{1,0:T(8,128)(2,1)} %add_convert_fusion.1), channel_id=1, source_target_pairs={{0,2},{2,0},{1,3},{3,1},{4,6},{6,4},{5,7},{7,5},{8,10},{10,8},{9,1... | collective-permute-start | bytes 1572872 | tf_op jit(solution)/shard_map/ppermute | solution.py:594
  254.8 23.0 %collective-permute-start.17 = (bf16[512,512]{1,0:T(8,128)(2,1)}, bf16[512,512]{1,0:T(8,128)(2,1)}, u32[]{:S(2)}, u32[]{:S(2)}) collective-permute-start(bf16[512,512]{1,0:T(8,128)(2,1)} %add_convert_fusion), channel_id=1, source_target_pairs={{0,1},{1,0},{2,3},{3,2},{4,5},{5,4},{6,7},{7,6},{8,9},{9,8},{10,11... | collective-permute-start | bytes 1572872 | tf_op jit(solution)/shard_map/ppermute | solution.py:590
  260.2 9.2 %collective-permute-start.21 = (f32[16,1024]{1,0:T(8,128)S(1)}, f32[16,1024]{1,0:T(8,128)S(1)}, u32[]{:S(2)}, u32[]{:S(2)}) collective-permute-start(f32[16,1024]{1,0:T(8,128)S(1)} %add.165), channel_id=1, source_target_pairs={{0,1},{1,0},{2,3},{3,2},{4,5},{5,4},{6,7},{7,6},{8,9},{9,8},{10,11... | collective-permute-start | bytes 196616 | tf_op jit(solution)/shard_map/ppermute | solution.py:590
  260.4 17.3 %copy-start.16 = (bf16[1024,512]{1,0:T(8,128)(2,1)S(1)}, bf16[1024,512]{1,0:T(8,128)(2,1)}, u32[]{:S(2)}) copy-start(bf16[1024,512]{1,0:T(8,128)(2,1)} %get-tuple-element.155) | copy-start | bytes 3145732
  269.4 4.3 %collective-permute-start.22 = (f32[16,1024]{1,0:T(8,128)S(1)}, f32[16,1024]{1,0:T(8,128)S(1)}, u32[]{:S(2)}, u32[]{:S(2)}) collective-permute-start(f32[16,1024]{1,0:T(8,128)S(1)} %add.166), channel_id=1, source_target_pairs={{0,2},{2,0},{1,3},{3,1},{4,6},{6,4},{5,7},{7,5},{8,10},{10,8},{9,1... | collective-permute-start | bytes 196616 | tf_op jit(solution)/shard_map/ppermute | solution.py:594
  279.1 1.2 copy-start.2
  280.4 2.2 copy-start.17
  282.6 7.2 %copy-start.21 = (bf16[128,896]{1,0:T(8,128)(2,1)S(1)}, bf16[128,896]{1,0:T(8,128)(2,1)}, u32[]{:S(2)}) copy-start(bf16[128,896]{1,0:T(8,128)(2,1)} %reduce-scatter.5.cloned.1.call-done) | copy-start | bytes 688132
  283.6 4.7 %collective-permute-start.23 = (bf16[128,384]{1,0:T(8,128)(2,1)S(1)}, bf16[128,384]{1,0:T(8,128)(2,1)S(1)}, u32[]{:S(2)}, u32[]{:S(2)}) collective-permute-start(bf16[128,384]{1,0:T(8,128)(2,1)S(1)} %slice.203), channel_id=1, source_target_pairs={{0,1},{1,0},{2,3},{3,2},{4,5},{5,4},{6,7},{7,6},{8,9},{9,8},{10,11... | collective-permute-start | bytes 294920 | tf_op jit(solution)/shard_map/ppermute | solution.py:590
  289.2 4.7 %collective-permute-start.24 = (bf16[128,384]{1,0:T(8,128)(2,1)S(1)}, bf16[128,384]{1,0:T(8,128)(2,1)S(1)}, u32[]{:S(2)}, u32[]{:S(2)}) collective-permute-start(bf16[128,384]{1,0:T(8,128)(2,1)S(1)} %add_convert_fusion.4), channel_id=1, source_target_pairs={{0,2},{2,0},{1,3},{3,1},{4,6},{6,4},{5,7},{7,5},{8,10},{10,8},{9,1... | collective-permute-start | bytes 294920 | tf_op jit(solution)/shard_map/ppermute | solution.py:594
Sparse Core Ops, SparseCore 0:
  10.3 29.6 all-gather.2
  42.2 28.7 all-gather.4
  171.7 35.7 reduce-scatter.2
  229.8 34.1 reduce-scatter.4

commit v2 on v1

v2 whole, which is shorter than its diff:
```python
import functools

import jax
import jax.numpy as jnp
import numpy as np
from jax import lax
from jax.experimental import pallas as pl
from jax.experimental.pallas import tpu as pltpu
from jax.sharding import PartitionSpec as P

HEADDIM = 64
STATE = 128
INNER = 2048
LANES = 128
ROWS = 256
WIDE_ROWS = 512
FIELD = 32
SUB = 128
EPS = 1e-05
LOG2E = 1.4426950408889634

f32 = jnp.float32
bf16 = jnp.bfloat16


def nn(a, b):
    return lax.dot_general(a, b, (((1,), (0,)), ((), ())), preferred_element_type=f32)


def nt(a, b):
    return lax.dot_general(a, b, (((1,), (1,)), ((), ())), preferred_element_type=f32)


def tn(a, b):
    return lax.dot_general(a, b, (((0,), (0,)), ((), ())), preferred_element_type=f32)


def pieces(z, count):
    parts = []
    for _ in range(count - 1):
        part = z.astype(bf16)
        parts.append(part)
        z = z - part.astype(f32)
    parts.append(z.astype(bf16))
    return parts


def spread_heads(z, heads):
    return nn(jnp.concatenate(pieces(z, 2), axis=1), heads)


def gather_heads(z, heads):
    return nn(jnp.concatenate(pieces(z, 2), axis=1), heads)


def triangle_sum(triangle, z):
    return nn(triangle, jnp.concatenate(pieces(z, 3), axis=0))


def constants(channels):
    row, col = np.arange(ROWS)[:, None], np.arange(ROWS)[None, :]
    same = row // SUB == col // SUB
    lower = np.concatenate([same & (row >= col)] * 3, axis=1)
    upper = np.concatenate([same & (row <= col)] * 3, axis=1)
    heads = np.arange(LANES)[:, None] == np.arange(channels)[None, :] // HEADDIM
    spread = np.concatenate([heads] * 2, axis=0)
    gather = np.concatenate([heads.T] * 2, axis=0)
    return [jnp.asarray(z, bf16) for z in (lower, upper, spread, gather)]


def ends_of(len_ref, count):
    ends, total = [], 0
    for s in range(count):
        total = total + len_ref[0, s]
        ends.append(total)
    return ends


def segment_of(places, ends):
    return sum((places >= end).astype(jnp.int32) for end in ends)


def start_of(places, ends):
    start = jnp.zeros_like(places)
    for end in ends:
        start = jnp.where(places >= end, end, start)
    return start


def scan_steps(raw, decay, lower):
    step = jnp.maximum(raw, 0.0) + jnp.log1p(jnp.exp(-jnp.abs(raw)))
    return step, triangle_sum(lower, -decay * step)


def scan_weights(step, cum, base, ends, spread):
    rows = step.shape[0]
    segment = segment_of(base + lax.broadcasted_iota(jnp.int32, (rows, 1), 0), ends)
    carried, keep, survive = [], [], []
    for low in range(0, rows, SUB):
        before = segment_of(base + low - 1, ends)
        tail = segment_of(base + low + SUB - 1, ends)
        part, own = cum[low : low + SUB], segment[low : low + SUB]
        last = part[SUB - 1 :]
        carried.append(jnp.where(own == before, jnp.exp(part), 0.0))
        keep.append(jnp.where(own == tail, jnp.exp(last - part), 0.0))
        survive.append(jnp.where(tail == before, jnp.exp(last), 0.0))
    survive.append(jnp.zeros((-len(survive) % 8, LANES), f32))
    wide = spread_heads(jnp.concatenate([step] + carried + keep + survive, axis=0), spread)
    return wide[:rows], wide[rows : 2 * rows], wide[2 * rows : 3 * rows], wide[3 * rows :]


def pair_stack(z):
    lane = lax.broadcasted_iota(jnp.int32, z.shape, 1)
    zero = jnp.zeros_like(z)
    return jnp.concatenate(
        [jnp.where(lane < HEADDIM, z, zero), jnp.where(lane >= HEADDIM, z, zero)], axis=0
    )


def silu(u):
    return u * jax.nn.sigmoid(u)


def own_lanes(z, shift, count):
    moved = pltpu.roll(z, (z.shape[1] - shift) % z.shape[1], 1)
    lane = lax.broadcasted_iota(jnp.int32, z.shape, 1)
    return jnp.where(lane < count, moved, 0.0)


def nn3(a, b):
    a, a_low = pieces(a, 2)
    b, b_low = pieces(b, 2)
    return nn(jnp.concatenate([a, a_low, a], axis=1), jnp.concatenate([b, b, b_low], axis=0))


def nt3(a, b):
    a, a_low = pieces(a, 2)
    b, b_low = pieces(b, 2)
    return nt(jnp.concatenate([a, a_low, a], axis=1), jnp.concatenate([b, b, b_low], axis=1))


def pair_product(mixing, z):
    high, low = pieces(z, 2)
    both = nn(
        jnp.concatenate(mixing, axis=1),
        jnp.concatenate([pair_stack(high), pair_stack(low)], axis=1),
    )
    return both[:, :LANES] + both[:, LANES:]


def take_rows(refs, which, buffer):
    if len(refs) == 1:
        return refs[0][...]
    half = refs[3].shape[1]
    for k in range(3):

        @pl.when(which == k)
        def _(k=k):
            buffer[...] = refs[k][...]

    @pl.when(which == 3)
    def _():
        buffer[:, :half] = refs[3][...]
        buffer[:, half:] = refs[4][...]

    return buffer[...]


def put_halves(refs, which, product):
    half = product.shape[1] // 2
    left, right = product[:, :half], product[:, half:]
    if len(refs) == 2:
        refs[0][...] = left
        refs[1][...] = right
        return
    left_sent, left_kept, right_sent, right_kept = refs

    @pl.when(which % 2 == 1)
    def _():
        left_sent[...] = left

    @pl.when(which % 2 == 0)
    def _():
        left_kept[...] = left

    @pl.when(which >= 2)
    def _():
        right_sent[...] = right

    @pl.when(which < 2)
    def _():
        right_kept[...] = right


def scan_kernel(
    len_ref, first_ref, place_ref, *refs, parts, seqs, taps, head_count, first_block, kept, starts, place_at
):
    part_refs, refs = refs[:parts], refs[parts:]
    w_ref, gain_ref, prm_ref, prs_ref, prh_ref, lower_ref, spread_ref = refs[:7]
    start_refs, refs = refs[7 : 7 + starts], refs[7 + starts :]
    (
        normed_ref,
        v_ref,
        u_ref,
        vs_ref,
        us_ref,
        terms_ref,
        y_ref,
        st_ref,
        gate_ref,
        ga_ref,
        total_ref,
        square_ref,
        vtail_out,
        stail_out,
        carry,
        hid_buf,
        vbuf,
        sbuf,
    ) = refs[kept:]
    rows, channels = v_ref.shape
    step_id = pl.program_id(0)
    block = step_id + first_block
    base = block * rows
    ends = ends_of(len_ref, seqs)

    @pl.when(step_id == 0)
    def _():
        if start_refs:
            vbuf[0:8, :] = start_refs[0][...]
            sbuf[0:8, :] = start_refs[1][...]
            carry[...] = start_refs[2][...]
        else:
            vbuf[0:8, :] = jnp.zeros((8, channels), f32)
            sbuf[0:8, :] = jnp.zeros((8, 2 * STATE), f32)
            carry[...] = jnp.zeros_like(carry)

    values = take_rows(part_refs, place_ref[place_at + block], hid_buf).astype(f32)
    inverse = lax.rsqrt(jnp.mean(values * values, axis=1, keepdims=True) + EPS)
    normed = (values * inverse * gain_ref[...]).astype(bf16)
    normed_ref[...] = normed
    gate_pre = nn(normed, w_ref[:, :channels])
    gate_ref[...] = gate_pre.astype(bf16)
    conv_pre = nn(normed, w_ref[:, channels : 2 * channels])
    state_all = nn(normed, w_ref[:, 2 * channels :])
    v_ref[...] = conv_pre.astype(bf16)
    vs_ref[...] = state_all[:, : 2 * STATE].astype(bf16)
    vbuf[8 : 8 + rows, :] = conv_pre
    sbuf[8 : 8 + rows, :] = state_all[:, : 2 * STATE]
    start = start_of(base + lax.broadcasted_iota(jnp.int32, (rows, 1), 0), ends)
    u = prm_ref[taps : taps + 1, :] + prm_ref[taps - 1 : taps, :] * conv_pre
    us = prs_ref[taps : taps + 1, :] + prs_ref[taps - 1 : taps, :] * state_all[:, : 2 * STATE]
    for lag in range(1, taps):
        usable = base + lax.broadcasted_iota(jnp.int32, (rows, 1), 0) - lag >= start
        tap = taps - 1 - lag
        u = u + prm_ref[tap : tap + 1, :] * jnp.where(usable, vbuf[8 - lag : 8 - lag + rows, :], 0.0)
        us = us + prs_ref[tap : tap + 1, :] * jnp.where(usable, sbuf[8 - lag : 8 - lag + rows, :], 0.0)
    vbuf[0:8, :] = vbuf[rows : rows + 8, :]
    sbuf[0:8, :] = sbuf[rows : rows + 8, :]
    vtail_out[...] = vbuf[0:8, :]
    stail_out[...] = sbuf[0:8, :]
    u_ref[...] = u
    us_ref[...] = us
    raw = own_lanes(state_all[:, 2 * STATE :], first_ref[0], head_count) + prh_ref[0:1, :]

    x = silu(u)
    maps = silu(us)
    step, cum = scan_steps(raw, prh_ref[1:2, :], lower_ref[...])
    lane = lax.broadcasted_iota(jnp.int32, (rows, LANES), 1)
    terms_ref[...] = jnp.where(
        lane < FIELD,
        step,
        jnp.where(lane < 2 * FIELD, pltpu.roll(raw, FIELD, 1), pltpu.roll(cum, 2 * FIELD, 1)),
    )
    step_w, carried_w, keep_w, survive_w = scan_weights(step, cum, base, ends, spread_ref[...])
    cum = cum * LOG2E
    cum_row = cum.T
    stepped = step_w * x
    kept_b = keep_w * stepped
    row = lax.broadcasted_iota(jnp.int32, (SUB, SUB), 0)
    col = lax.broadcasted_iota(jnp.int32, (SUB, SUB), 1)
    state = carry[...]
    y_parts = []
    for q in range(rows // SUB):
        at = slice(q * SUB, (q + 1) * SUB)
        low = base + q * SUB
        mask = (row >= col) & (segment_of(low + row, ends) == segment_of(low + col, ends))
        b_map, c_map = maps[at, :STATE], maps[at, STATE:]
        gram = jnp.where(mask, nt3(c_map, b_map), 0.0)
        st_ref[q] = state
        outer = carried_w[at] * nn3(c_map, state)
        inner = []
        for pair in range(channels // LANES):
            mixing = []
            for h in (2 * pair, 2 * pair + 1):
                spread = cum[at, h : h + 1] - cum_row[h : h + 1, at]
                mixing.append((jnp.exp2(jnp.minimum(spread, 0.0)) * gram).astype(bf16))
            inner.append(pair_product(mixing, stepped[at, pair * LANES : (pair + 1) * LANES]))
        y_parts.append(jnp.concatenate(inner, axis=1) + outer)
        state = survive_w[q : q + 1] * state + nn3(b_map.T, kept_b[at])
    carry[...] = state
    y_scan = jnp.concatenate(y_parts, axis=0)
    y_ref[...] = y_scan
    y_total = y_scan + prm_ref[taps + 1 : taps + 2, :] * x
    total_ref[...] = y_total.astype(bf16)
    g = y_total * silu(gate_pre)
    ga_ref[...] = (g * prm_ref[taps + 2 : taps + 3, :]).astype(bf16)
    square = jnp.sum(g * g, axis=1, keepdims=True)
    square_ref[...] = jnp.broadcast_to(square, (rows, LANES)).T[:8, :]


def product_kernel(place_ref, ga_ref, w_ref, *refs, place_at):
    product = nt(ga_ref[...], w_ref[...]).astype(bf16)
    put_halves(refs, place_ref[place_at + pl.program_id(0)], product)


def cotangent_kernel(place_ref, *refs, parts, place_at):
    part_refs, refs = refs[:parts], refs[parts:]
    w_ref, ga_ref, square_ref, gg_ref, sums_ref, cot_buf = refs
    rows = gg_ref.shape[0]
    cotangent = take_rows(part_refs, place_ref[place_at + pl.program_id(0)], cot_buf)
    grad_gated = nn(cotangent, w_ref[...])
    gg_ref[...] = grad_gated.astype(bf16)
    inner = jnp.sum(grad_gated * ga_ref[...].astype(f32), axis=1, keepdims=True)
    inner_row = jnp.broadcast_to(inner, (rows, LANES)).T[:8, :]
    sublane = lax.broadcasted_iota(jnp.int32, (8, rows), 0)
    sums_ref[...] = jnp.where(sublane == 0, square_ref[...], inner_row)


def gain_row(weights, grads):
    terms = jnp.sum(weights.astype(f32) * grads, axis=1, keepdims=True)
    return jnp.broadcast_to(terms, (terms.shape[0], LANES)).T[:8, :]


def gate_kernel(place_ref, *refs, parts, taps, place_at):
    part_refs, refs = refs[:parts], refs[parts:]
    (
        sums_ref,
        prm_ref,
        w_ref,
        gate_ref,
        y_ref,
        gg_ref,
        normed_ref,
        dgate_ref,
        dy_ref,
        dprm_ref,
        out_ref,
        gain_ref,
        cot_buf,
        total,
    ) = refs
    rows, channels = gate_ref.shape
    step_id = pl.program_id(0)

    @pl.when(step_id == 0)
    def _():
        dprm_ref[...] = jnp.zeros_like(dprm_ref)
        total[...] = jnp.zeros_like(total)

    sums = jnp.concatenate([sums_ref[...], jnp.zeros((LANES - 8, rows), f32)], axis=0).T
    inverse = lax.rsqrt(sums[:, 0:1] * (1.0 / INNER) + EPS)
    inner_mean = sums[:, 1:2] * inverse * (1.0 / INNER)
    gain = prm_ref[taps + 2 : taps + 3, :]
    gate_pre = gate_ref[...].astype(f32)
    sig_gate = jax.nn.sigmoid(gate_pre)
    act = gate_pre * sig_gate
    y = y_ref[...].astype(f32)
    hat = y * act * inverse
    gated = (hat * gain).astype(bf16)
    grad_gated = gg_ref[...].astype(f32)
    dprm_ref[taps + 2 : taps + 3, :] += jnp.sum(grad_gated * hat, axis=0, keepdims=True)
    grad_inner = inverse * (grad_gated * gain - hat * inner_mean)
    dy = grad_inner * act
    dgate = (grad_inner * y * sig_gate * (1.0 + gate_pre * (1.0 - sig_gate))).astype(bf16)
    dgate_ref[...] = dgate
    dy_ref[...] = dy
    total[:, :channels] += tn(normed_ref[...], dgate)
    cotangent = take_rows(part_refs, place_ref[place_at + step_id], cot_buf)
    total[:, channels:] += tn(cotangent, gated)

    @pl.when(step_id == pl.num_programs(0) - 1)
    def _():
        out_ref[...] = total[...].astype(bf16)
        gain_ref[...] = gain_row(w_ref[...], total[:, :channels])


def backward_kernel(len_ref, first_ref, place_ref, *refs, seqs, taps, halves, place_at):
    (
        w_ref,
        gain_ref,
        terms_ref,
        dprm_gate_ref,
        prm_ref,
        prs_ref,
        prh_ref,
        upper_ref,
        spread_ref,
        gather_ref,
        normed_ref,
        dgate_ref,
        dy_ref,
        v_ref,
        u_ref,
        vs_ref,
        us_ref,
        scan_ref,
        y_ref,
        st_ref,
    ) = refs[:20]
    half_refs = refs[20 : 20 + halves]
    out_ref, small_ref, dprm_ref, dprs_ref, dprh_ref, dbuf, dsbuf, carry, ending, gb_ref, total = refs[20 + halves :]
    rows, channels = dgate_ref.shape
    step_id = pl.program_id(0)
    base = (pl.num_programs(0) - 1 - step_id) * rows
    ends = ends_of(len_ref, seqs)

    @pl.when(step_id == 0)
    def _():
        dbuf[rows : rows + 8, :] = jnp.zeros((8, channels), f32)
        dsbuf[rows : rows + 8, :] = jnp.zeros((8, 2 * STATE), f32)
        carry[...] = jnp.zeros_like(carry)
        ending[...] = jnp.zeros_like(ending)
        dprm_ref[...] = jnp.zeros_like(dprm_ref)
        dprs_ref[...] = jnp.zeros_like(dprs_ref)
        dprh_ref[...] = jnp.zeros_like(dprh_ref)
        total[...] = jnp.zeros_like(total)

    def add_row(ref, at, z):
        ref[at : at + 1, :] += jnp.sum(z, axis=0, keepdims=True)

    skip = prm_ref[taps + 1 : taps + 2, :]
    u = u_ref[...]
    sig_u = jax.nn.sigmoid(u)
    x = u * sig_u
    y_scan = y_ref[...]
    dy = dy_ref[...]
    dy_b = dy.astype(bf16)

    add_row(dprm_ref, taps + 1, dy * x)
    us = us_ref[...]
    sig_us = jax.nn.sigmoid(us)
    maps = us * sig_us
    maps_b = maps.astype(bf16)
    terms = scan_ref[...]
    lane = lax.broadcasted_iota(jnp.int32, (rows, LANES), 1)
    inside = lane < FIELD
    step = jnp.where(inside, terms, 0.0)
    raw = jnp.where(inside, pltpu.roll(terms, LANES - FIELD, 1), 0.0)
    cum = jnp.where(inside, pltpu.roll(terms, LANES - 2 * FIELD, 1), 0.0)
    decay = prh_ref[1:2, :]
    step_w, carried_w, keep_w, survive_w = scan_weights(step, cum, base, ends, spread_ref[...])
    cum = cum * LOG2E
    cum_row = cum.T
    stepped = step_w * x
    stepped_b = stepped.astype(bf16)
    kept_b = (keep_w * stepped).astype(bf16)
    dy_carried = carried_w * dy
    dy_carried_b = dy_carried.astype(bf16)
    row = lax.broadcasted_iota(jnp.int32, (SUB, SUB), 0)
    col = lax.broadcasted_iota(jnp.int32, (SUB, SUB), 1)
    dstate = carry[...]
    state_end = ending[0:1, :]
    subs = rows // SUB
    dsteppeds, dmaps, state_ends = [None] * subs, [None] * subs, [None] * subs
    for q in reversed(range(subs)):
        at = slice(q * SUB, (q + 1) * SUB)
        low = base + q * SUB
        mask = (row <= col) & (segment_of(low + row, ends) == segment_of(low + col, ends))
        b_map, c_map = maps[at, :STATE], maps[at, STATE:]
        gram = jnp.where(mask, nt3(b_map, c_map), 0.0)
        state = st_ref[q]
        dstate_b = dstate.astype(bf16)
        dgram = jnp.zeros((SUB, SUB), f32)
        inner = []
        for pair in range(channels // LANES):
            lanes = slice(pair * LANES, (pair + 1) * LANES)
            dmix = nt(pair_stack(stepped_b[at, lanes]), dy_b[at, lanes])
            mixing = []
            for i, h in enumerate((2 * pair, 2 * pair + 1)):
                spread = cum_row[h : h + 1, at] - cum[at, h : h + 1]
                weight = jnp.exp2(jnp.minimum(spread, 0.0))
                mixing.append((weight * gram).astype(bf16))
                dgram = dgram + dmix[i * SUB : (i + 1) * SUB] * weight
            inner.append(pair_product(mixing, dy[at, lanes]))
        dsteppeds[q] = jnp.concatenate(inner, axis=1) + keep_w[at] * nn3(b_map, dstate)
        dgram = jnp.where(mask, dgram, 0.0).astype(bf16)
        db = nn(dgram, maps_b[at, STATE:]) + nt(kept_b[at], dstate_b)
        dc = tn(dgram, maps_b[at, :STATE]) + nt(dy_carried_b[at], state.astype(bf16))
        dmaps[q] = jnp.concatenate([db, dc], axis=1)
        state_ends[q] = state_end
        dstate = survive_w[q : q + 1] * dstate + nn3(c_map.T, dy_carried[at])
        state_end = jnp.sum(state * dstate, axis=0, keepdims=True)
    carry[...] = dstate
    ending[0:1, :] = state_end
    dstepped = jnp.concatenate(dsteppeds, axis=0)
    dmap = jnp.concatenate(dmaps, axis=0)
    state_ends.append(jnp.zeros((-subs % 8, channels), f32))
    by_head = gather_heads(
        jnp.concatenate([dy * y_scan - stepped * dstepped, x * dstepped] + state_ends, axis=0),
        gather_ref[...],
    )
    dlog = triangle_sum(upper_ref[...], by_head[:rows])
    dlog = jnp.concatenate(
        [
            dlog[q * SUB : (q + 1) * SUB] + by_head[2 * rows + q : 2 * rows + q + 1]
            for q in range(subs)
        ],
        axis=0,
    )
    draw = (by_head[rows : 2 * rows] - decay * dlog) * jax.nn.sigmoid(raw)
    add_row(dprh_ref, 0, draw)
    add_row(dprh_ref, 1, dlog * step * -decay)
    du = (step_w * dstepped + skip * dy) * sig_u * (1.0 + u * (1.0 - sig_u))
    dus = dmap * sig_us * (1.0 + us * (1.0 - sig_us))
    dbuf[0:rows, :] = du
    dsbuf[0:rows, :] = dus
    v = v_ref[...].astype(f32)
    vs = vs_ref[...].astype(f32)
    places = base + lax.broadcasted_iota(jnp.int32, (rows, 1), 0)
    segment = segment_of(places, ends)
    dv = prm_ref[taps - 1 : taps, :] * du
    dvs = prs_ref[taps - 1 : taps, :] * dus
    add_row(dprm_ref, taps - 1, du * v)
    add_row(dprs_ref, taps - 1, dus * vs)
    add_row(dprm_ref, taps, du)
    add_row(dprs_ref, taps, dus)
    for lag in range(1, taps):
        usable = segment_of(places + lag, ends) == segment
        tap = taps - 1 - lag
        later = jnp.where(usable, dbuf[lag : lag + rows, :], 0.0)
        later_s = jnp.where(usable, dsbuf[lag : lag + rows, :], 0.0)
        dv = dv + prm_ref[tap : tap + 1, :] * later
        dvs = dvs + prs_ref[tap : tap + 1, :] * later_s
        add_row(dprm_ref, tap, later * v)
        add_row(dprs_ref, tap, later_s * vs)
    dbuf[rows : rows + 8, :] = dbuf[0:8, :]
    dsbuf[rows : rows + 8, :] = dsbuf[0:8, :]
    gb_ref[:, :channels] = dv.astype(bf16)
    gb_ref[:, channels : channels + 2 * STATE] = dvs.astype(bf16)
    gb_ref[:, channels + 2 * STATE :] = pltpu.roll(draw, first_ref[0], 1).astype(bf16)
    product = nt(dgate_ref[...], w_ref[:, :channels]) + nt(gb_ref[...], w_ref[:, channels:])
    put_halves(half_refs, place_ref[place_at + step_id], product.astype(bf16))
    total[...] += tn(normed_ref[...], gb_ref[...])

    @pl.when(step_id == pl.num_programs(0) - 1)
    def _():
        grads = total[...]
        out_ref[...] = grads.astype(bf16)
        gains = (gain_row(w_ref[:, channels:], grads) + terms_ref[...]) / gain_ref[...]
        line = lax.broadcasted_iota(jnp.int32, (8, 1), 0)
        both = jnp.where(line == taps + 2, dprm_gate_ref[...], dprm_ref[...])
        skips = gather_heads(dprm_ref[...], gather_ref[...])
        by_head = jnp.where(line == 2, pltpu.roll(skips, 8 - (taps - 1), 0), dprh_ref[...])
        small_ref[...] = jnp.zeros_like(small_ref)
        small_ref[0:8, :channels] = both
        small_ref[0:8, channels : channels + 2 * STATE] = dprs_ref[...]
        small_ref[0:8, channels + 2 * STATE : channels + 2 * STATE + LANES] = pltpu.roll(
            by_head, first_ref[0], 1
        )
        small_ref[8:16, :] = gains


def held(places):
    last = next(p for p in places if p is not None)
    filled = []
    for p in places:
        last = last if p is None else p
        filled.append(last)
    return filled


def place_table(tensor_place, quarter_blocks, order):
    relative = [(b // quarter_blocks) ^ tensor_place for b in order]
    inside = [b % quarter_blocks for b in order]

    def places(slots):
        return held(
            [slots.index(r) * quarter_blocks + w if r in slots else None for r, w in zip(relative, inside)]
        )

    return [
        relative,
        places([0]),
        places([1]),
        places([2]),
        places([3]),
        places([1, 3]),
        places([0, 2]),
        places([2, 3]),
        places([0, 1]),
    ]


def over_x(z):
    return lax.ppermute(z, "tensor", [(0, 1), (1, 0), (2, 3), (3, 2)])


def over_y(z):
    return lax.ppermute(z, "tensor", [(0, 2), (2, 0), (1, 3), (3, 1)])


def gather_start(z):
    return over_x(z), over_y(z)


def gather_end(z, from_x, from_y, after=()):
    half = z.shape[1] // 2
    far = (from_x[:, :half], from_y[:, half:])
    far, after = lax.optimization_barrier((far, after))
    return [z, from_x, from_y, over_y(far[0]), over_x(far[1])], after


def scatter_start(halves):
    return over_x(halves[0]), over_y(halves[2])


def scatter_middle(halves, from_x, from_y, after=()):
    rows = from_x.shape[0] // 2
    left, right = halves[1], halves[3]
    left_far = left[rows:].astype(f32) + from_x[rows:].astype(f32)
    right_far = right[rows:].astype(f32) + from_y[rows:].astype(f32)
    far = (left_far.astype(bf16), right_far.astype(bf16))
    far, after = lax.optimization_barrier((far, after))
    return (over_y(far[0]), over_x(far[1])), after


def scatter_end(halves, from_x, from_y, far_left, far_right):
    rows = from_x.shape[0] // 2
    left, right = halves[1][:rows].astype(f32), halves[3][:rows].astype(f32)
    left = left + from_x[:rows].astype(f32) + far_left.astype(f32)
    right = right + from_y[:rows].astype(f32) + far_right.astype(f32)
    return jnp.concatenate([left, right], axis=1)


def sum_over_tensor(z):
    z = (z.astype(f32) + over_x(z).astype(f32)).astype(z.dtype)
    return z.astype(f32) + over_y(z).astype(f32)


def sum_over_dp(z):
    count = lax.axis_size("dp")
    bit = 1
    while bit < count:
        z = z + lax.ppermute(z, "dp", [(i, i ^ bit) for i in range(count)])
        bit *= 2
    return z


class Kernels:
    def __init__(self, lengths, first, tensor_place, tensor_count, group_rows, width, channels, taps, head_count):
        self.lengths, self.first = lengths, first
        self.tensor_place, self.tensor_count = tensor_place, tensor_count
        self.square = tensor_count == 4
        self.group_rows, self.width, self.channels = group_rows, width, channels
        self.taps, self.head_count = taps, head_count
        self.seqs = lengths.shape[1]
        self.lower, self.upper, self.spread, self.gather = constants(channels)
        self.tables()

    def tables(self):
        kinds = ((ROWS, False), (ROWS, True), (WIDE_ROWS, False))
        self.kinds = {kind: k for k, kind in enumerate(kinds)}
        places = range(4) if self.square else range(1)
        made = []
        for t in places:
            lines = []
            for block, backwards in kinds:
                order = list(range(self.group_rows // block))[:: -1 if backwards else 1]
                table = place_table(t, len(order) // 4, order) if self.square else [order]
                lines += [line + [0] * (self.group_rows // ROWS - len(order)) for line in table]
            made.append(lines)
        self.lines = len(made[0]) // len(kinds)
        made = jnp.asarray(np.array(made, np.int32).reshape(len(made), -1))
        place = self.tensor_place if self.square else 0
        self.place = lax.dynamic_index_in_dim(made, place, 0, keepdims=False)
        self.steps = self.group_rows // ROWS

    def at(self, block, backwards, line):
        return (self.kinds[(block, backwards)] * self.lines + line) * self.steps

    def call(self, kernel, scalars, steps, ins, outs, scratch, aliases=None):
        specs, arrays = zip(*ins)
        out_specs, out_shapes = zip(*outs)
        return pl.pallas_call(
            kernel,
            grid_spec=pltpu.PrefetchScalarGridSpec(
                num_scalar_prefetch=len(scalars),
                grid=(steps,),
                in_specs=list(specs),
                out_specs=list(out_specs),
                scratch_shapes=scratch,
            ),
            out_shape=list(out_shapes),
            input_output_aliases=aliases or {},
            compiler_params=pltpu.CompilerParams(vmem_limit_bytes=56 * 2**20),
            cost_estimate=pl.CostEstimate(flops=1000, bytes_accessed=1000, transcendentals=0),
            name=getattr(kernel, "func", kernel).__name__,
        )(*scalars, *arrays)

    def whole(self, array):
        return pl.BlockSpec(array.shape, lambda i, *s: (0,) * len(array.shape)), array

    def columns(self, array, width, place):
        return pl.BlockSpec((array.shape[0], width), lambda i, *s: (0, place)), array

    def rows(self, array, block, backwards=False, low=0):
        last = self.group_rows // block - 1

        def at(i, *s):
            return (last - i if backwards else i + low,) + (0,) * (len(array.shape) - 1)

        size = array.shape[0] * block // self.group_rows
        return pl.BlockSpec((size,) + array.shape[1:], at), array

    def across(self, array, block, low=0):
        return pl.BlockSpec((8, block), lambda i, *s: (0, i + low)), array

    def out(self, columns, dtype):
        return jax.ShapeDtypeStruct((self.group_rows, columns), dtype)

    def parts(self, arrays, block, low=0):
        if not self.square:
            return [self.rows(arrays[0], block, low=low)]
        return [
            (
                pl.BlockSpec(
                    (block, z.shape[1]), lambda i, *s, at=self.at(block, False, k): (s[-1][at + i + low], 0)
                ),
                z,
            )
            for k, z in zip((1, 2, 3, 4, 4), arrays)
        ]

    def halves(self, block, backwards=False):
        half = self.width // 2
        lines = (5, 6, 7, 8) if self.square else (0, 0)
        rows = self.group_rows // 2 if self.square else self.group_rows
        shape = jax.ShapeDtypeStruct((rows, half), bf16)
        return [
            (
                pl.BlockSpec((block, half), lambda i, *s, at=self.at(block, backwards, k): (s[-1][at + i], 0)),
                shape,
            )
            for k in lines
        ]

    def scan(self, low, high, hidden, weights, gain, prm, prs, prh, carried, before=()):
        channels, count = self.channels, self.group_rows
        parts = self.parts(hidden, ROWS, low)
        shapes = [
            self.out(self.width, bf16),
            self.out(channels, bf16),
            self.out(channels, f32),
            self.out(2 * STATE, bf16),
            self.out(2 * STATE, f32),
            self.out(LANES, f32),
            self.out(channels, f32),
            jax.ShapeDtypeStruct((count // SUB, STATE, channels), f32),
            self.out(channels, bf16),
            self.out(channels, bf16),
            self.out(channels, bf16),
        ]
        outs = [self.rows(z, ROWS, low=low) for z in shapes]
        outs.append(self.across(jax.ShapeDtypeStruct((8, count), f32), ROWS, low))
        kept = len(outs)
        ins = parts + [self.whole(z) for z in [weights, gain, prm, prs, prh, self.lower, self.spread] + list(carried)]
        aliases = {3 + len(ins) + k: k for k in range(len(before))}
        ins += [(pl.BlockSpec(memory_space=pl.ANY), z) for z in before]
        sizes = ((8, channels), (8, 2 * STATE), (STATE, channels))
        outs += [self.whole(jax.ShapeDtypeStruct(size, f32)) for size in sizes]
        result = self.call(
            functools.partial(
                scan_kernel,
                parts=len(parts),
                seqs=self.seqs,
                taps=self.taps,
                head_count=self.head_count,
                first_block=low,
                kept=len(before),
                starts=len(carried),
                place_at=self.at(ROWS, False, 0),
            ),
            (self.lengths, self.first, self.place),
            high - low,
            ins,
            outs,
            [
                pltpu.VMEM((ROWS, self.width), bf16),
                pltpu.VMEM((ROWS + 8, channels), f32),
                pltpu.VMEM((ROWS + 8, 2 * STATE), f32),
            ],
            aliases,
        )
        return result[:kept], result[kept:]

    def product(self, ga, weights):
        return self.call(
            functools.partial(product_kernel, place_at=self.at(WIDE_ROWS, False, 0)),
            (self.place,),
            self.group_rows // WIDE_ROWS,
            [self.rows(ga, WIDE_ROWS), self.whole(weights)],
            self.halves(WIDE_ROWS),
            [],
        )

    def cotangent(self, cotangent, weights, ga, square):
        parts = self.parts(cotangent, WIDE_ROWS)
        return self.call(
            functools.partial(cotangent_kernel, parts=len(parts), place_at=self.at(WIDE_ROWS, False, 0)),
            (self.place,),
            self.group_rows // WIDE_ROWS,
            parts + [self.whole(weights), self.rows(ga, WIDE_ROWS), self.across(square, WIDE_ROWS)],
            [
                self.rows(self.out(self.channels, bf16), WIDE_ROWS),
                self.across(jax.ShapeDtypeStruct((8, self.group_rows), f32), WIDE_ROWS),
            ],
            [pltpu.VMEM((WIDE_ROWS, self.width), bf16)],
        )

    def gate(self, cotangent, sums, prm, weights, gate, y, gg, normed):
        channels = self.channels
        parts = self.parts(cotangent, WIDE_ROWS)
        return self.call(
            functools.partial(
                gate_kernel, parts=len(parts), taps=self.taps, place_at=self.at(WIDE_ROWS, False, 0)
            ),
            (self.place,),
            self.group_rows // WIDE_ROWS,
            parts
            + [self.across(sums, WIDE_ROWS), self.whole(prm), self.columns(weights, channels, 0)]
            + [self.rows(z, WIDE_ROWS) for z in (gate, y, gg, normed)],
            [
                self.rows(self.out(channels, bf16), WIDE_ROWS),
                self.rows(self.out(channels, f32), WIDE_ROWS),
                self.whole(jax.ShapeDtypeStruct(prm.shape, f32)),
                self.whole(jax.ShapeDtypeStruct((self.width, 2 * channels), bf16)),
                self.whole(jax.ShapeDtypeStruct((8, self.width), f32)),
            ],
            [pltpu.VMEM((WIDE_ROWS, self.width), bf16), pltpu.VMEM((self.width, 2 * channels), f32)],
        )

    def backward(self, weights, gain, terms, dprm_gate, prm, prs, prh, saved):
        channels = self.channels
        gradients = channels + 3 * STATE
        halves = self.halves(ROWS, True)
        shapes = [
            jax.ShapeDtypeStruct((self.width, gradients), bf16),
            jax.ShapeDtypeStruct((16, self.width), f32),
        ]
        shapes += [jax.ShapeDtypeStruct(z.shape, f32) for z in (prm, prs, prh)]
        result = self.call(
            functools.partial(
                backward_kernel,
                seqs=self.seqs,
                taps=self.taps,
                halves=len(halves),
                place_at=self.at(ROWS, True, 0),
            ),
            (self.lengths, self.first, self.place),
            self.group_rows // ROWS,
            [
                self.whole(z)
                for z in (weights, gain, terms, dprm_gate, prm, prs, prh, self.upper, self.spread, self.gather)
            ]
            + [self.rows(z, ROWS, True) for z in saved],
            halves + [self.whole(z) for z in shapes],
            [
                pltpu.VMEM((ROWS + 8, channels), f32),
                pltpu.VMEM((ROWS + 8, 2 * STATE), f32),
                pltpu.VMEM((STATE, channels), f32),
                pltpu.VMEM((8, channels), f32),
                pltpu.VMEM((ROWS, gradients), bf16),
                pltpu.VMEM((self.width, gradients), f32),
            ],
        )
        return result[: len(halves)], result[len(halves)], result[len(halves) + 1]


def per_device(
    hidden_in,
    norm_gain,
    proj_gate,
    proj_conv,
    proj_state,
    conv_kernel,
    conv_offset,
    state_kernel,
    state_offset,
    step_bias,
    decay_log,
    skip_gain,
    gate_gain,
    proj_out,
    out_cotangent,
    seq_lengths,
):
    tensor_count = lax.axis_size("tensor")
    tensor_place = lax.axis_index("tensor")
    dp_count = lax.axis_size("dp")
    dp_place = lax.axis_index("dp")
    square_mesh = tensor_count == 4
    own_rows, width = hidden_in.shape
    depth, channels = proj_gate.shape
    taps, heads_here, cut = conv_kernel.shape
    head_cut = step_bias.shape[0]
    state_cut = state_kernel.shape[1]
    state_width = proj_state.shape[1]
    group_rows = own_rows * tensor_count
    first_head = (tensor_place * heads_here).astype(jnp.int32)

    state_part = jnp.pad(proj_state, ((0, 0), (0, 3 * STATE - state_width)))
    weights = lax.all_gather(
        jnp.concatenate([proj_gate, proj_conv, state_part], axis=1), "dp", axis=0, tiled=True
    )
    out_weights = lax.all_gather(proj_out.T, "dp", axis=0, tiled=True)
    if square_mesh:
        from_x, from_y = gather_start(hidden_in)

    small = [
        norm_gain,
        conv_kernel,
        conv_offset,
        state_kernel,
        state_offset,
        step_bias,
        decay_log,
        skip_gain,
        gate_gain,
    ]
    flat = jnp.concatenate([z.reshape(-1) for z in small])
    flat = jnp.pad(flat, (0, -flat.shape[0] % 1024)).reshape(-1, LANES)
    small_all = lax.all_gather(flat, "dp", axis=0)
    if square_mesh:
        from_x, from_y, small_all = lax.optimization_barrier((from_x, from_y, small_all))
        hidden_all, _ = gather_end(hidden_in, from_x, from_y)
        hidden_all, cot = lax.optimization_barrier((hidden_all, out_cotangent))
    else:
        hidden_all = [lax.all_gather(hidden_in, "tensor", axis=0, tiled=True)]
    small_all = small_all.reshape(dp_count, -1).astype(f32)
    shares, at = [], 0
    for z in small:
        shares.append(small_all[:, at : at + z.size].reshape((dp_count,) + z.shape))
        at += z.size
    gain_in = shares[0].reshape(1, width)
    taps_conv = shares[1].transpose(1, 2, 0, 3).reshape(taps, channels)
    off_conv = shares[2].transpose(1, 0, 2).reshape(1, channels)
    taps_state = shares[3].transpose(1, 0, 2).reshape(taps, 2 * STATE)
    off_state = shares[4].reshape(1, 2 * STATE)
    gain_gate = shares[8].transpose(1, 0, 2).reshape(1, channels)

    def own_heads(z):
        return lax.dynamic_slice_in_dim(z.reshape(-1), first_head, heads_here, 0)

    skip = jnp.repeat(own_heads(shares[7]), HEADDIM).reshape(1, channels)
    prm = jnp.concatenate([taps_conv, off_conv, skip, gain_gate], axis=0)
    prm = jnp.pad(prm, ((0, -prm.shape[0] % 8), (0, 0)))
    prs = jnp.concatenate([taps_state, off_state], axis=0)
    prs = jnp.pad(prs, ((0, -prs.shape[0] % 8), (0, 0)))
    prh = jnp.stack([own_heads(shares[5]), jnp.exp(own_heads(shares[6]))])
    prh = jnp.pad(prh, ((0, 6), (0, LANES - heads_here)))

    kernels = Kernels(
        seq_lengths,
        first_head.reshape(1),
        tensor_place,
        tensor_count,
        group_rows,
        width,
        channels,
        taps,
        heads_here,
    )

    blocks = group_rows // ROWS
    common = (hidden_all, weights, gain_in, prm, prs, prh)
    if square_mesh:
        moving = gather_start(cot)
        middle = blocks * 3 // 4
        saved, carried = kernels.scan(0, middle, *common, ())
        carried, moving = lax.optimization_barrier((carried, moving))
        cotangent_all, carried = gather_end(cot, *moving, carried)
        saved, _ = kernels.scan(middle, blocks, *common, carried, saved)
    else:
        cotangent_all = [lax.all_gather(out_cotangent, "tensor", axis=0, tiled=True)]
        saved, _ = kernels.scan(0, blocks, *common, ())
    normed, v, u, vs, us, scan_terms, y_scan, states, gate_pre, ga, y_total, square = saved
    gg, sums = kernels.cotangent(cotangent_all, out_weights, ga, square)
    gg, ga = lax.optimization_barrier((gg, ga))
    out_halves = kernels.product(ga, out_weights)
    if square_mesh:
        sums = sums + over_x(sums)
        sums, out_halves = lax.optimization_barrier((sums, out_halves))
        sums = sums + over_y(sums)
        sums, out_halves = lax.optimization_barrier((sums, out_halves))
        moving = scatter_start(out_halves)
    else:
        sums = lax.psum(sums, "tensor")

    dgate, dy, dprm_gate, grad_first, terms = kernels.gate(
        cotangent_all, sums, prm, weights, gate_pre, y_total, gg, normed
    )
    if square_mesh:
        dy, grad_first, moving = lax.optimization_barrier((dy, grad_first, moving))
        far, dy = scatter_middle(out_halves, *moving, dy)
        out_moving = moving + far
    own_first = lax.psum_scatter(grad_first, "dp", scatter_dimension=0, tiled=True)
    gn_halves, grad_last, small_sum = kernels.backward(
        weights,
        gain_in,
        terms,
        dprm_gate,
        prm,
        prs,
        prh,
        [normed, dgate, dy, v, u, vs, us, scan_terms, y_scan, states],
    )

    def own_sum(halves):
        return lax.psum_scatter(
            jnp.concatenate(halves, axis=1), "tensor", scatter_dimension=0, tiled=True
        ).astype(f32)

    if square_mesh:
        gn_halves, grad_last, small_sum, own_first, out_moving = lax.optimization_barrier(
            (gn_halves, grad_last, small_sum, own_first, out_moving)
        )
        moving = scatter_start(gn_halves)
    own_last = lax.psum_scatter(grad_last, "dp", scatter_dimension=0, tiled=True)
    small_sum = sum_over_dp(small_sum)
    if square_mesh:
        small_sum, moving = lax.optimization_barrier((small_sum, moving))
        far, small_sum = scatter_middle(gn_halves, *moving, small_sum)
    small_shared = sum_over_tensor(small_sum) if square_mesh else lax.psum(small_sum, "tensor")

    if square_mesh:
        own_state = own_last[:, channels:].astype(f32)
        own_state = (own_state + over_x(own_last[:, channels:]).astype(f32)).astype(bf16)
        far, own_state, small_shared = lax.optimization_barrier((far, own_state, small_shared))
        own_state = own_state.astype(f32) + over_y(own_state).astype(f32)
        grad_normed = scatter_end(gn_halves, *moving, *far)
        branch = scatter_end(out_halves, *out_moving)
    else:
        grad_normed = own_sum(gn_halves)
        own_state = lax.psum(own_last[:, channels:].astype(f32), "tensor")
        branch = own_sum(out_halves)

    own_square = lax.dynamic_slice_in_dim(sums[0], tensor_place * own_rows, own_rows, 0)
    inverse_gate = lax.rsqrt(own_square * (1.0 / INNER) + EPS)[:, None]
    values = hidden_in.astype(f32)
    block_out = (values + branch * inverse_gate).astype(bf16)

    inverse_in = lax.rsqrt(jnp.mean(values * values, axis=1, keepdims=True) + EPS)
    scaled = values * inverse_in
    grad_scaled = grad_normed * gain_in
    grad_hidden = out_cotangent.astype(f32) + inverse_in * (
        grad_scaled - scaled * jnp.mean(grad_scaled * scaled, axis=1, keepdims=True)
    )

    own_part = depth // tensor_count
    own_state = lax.dynamic_slice_in_dim(own_state, tensor_place * own_part, own_part, 0)[:, :state_width]

    def own_cut(z, size, axis):
        return lax.dynamic_slice_in_dim(z, dp_place * size, size, axis)

    by_channel = small_sum[: taps + 3, :channels].reshape(taps + 3, heads_here, HEADDIM)
    by_channel = own_cut(by_channel, cut, 2)
    by_map = own_cut(small_shared[: taps + 1, channels : channels + 2 * STATE], state_cut, 1)
    heads_at = channels + 2 * STATE
    by_head = own_cut(small_shared[:3, heads_at : heads_at + LANES], head_cut, 1)
    gain_grad = lax.dynamic_slice_in_dim(
        small_shared[8], (dp_place * tensor_count + tensor_place) * own_part, own_part, 0
    )
    own_first = own_first.astype(f32)
    return (
        block_out,
        grad_hidden,
        gain_grad,
        own_first[:, :channels],
        own_last[:, :channels].astype(f32),
        own_state,
        own_first[:, channels:].T,
        by_channel[:taps],
        by_channel[taps],
        by_map[:taps],
        by_map[taps],
        by_head[0],
        by_head[1],
        by_head[2],
        by_channel[taps + 2],
    )


def solution(mesh):
    placed = (
        P(("dp", "tensor"), None),
        P("dp"),
        P("dp", "tensor"),
        P("dp", "tensor"),
        P("dp", None),
        P(None, "tensor", "dp"),
        P("tensor", "dp"),
        P(None, "dp"),
        P("dp"),
        P("dp"),
        P("dp"),
        P("dp"),
        P("tensor", "dp"),
        P("tensor", "dp"),
        P(("dp", "tensor"), None),
        P("dp", None),
    )
    return jax.shard_map(
        per_device,
        mesh=mesh,
        in_specs=placed,
        out_specs=(
            P(("dp", "tensor"), None),
            P(("dp", "tensor"), None),
            P(("dp", "tensor")),
            P("dp", "tensor"),
            P("dp", "tensor"),
            P(("dp", "tensor"), None),
            P("tensor", "dp"),
            P(None, "tensor", "dp"),
            P("tensor", "dp"),
            P(None, "dp"),
            P("dp"),
            P("dp"),
            P("dp"),
            P("dp"),
            P("tensor", "dp"),
        ),
        check_vma=False,
    )
```

time: 302 us -> 260 us (0.86)
  waiting for transfers between devices: 76.6 us -> 36.1 us
  Pallas kernels: 127 us -> 119 us
  starting transfers between devices: 26.2 us -> 30.3 us
    ppermute x11, waiting for transfers between devices: 55.8 us -> 6.42 us  [over_x(): return lax.ppermute(z, 'tensor', [(0, 1), (1, 0), (2, 3), (3, 2)])]
    ppermute x11, waiting for transfers between devices: 11.5 us -> 23.6 us  [over_y(): return lax.ppermute(z, 'tensor', [(0, 2), (2, 0), (1, 3), (3, 1)])]
    pallas_call x7 -> x6, Pallas kernels: 127 us -> 119 us  [call(): pl.pallas_call(kernel, grid_spec=pltpu.PrefetchScalarGridSpec(num_scalar_...]
    squeeze x6 -> x0, local copies, waits for them, and re-layouts: 4.11 us -> none  [table(): lax.dynamic_index_in_dim(jnp.asarray(tables), self.tensor_place, 0, keepd...]
    concatenate x1, local copies, waits for them, and re-layouts: 0.09 us -> 3.42 us  [per_device(): flat = jnp.concatenate([z.reshape(-1) for z in small])]
    ppermute x3, waiting for transfers between devices: 9.15 us -> 5.99 us  [sum_over_dp(): z = z + lax.ppermute(z, 'dp', [(i, i ^ bit) for i in range(count)])]
    unnamed x68 -> x40, local copies, waits for them, and re-layouts: 7.3 us -> 4.9 us
  transfers between devices with their start and end apart: 29 -> 29, of which waited for: 12 -> 13; matrix products, arithmetic and copies ran while one was open for 11% -> 15% of each run, Pallas kernels for 42% -> 43%
where the time goes in v2:
time: 260 us; the launch traced here: 259 us
  Pallas kernels  119 us (46%)
  waiting for transfers between devices  36.1 us (14%)
  starting transfers between devices  30.3 us (12%)
  local copies, waits for them, and re-layouts  24.3 us (9%)
  other arithmetic  21.8 us (8%)
  between operations  15 us (6%)
  blocking collectives  13.2 us (5%)
    pallas_call x6, Pallas kernels, call(): pl.pallas_call(kernel, grid_spec=pltpu.PrefetchScalarGridSpec(num_scalar_...  119 us
    ppermute x11, waiting for transfers between devices, over_y(): return lax.ppermute(z, 'tensor', [(0, 2), (2, 0), (1, 3), (3, 1)])  23.6 us
    ppermute x11, starting transfers between devices, over_x(): return lax.ppermute(z, 'tensor', [(0, 1), (1, 0), (2, 3), (3, 2)])  14.1 us
    all_gather x1, blocking collectives, per_device(): small_all = lax.all_gather(flat, 'dp', axis=0)  13.2 us
    ppermute x11, starting transfers between devices, over_y(): return lax.ppermute(z, 'tensor', [(0, 2), (2, 0), (1, 3), (3, 1)])  10.7 us
    ppermute x11, waiting for transfers between devices, over_x(): return lax.ppermute(z, 'tensor', [(0, 1), (1, 0), (2, 3), (3, 2)])  6.42 us
    ppermute x3, waiting for transfers between devices, sum_over_dp(): z = z + lax.ppermute(z, 'dp', [(i, i ^ bit) for i in range(count)])  5.99 us
    convert_element_type x4, other arithmetic, scatter_middle(): far = (left_far.astype(bf16), right_far.astype(bf16))  5.42 us
  transfers between devices with their start and end apart: 29, of which 13 were waited for; matrix products, arithmetic and copies ran while one was open for 15% of the time, Pallas kernels for 43%

profile of v2, /device:TPU:0, one launch (start us, length us, event | category | flops | bytes accessed | tf_op | source)
XLA Modules:
  0.0 259.3 jit_solution(16554720241470168708)
XLA Ops:
  7.2 1.1 copy.62
  8.3 1.7 fusion.9
  10.2 3.0 %collective-permute-start = (bf16[512,1024]{1,0:T(8,128)(2,1)}, bf16[512,1024]{1,0:T(8,128)(2,1)S(1)}, u32[]{:S(2)}, u32[]{:S(2)}) collective-permute-start(bf16[512,1024]{1,0:T(8,128)(2,1)} %refs_0_.1), channel_id=1, source_target_pairs={{0,1},{1,0},{2,3},{3,2},{4,5},{5,4},{6,7},{7,6},{8,9},{9,8},{10,11... | collective-permute-start | bytes 3145736 | tf_op jit(solution)/shard_map/ppermute | solution.py:596
  13.2 1.5 collective-permute-start.1
  14.7 0.8 reshape.117
  15.5 0.8 reshape.118
  16.2 0.8 reshape.119
  17.0 0.8 reshape.120
  17.8 3.4 %concatenate.18 = bf16[684]{0:T(1024)(128)(2,1)S(1)} concatenate(bf16[128]{0:T(256)(128)(2,1)} %param.22, bf16[256]{0:T(256)(128)(2,1)S(1)} %reshape.117, bf16[64]{0:T(256)(128)(2,1)S(1)} %reshape.118, bf16[128]{0:T(256)(128)(2,1)S(1)} %reshape.119, bf16[32]{0:T(256)(128)(2,1)} %param.29, bf16[4]{0:T(256)(128)(2,1)} %param.30, bf16[4]{0:T(256)(128)(2,1)} %param.31, ...), dimensions={0} | concatenate | bytes 2736 | tf_op jit(solution)/shard_map/concatenate | solution.py:931
  21.2 13.2 %all_gather.9 = bf16[8,8,128]{2,1,0:T(8,128)(2,1)S(1)} all-gather(bf16[1,8,128]{2,1,0:T(8,128)(2,1)S(1)} %pad_bitcast_fusion), channel_id=1, replica_groups=mesh['dp'=8,'tensor'=4] {'dp'}, dimensions={0}, use_global_device_ids=true | all-gather | bytes 18432 | tf_op jit(solution)/shard_map/all_gather | solution.py:933
  34.4 2.2 collective-permute-done.refs_1_
  36.5 1.5 collective-permute-done.1.refs_2_
  38.0 0.9 slice.142
  38.9 0.9 slice.143
  39.7 1.5 collective-permute-start.2
  41.9 0.8 copy.67
  43.4 1.3 constant_dynamic-slice_fusion.5
  44.8 7.8 %collective-permute-done.2.refs_3_ = bf16[512,512]{1,0:T(8,128)(2,1)} collective-permute-done((bf16[512,512]{1,0:T(8,128)(2,1)}, bf16[512,512]{1,0:T(8,128)(2,1)}, u32[]{:S(2)}, u32[]{:S(2)}) %collective-permute-start.2) | collective-permute-done | bytes 524320 | tf_op jit(solution)/shard_map/ppermute | solution.py:600
  52.6 1.3 collective-permute-done.3.refs_4_
  54.5 0.7 collective-permute-start.5
  59.3 22.7 %scan_kernel.2 = (bf16[2048,1024]{1,0:T(8,128)(2,1)}, bf16[2048,512]{1,0:T(8,128)(2,1)}, f32[2048,512]{1,0:T(8,128)}, bf16[2048,256]{1,0:T(8,128)(2,1)}, f32[204...) custom-call(s32[1,1]{1,0:T(1,128)S(6)} %copy.92.len_ref, ...), custom_call_target="tpu_custom_call" | custom-call | flops 1000 | bytes 1000 | tf_op jit(solution)/shard_map/scan_kernel/pallas_call | solution.py:685
  82.0 1.1 slice.153
  83.1 1.1 slice.154
  84.2 1.4 collective-permute-start.6
  85.5 1.5 collective-permute-start.7
  87.0 11.1 %scan_kernel.3 = (bf16[2048,1024]{1,0:T(8,128)(2,1)}, bf16[2048,512]{1,0:T(8,128)(2,1)}, f32[2048,512]{1,0:T(8,128)}, bf16[2048,256]{1,0:T(8,128)(2,1)}, f32[204...) custom-call(s32[1,1]{1,0:T(1,128)S(6)} %copy.92.len_ref, ...), custom_call_target="tpu_custom_call", output_to_operand_aliasing={{0}: (18, {}), {1}: (19, {}), {2}: (20, {}), {3}: (21, {}),... | custom-call | flops 1000 | bytes 1000 | tf_op jit(solution)/shard_map/scan_kernel/pallas_call | solution.py:685
  98.2 0.8 copy-done.5
  99.2 8.3 %cotangent_kernel.1 = (bf16[2048,512]{1,0:T(8,128)(2,1)}, f32[8,2048]{1,0:T(8,128)}) custom-call(s32[216]{0:T(256)} %bitcast.63, bf16[512,1024]{1,0:T(8,128)(2,1)} %refs_0_.3, bf16[512,1024]{1,0:T(8,128)(2,1)} %collective-permute-done.4.refs_1_, bf16[512,1024]{1,0:T(8,128)(2,1)} %collective-permute-done.5.refs_2_, bf16[512,512]{1,0:T(8,128)(2,1)} %copy-done.5, ...), custom_call_target="tpu_custom_call" | custom-call | flops 1000 | bytes 1000 | tf_op jit(solution)/shard_map/cotangent_kernel/pallas_call | solution.py:685
  108.0 7.4 %product_kernel.1 = (bf16[1024,512]{1,0:T(8,128)(2,1)}, bf16[1024,512]{1,0:T(8,128)(2,1)}, bf16[1024,512]{1,0:T(8,128)(2,1)}, bf16[1024,512]{1,0:T(8,128)(2,1)}) custom-call(s32[216]{0:T(256)} %bitcast.64, bf16[2048,512]{1,0:T(8,128)(2,1)} %get-tuple-element.160.refs_6_.ga_ref, bf16[1024,512]{1,0:T(8,128)(2,1)} %all-gather.5.cloned.1.call-done.refs_5_.w_ref), custom_call_target="tpu_custom_call" | custom-call | flops 1000 | bytes 1000 | tf_op jit(solution)/shard_map/product_kernel/pallas_call | solution.py:685
  115.4 0.8 collective-permute-start.9
  116.2 3.8 %collective-permute-done.9 = f32[8,2048]{1,0:T(8,128)S(1)} collective-permute-done((f32[8,2048]{1,0:T(8,128)S(1)}, f32[8,2048]{1,0:T(8,128)S(1)}, u32[]{:S(2)}, u32[]{:S(2)}) %collective-permute-start.9) | collective-permute-done | bytes 65568 | tf_op jit(solution)/shard_map/ppermute | solution.py:600
  120.7 1.9 collective-permute-start.10
  123.3 18.0 %gate_kernel.1 = (bf16[2048,512]{1,0:T(8,128)(2,1)}, f32[2048,512]{1,0:T(8,128)}, f32[8,512]{1,0:T(8,128)}, bf16[1024,1024]{1,0:T(8,128)(2,1)}, f32[8,1024]{1,0:T(8,128)}) custom-call(s32[216]{0:T(256)} %bitcast.65, bf16[512,1024]{1,0:T(8,128)(2,1)} %refs_0_.3, bf16[512,1024]{1,0:T(8,128)(2,1)} %collective-permute-done.4.refs_1_, ...), custom_call_target="tpu_custom_call" | custom-call | flops 1000 | bytes 1000 | tf_op jit(solution)/shard_map/gate_kernel/pallas_call | solution.py:685
  141.3 2.2 collective-permute-done.11
  143.9 1.2 add_convert_fusion.3
  145.8 1.2 collective-permute-start.13
  147.0 51.0 %backward_kernel.1 = (bf16[1024,512]{1,0:T(8,128)(2,1)}, bf16[1024,512]{1,0:T(8,128)(2,1)}, bf16[1024,512]{1,0:T(8,128)(2,1)}, bf16[1024,512]{1,0:T(8,128)(2,1)}...) custom-call(s32[1,1]{1,0:T(1,128)S(6)} %copy.92.len_ref, ...), custom_call_target="tpu_custom_call" | custom-call | flops 1000 | bytes 1000 | tf_op jit(solution)/shard_map/backward_kernel/pallas_call | solution.py:685
  198.1 1.1 copy-done
  199.5 0.8 collective-permute-start.17
  200.4 1.4 collective-permute-start.18
  201.9 1.4 convert_add_fusion.4
  203.3 1.7 collective-permute-start.15
  205.0 1.6 convert_add_fusion.3
  206.6 1.8 collective-permute-done.15
  208.5 3.4 %collective-permute-start.16 = (f32[16,1024]{1,0:T(8,128)S(1)}, f32[16,1024]{1,0:T(8,128)S(1)}, u32[]{:S(2)}, u32[]{:S(2)}) collective-permute-start(f32[16,1024]{1,0:T(8,128)S(1)} %add.152), channel_id=1, source_target_pairs={{0,16},{4,20},{8,24},{12,28},{16,0},{20,4},{24,8},{28,12},{1,17},{... | collective-permute-start | bytes 196616 | tf_op jit(solution)/shard_map/ppermute | solution.py:645
  211.9 0.7 slice.199
  212.6 0.8 copy.68
  213.5 4.1 %collective-permute-done.16 = f32[16,1024]{1,0:T(8,128)S(1)} collective-permute-done((f32[16,1024]{1,0:T(8,128)S(1)}, f32[16,1024]{1,0:T(8,128)S(1)}, u32[]{:S(2)}, u32[]{:S(2)}) %collective-permute-start.16) | collective-permute-done | bytes 65568 | tf_op jit(solution)/shard_map/ppermute | solution.py:645
  217.9 0.8 collective-permute-done.18
  218.6 2.1 add_convert_fusion
  220.8 2.0 add_convert_fusion.1
  222.7 1.0 collective-permute-start.22
  224.4 1.1 collective-permute-start.20
  226.3 1.5 collective-permute-done.22
  227.8 0.8 collective-permute-start.23
  229.2 7.6 %collective-permute-done.23 = f32[16,1024]{1,0:T(8,128)S(1)} collective-permute-done((f32[16,1024]{1,0:T(8,128)S(1)}, f32[16,1024]{1,0:T(8,128)S(1)}, u32[]{:S(2)}, u32[]{:S(2)}) %collective-permute-start.23) | collective-permute-done | bytes 65568 | tf_op jit(solution)/shard_map/ppermute | solution.py:600
  236.8 1.0 slice.198
  237.8 1.8 collective-permute-start.21
  239.6 1.6 slice_convert_fusion
  241.3 1.2 collective-permute-done.21
  242.5 0.9 add_convert_fusion.4
  245.2 1.5 convert_add_fusion.2
  246.8 1.4 convert_add_fusion.1
  249.4 2.1 fusion.5
  (130 shorter events, 15.8 us)
Async XLA Ops:
  7.2 34.7 %copy-start.14 = (bf16[512,128]{1,0:T(8,128)(2,1)S(1)}, bf16[512,128]{1,0:T(8,128)(2,1)}, u32[]{:S(2)}) copy-start(bf16[512,128]{1,0:T(8,128)(2,1)} %param.34) | copy-start | bytes 393220
  7.2 46.7 %copy-start.1 = (bf16[512,1024]{1,0:T(8,128)(2,1)S(1)}, bf16[512,1024]{1,0:T(8,128)(2,1)}, u32[]{:S(2)}) copy-start(bf16[512,1024]{1,0:T(8,128)(2,1)} %refs_0_.3) | copy-start | bytes 3145732
  7.2 52.1 %all-gather.3.cloned.1.call-start = ((), (), s32[]{:S(2)}) async-start(), calls=%async_computation.2 | async-start | bytes 3244032 | tf_op jit(solution)/shard_map/all_gather | solution.py:913
  10.1 88.1 %all-gather.5.cloned.1.call-start = ((), (), s32[]{:S(2)}) async-start(), calls=%async_computation.3 | async-start | bytes 1179648 | tf_op jit(solution)/shard_map/all_gather | solution.py:916
  10.2 26.4 %collective-permute-start = (bf16[512,1024]{1,0:T(8,128)(2,1)}, bf16[512,1024]{1,0:T(8,128)(2,1)S(1)}, u32[]{:S(2)}, u32[]{:S(2)}) collective-permute-start(bf16[512,1024]{1,0:T(8,128)(2,1)} %refs_0_.1), channel_id=1, source_target_pairs={{0,1},{1,0},{2,3},{3,2},{4,5},{5,4},{6,7},{7,6},{8,9},{9,8},{10,11... | collective-permute-start | bytes 3145736 | tf_op jit(solution)/shard_map/ppermute | solution.py:596
  13.2 24.8 %collective-permute-start.1 = (bf16[512,1024]{1,0:T(8,128)(2,1)}, bf16[512,1024]{1,0:T(8,128)(2,1)S(1)}, u32[]{:S(2)}, u32[]{:S(2)}) collective-permute-start(bf16[512,1024]{1,0:T(8,128)(2,1)} %refs_0_.1), channel_id=1, source_target_pairs={{0,2},{2,0},{1,3},{3,1},{4,6},{6,4},{5,7},{7,5},{8,10},{10,8},{9,1... | collective-permute-start | bytes 3145736 | tf_op jit(solution)/shard_map/ppermute | solution.py:600
  36.5 22.7 %copy-start.3 = (bf16[512,1024]{1,0:T(8,128)(2,1)}, bf16[512,1024]{1,0:T(8,128)(2,1)S(1)}, u32[]{:S(2)}) copy-start(bf16[512,1024]{1,0:T(8,128)(2,1)S(1)} %collective-permute-done.refs_1_) | copy-start | bytes 3145732
  38.0 21.3 %copy-start.4 = (bf16[512,1024]{1,0:T(8,128)(2,1)}, bf16[512,1024]{1,0:T(8,128)(2,1)S(1)}, u32[]{:S(2)}) copy-start(bf16[512,1024]{1,0:T(8,128)(2,1)S(1)} %collective-permute-done.1.refs_2_) | copy-start | bytes 3145732
  39.7 12.9 %collective-permute-start.2 = (bf16[512,512]{1,0:T(8,128)(2,1)}, bf16[512,512]{1,0:T(8,128)(2,1)}, u32[]{:S(2)}, u32[]{:S(2)}) collective-permute-start(bf16[512,512]{1,0:T(8,128)(2,1)} %slice.142), channel_id=1, source_target_pairs={{0,2},{2,0},{1,3},{3,1},{4,6},{6,4},{5,7},{7,5},{8,10},{10,8},{9,1... | collective-permute-start | bytes 1572872 | tf_op jit(solution)/shard_map/ppermute | solution.py:600
  41.3 12.6 %collective-permute-start.3 = (bf16[512,512]{1,0:T(8,128)(2,1)}, bf16[512,512]{1,0:T(8,128)(2,1)}, u32[]{:S(2)}, u32[]{:S(2)}) collective-permute-start(bf16[512,512]{1,0:T(8,128)(2,1)} %slice.143), channel_id=1, source_target_pairs={{0,1},{1,0},{2,3},{3,2},{4,5},{5,4},{6,7},{7,6},{8,9},{9,8},{10,11... | collective-permute-start | bytes 1572872 | tf_op jit(solution)/shard_map/ppermute | solution.py:596
  42.7 155.4 %reduce-scatter.3.cloned.1.call-start = ((), (), s32[]{:S(2)}) async-start(), calls=%async_computation.4 | async-start | bytes 2359296 | tf_op jit(solution)/shard_map/reduce_scatter | solution.py:1007
  53.9 28.1 %collective-permute-start.4 = (bf16[512,1024]{1,0:T(8,128)(2,1)S(1)}, bf16[512,1024]{1,0:T(8,128)(2,1)}, u32[]{:S(2)}, u32[]{:S(2)}) collective-permute-start(bf16[512,1024]{1,0:T(8,128)(2,1)S(1)} %copy-done.1), channel_id=1, source_target_pairs={{0,1},{1,0},{2,3},{3,2},{4,5},{5,4},{6,7},{7,6},{8,9},{9,8},{10,11... | collective-permute-start | bytes 3145736 | tf_op jit(solution)/shard_map/ppermute | solution.py:596
  54.5 27.5 %collective-permute-start.5 = (bf16[512,1024]{1,0:T(8,128)(2,1)S(1)}, bf16[512,1024]{1,0:T(8,128)(2,1)}, u32[]{:S(2)}, u32[]{:S(2)}) collective-permute-start(bf16[512,1024]{1,0:T(8,128)(2,1)S(1)} %copy-done.1), channel_id=1, source_target_pairs={{0,2},{2,0},{1,3},{3,1},{4,6},{6,4},{5,7},{7,5},{8,10},{10,8},{9,1... | collective-permute-start | bytes 3145736 | tf_op jit(solution)/shard_map/ppermute | solution.py:600
  84.2 14.0 %collective-permute-start.6 = (bf16[512,512]{1,0:T(8,128)(2,1)S(1)}, bf16[512,512]{1,0:T(8,128)(2,1)S(1)}, u32[]{:S(2)}, u32[]{:S(2)}) collective-permute-start(bf16[512,512]{1,0:T(8,128)(2,1)S(1)} %slice.153), channel_id=1, source_target_pairs={{0,2},{2,0},{1,3},{3,1},{4,6},{6,4},{5,7},{7,5},{8,10},{10,8},{9,1... | collective-permute-start | bytes 1572872 | tf_op jit(solution)/shard_map/ppermute | solution.py:600
  85.5 12.7 %collective-permute-start.7 = (bf16[512,512]{1,0:T(8,128)(2,1)S(1)}, bf16[512,512]{1,0:T(8,128)(2,1)S(1)}, u32[]{:S(2)}, u32[]{:S(2)}) collective-permute-start(bf16[512,512]{1,0:T(8,128)(2,1)S(1)} %slice.154), channel_id=1, source_target_pairs={{0,1},{1,0},{2,3},{3,2},{4,5},{5,4},{6,7},{7,6},{8,9},{9,8},{10,11... | collective-permute-start | bytes 1572872 | tf_op jit(solution)/shard_map/ppermute | solution.py:596
  98.2 0.8 copy-start.5
  98.2 0.9 copy-start.6
  107.5 7.9 %copy-start.17 = (f32[8,2048]{1,0:T(8,128)S(1)}, f32[8,2048]{1,0:T(8,128)}, u32[]{:S(2)}) copy-start(f32[8,2048]{1,0:T(8,128)} %get-tuple-element.158) | copy-start | bytes 196612
  107.5 7.9 %collective-permute-start.8 = (f32[8,2048]{1,0:T(8,128)}, f32[8,2048]{1,0:T(8,128)S(1)}, u32[]{:S(2)}, u32[]{:S(2)}) collective-permute-start(f32[8,2048]{1,0:T(8,128)} %get-tuple-element.158), channel_id=1, source_target_pairs={{0,1},{1,0},{2,3},{3,2},{4,5},{5,4},{6,7},{7,6},{8,9},{9,8},{10,11... | collective-permute-start | bytes 196616 | tf_op jit(solution)/shard_map/ppermute | solution.py:596
  115.4 4.6 %collective-permute-start.9 = (f32[8,2048]{1,0:T(8,128)S(1)}, f32[8,2048]{1,0:T(8,128)S(1)}, u32[]{:S(2)}, u32[]{:S(2)}) collective-permute-start(f32[8,2048]{1,0:T(8,128)S(1)} %add.137), channel_id=1, source_target_pairs={{0,2},{2,0},{1,3},{3,1},{4,6},{6,4},{5,7},{7,5},{8,10},{10,8},{9,1... | collective-permute-start | bytes 196616 | tf_op jit(solution)/shard_map/ppermute | solution.py:600
  120.7 20.6 %collective-permute-start.10 = (bf16[1024,512]{1,0:T(8,128)(2,1)}, bf16[1024,512]{1,0:T(8,128)(2,1)S(1)}, u32[]{:S(2)}, u32[]{:S(2)}) collective-permute-start(bf16[1024,512]{1,0:T(8,128)(2,1)} %get-tuple-element.181), channel_id=1, source_target_pairs={{0,1},{1,0},{2,3},{3,2},{4,5},{5,4},{6,7},{7,6},{8,9},{9,8},{10,11... | collective-permute-start | bytes 3145736 | tf_op jit(solution)/shard_map/ppermute | solution.py:596
  122.6 20.8 %collective-permute-start.11 = (bf16[1024,512]{1,0:T(8,128)(2,1)}, bf16[1024,512]{1,0:T(8,128)(2,1)S(1)}, u32[]{:S(2)}, u32[]{:S(2)}) collective-permute-start(bf16[1024,512]{1,0:T(8,128)(2,1)} %get-tuple-element.182), channel_id=1, source_target_pairs={{0,2},{2,0},{1,3},{3,1},{4,6},{6,4},{5,7},{7,5},{8,10},{10,8},{9,1... | collective-permute-start | bytes 3145736 | tf_op jit(solution)/shard_map/ppermute | solution.py:600
  141.2 2.5 copy-start.9
  141.2 2.6 %copy-start.10 = (bf16[1024,512]{1,0:T(8,128)(2,1)S(1)}, bf16[1024,512]{1,0:T(8,128)(2,1)}, u32[]{:S(2)}) copy-start(bf16[1024,512]{1,0:T(8,128)(2,1)} %get-tuple-element.170) | copy-start | bytes 3145732
  141.3 2.2 copy-start.12
  143.4 1.6 copy-start.11
  143.5 93.4 %reduce-scatter.5.cloned.1.call-start = ((), (), s32[]{:S(2)}) async-start(), calls=%async_computation.5 | async-start | bytes 2064384 | tf_op jit(solution)/shard_map/reduce_scatter | solution.py:1029
  145.1 53.0 %collective-permute-start.12 = (bf16[512,512]{1,0:T(8,128)(2,1)S(1)}, bf16[512,512]{1,0:T(8,128)(2,1)}, u32[]{:S(2)}, u32[]{:S(2)}) collective-permute-start(bf16[512,512]{1,0:T(8,128)(2,1)S(1)} %add_convert_fusion.3), channel_id=1, source_target_pairs={{0,2},{2,0},{1,3},{3,1},{4,6},{6,4},{5,7},{7,5},{8,10},{10,8},{9,1... | collective-permute-start | bytes 1572872 | tf_op jit(solution)/shard_map/ppermute | solution.py:600
  145.8 52.3 %collective-permute-start.13 = (bf16[512,512]{1,0:T(8,128)(2,1)S(1)}, bf16[512,512]{1,0:T(8,128)(2,1)}, u32[]{:S(2)}, u32[]{:S(2)}) collective-permute-start(bf16[512,512]{1,0:T(8,128)(2,1)S(1)} %add_convert_fusion.2), channel_id=1, source_target_pairs={{0,1},{1,0},{2,3},{3,2},{4,5},{5,4},{6,7},{7,6},{8,9},{9,8},{10,11... | collective-permute-start | bytes 1572872 | tf_op jit(solution)/shard_map/ppermute | solution.py:596
  198.0 1.2 copy-start
  198.0 3.7 %slice-start = ((f32[8,2048]{1,0:T(8,128)}), f32[1,2048]{1,0:T(1,128)S(1)}, s32[]{:S(2)}) async-start(f32[8,2048]{1,0:T(8,128)} %add.138.refs_5_), calls=%async_computation.6 | async-start | bytes 16384 | tf_op jit(solution)/shard_map/slice | solution.py:1048
  198.0 3.7 %copy-start.16 = (f32[16,1024]{1,0:T(8,128)S(1)}, f32[16,1024]{1,0:T(8,128)}, u32[]{:S(2)}) copy-start(f32[16,1024]{1,0:T(8,128)} %get-tuple-element.209) | copy-start | bytes 196612
  199.5 18.4 %collective-permute-start.17 = (bf16[1024,512]{1,0:T(8,128)(2,1)}, bf16[1024,512]{1,0:T(8,128)(2,1)}, u32[]{:S(2)}, u32[]{:S(2)}) collective-permute-start(bf16[1024,512]{1,0:T(8,128)(2,1)} %get-tuple-element.210), channel_id=1, source_target_pairs={{0,1},{1,0},{2,3},{3,2},{4,5},{5,4},{6,7},{7,6},{8,9},{9,8},{10,11... | collective-permute-start | bytes 3145736 | tf_op jit(solution)/shard_map/ppermute | solution.py:596
  200.4 18.3 %collective-permute-start.18 = (bf16[1024,512]{1,0:T(8,128)(2,1)}, bf16[1024,512]{1,0:T(8,128)(2,1)}, u32[]{:S(2)}, u32[]{:S(2)}) collective-permute-start(bf16[1024,512]{1,0:T(8,128)(2,1)} %get-tuple-element.211), channel_id=1, source_target_pairs={{0,2},{2,0},{1,3},{3,1},{4,6},{6,4},{5,7},{7,5},{8,10},{10,8},{9,1... | collective-permute-start | bytes 3145736 | tf_op jit(solution)/shard_map/ppermute | solution.py:600
  201.8 4.8 %copy-start.13 = (bf16[128,1024]{1,0:T(8,128)(2,1)S(1)}, bf16[128,1024]{1,0:T(8,128)(2,1)}, u32[]{:S(2)}) copy-start(bf16[128,1024]{1,0:T(8,128)(2,1)} %reduce-scatter.3.cloned.1.call-done) | copy-start | bytes 786436
  201.8 1.5 collective-permute-start.14
  203.3 5.1 %collective-permute-start.15 = (f32[16,1024]{1,0:T(8,128)S(1)}, f32[16,1024]{1,0:T(8,128)S(1)}, u32[]{:S(2)}, u32[]{:S(2)}) collective-permute-start(f32[16,1024]{1,0:T(8,128)S(1)} %add.151), channel_id=1, source_target_pairs={{0,8},{4,12},{8,0},{12,4},{16,24},{20,28},{24,16},{28,20},{1,9},{5... | collective-permute-start | bytes 196616 | tf_op jit(solution)/shard_map/ppermute | solution.py:645
  208.5 9.2 %collective-permute-start.16 = (f32[16,1024]{1,0:T(8,128)S(1)}, f32[16,1024]{1,0:T(8,128)S(1)}, u32[]{:S(2)}, u32[]{:S(2)}) collective-permute-start(f32[16,1024]{1,0:T(8,128)S(1)} %add.152), channel_id=1, source_target_pairs={{0,16},{4,20},{8,24},{12,28},{16,0},{20,4},{24,8},{28,12},{1,17},{... | collective-permute-start | bytes 196616 | tf_op jit(solution)/shard_map/ppermute | solution.py:645
  213.5 7.3 %copy-start.8 = (bf16[1024,512]{1,0:T(8,128)(2,1)S(1)}, bf16[1024,512]{1,0:T(8,128)(2,1)}, u32[]{:S(2)}) copy-start(bf16[1024,512]{1,0:T(8,128)(2,1)} %get-tuple-element.208) | copy-start | bytes 3145732
  222.7 5.0 %collective-permute-start.22 = (f32[16,1024]{1,0:T(8,128)S(1)}, f32[16,1024]{1,0:T(8,128)S(1)}, u32[]{:S(2)}, u32[]{:S(2)}) collective-permute-start(f32[16,1024]{1,0:T(8,128)S(1)} %add.153), channel_id=1, source_target_pairs={{0,1},{1,0},{2,3},{3,2},{4,5},{5,4},{6,7},{7,6},{8,9},{9,8},{10,11... | collective-permute-start | bytes 196616 | tf_op jit(solution)/shard_map/ppermute | solution.py:596
  223.7 19.7 %collective-permute-start.19 = (bf16[512,512]{1,0:T(8,128)(2,1)}, bf16[512,512]{1,0:T(8,128)(2,1)}, u32[]{:S(2)}, u32[]{:S(2)}) collective-permute-start(bf16[512,512]{1,0:T(8,128)(2,1)} %add_convert_fusion.1), channel_id=1, source_target_pairs={{0,2},{2,0},{1,3},{3,1},{4,6},{6,4},{5,7},{7,5},{8,10},{10,8},{9,1... | collective-permute-start | bytes 1572872 | tf_op jit(solution)/shard_map/ppermute | solution.py:600
  224.4 19.1 %collective-permute-start.20 = (bf16[512,512]{1,0:T(8,128)(2,1)}, bf16[512,512]{1,0:T(8,128)(2,1)}, u32[]{:S(2)}, u32[]{:S(2)}) collective-permute-start(bf16[512,512]{1,0:T(8,128)(2,1)} %add_convert_fusion), channel_id=1, source_target_pairs={{0,1},{1,0},{2,3},{3,2},{4,5},{5,4},{6,7},{7,6},{8,9},{9,8},{10,11... | collective-permute-start | bytes 1572872 | tf_op jit(solution)/shard_map/ppermute | solution.py:596
  227.8 9.0 %collective-permute-start.23 = (f32[16,1024]{1,0:T(8,128)S(1)}, f32[16,1024]{1,0:T(8,128)S(1)}, u32[]{:S(2)}, u32[]{:S(2)}) collective-permute-start(f32[16,1024]{1,0:T(8,128)S(1)} %add.158), channel_id=1, source_target_pairs={{0,2},{2,0},{1,3},{3,1},{4,6},{6,4},{5,7},{7,5},{8,10},{10,8},{9,1... | collective-permute-start | bytes 196616 | tf_op jit(solution)/shard_map/ppermute | solution.py:600
  236.8 11.4 %copy-start.15 = (f32[16,1024]{1,0:T(8,128)}, f32[16,1024]{1,0:T(8,128)S(1)}, u32[]{:S(2)}) copy-start(f32[16,1024]{1,0:T(8,128)S(1)} %add.159) | copy-start | bytes 196612
  236.8 9.9 %copy-start.7 = (bf16[1024,512]{1,0:T(8,128)(2,1)S(1)}, bf16[1024,512]{1,0:T(8,128)(2,1)}, u32[]{:S(2)}) copy-start(bf16[1024,512]{1,0:T(8,128)(2,1)} %get-tuple-element.213) | copy-start | bytes 3145732
  237.8 4.7 %collective-permute-start.21 = (bf16[128,384]{1,0:T(8,128)(2,1)S(1)}, bf16[128,384]{1,0:T(8,128)(2,1)S(1)}, u32[]{:S(2)}, u32[]{:S(2)}) collective-permute-start(bf16[128,384]{1,0:T(8,128)(2,1)S(1)} %slice.198), channel_id=1, source_target_pairs={{0,1},{1,0},{2,3},{3,2},{4,5},{5,4},{6,7},{7,6},{8,9},{9,8},{10,11... | collective-permute-start | bytes 294920 | tf_op jit(solution)/shard_map/ppermute | solution.py:596
  244.7 7.5 %collective-permute-start.24 = (bf16[128,384]{1,0:T(8,128)(2,1)S(1)}, bf16[128,384]{1,0:T(8,128)(2,1)S(1)}, u32[]{:S(2)}, u32[]{:S(2)}) collective-permute-start(bf16[128,384]{1,0:T(8,128)(2,1)S(1)} %add_convert_fusion.4), channel_id=1, source_target_pairs={{0,2},{2,0},{1,3},{3,1},{4,6},{6,4},{5,7},{7,5},{8,10},{10,8},{9,1... | collective-permute-start | bytes 294920 | tf_op jit(solution)/shard_map/ppermute | solution.py:600
  248.2 1.2 copy-start.2
  249.4 2.2 slice-start.1
Sparse Core Ops, SparseCore 0:
  10.2 38.9 all-gather.2
  51.4 21.0 all-gather.4
  143.6 35.6 reduce-scatter.2
  198.2 37.3 reduce-scatter.4

commit v3 on v2

--- a/solution.py
+++ b/solution.py
@@ -15,6 +15,7 @@
 ROWS = 256
 WIDE_ROWS = 512
 FIELD = 32
+PARAMS = 8
 SUB = 128
 EPS = 1e-05
 LOG2E = 1.4426950408889634
@@ -309,6 +310,56 @@
     square_ref[...] = jnp.broadcast_to(square, (rows, LANES)).T[:8, :]
 
 
+def parameter_kernel(
+    first_ref, packed_ref, prm_ref, prs_ref, prh_ref, gain_ref, *, taps, heads_here, cut, state_cut, head_cut, depth
+):
+    packed = packed_ref[...]
+    total = packed.shape[1]
+    source = lax.broadcasted_iota(jnp.int32, (total, 1), 0)
+    maps_at = heads_here * cut
+
+    def split(z, size):
+        return z >> (size.bit_length() - 1), z & (size - 1)
+
+    def moved(columns, lane_of):
+        lane = lane_of(lax.broadcasted_iota(jnp.int32, (1, columns), 1))
+        return nn(packed, jnp.where(source == lane, 1.0, 0.0).astype(bf16))
+
+    def by_channel(c):
+        head, inside = split(c, HEADDIM)
+        owner, place = split(inside, cut)
+        return owner * LANES + head * cut + place
+
+    def by_part(size, at):
+        def lane_of(c):
+            owner, place = split(c, size)
+            return owner * LANES + at + place
+
+        return lane_of
+
+    def own_head(at):
+        part = by_part(head_cut, at)
+        return lambda h: jnp.where(h < heads_here, part(first_ref[0] + h), -1)
+
+    channels = prm_ref.shape[1]
+    row = lax.broadcasted_iota(jnp.int32, (PARAMS, 1), 0)
+    by_head = moved(channels, by_channel)
+    skip = by_part(head_cut, maps_at + 2 * head_cut)
+    skips = moved(channels, lambda c: skip(first_ref[0] + split(c, HEADDIM)[0]))
+    prm_ref[...] = jnp.where(
+        row <= taps,
+        by_head,
+        jnp.where(row == taps + 1, skips, jnp.where(row == taps + 2, pltpu.roll(by_head, 1, 0), 0.0)),
+    )
+    prs_ref[...] = jnp.where(row <= taps, moved(2 * STATE, by_part(state_cut, maps_at)), 0.0)
+    bias = moved(LANES, own_head(maps_at))[taps + 1 : taps + 2]
+    rate = jnp.exp(moved(LANES, own_head(maps_at + head_cut))[taps + 1 : taps + 2])
+    lane = lax.broadcasted_iota(jnp.int32, (1, LANES), 1)
+    rate = jnp.where(lane < heads_here, rate, 0.0)
+    prh_ref[...] = jnp.where(row == 0, bias, jnp.where(row == 1, rate, 0.0))
+    gain_ref[...] = moved(gain_ref.shape[1], by_part(depth, 0))[taps + 2 : taps + 3]
+
+
 def product_kernel(place_ref, ga_ref, w_ref, *refs, place_at):
     product = nt(ga_ref[...], w_ref[...]).astype(bf16)
     put_halves(refs, place_ref[place_at + pl.program_id(0)], product)
@@ -361,6 +412,8 @@
     sums = jnp.concatenate([sums_ref[...], jnp.zeros((LANES - 8, rows), f32)], axis=0).T
     inverse = lax.rsqrt(sums[:, 0:1] * (1.0 / INNER) + EPS)
     inner_mean = sums[:, 1:2] * inverse * (1.0 / INNER)
+    normed = normed_ref[...]
+    cotangent = take_rows(part_refs, place_ref[place_at + step_id], cot_buf)
     gain = prm_ref[taps + 2 : taps + 3, :]
     gate_pre = gate_ref[...].astype(f32)
     sig_gate = jax.nn.sigmoid(gate_pre)
@@ -368,16 +421,14 @@
     y = y_ref[...].astype(f32)
     hat = y * act * inverse
     gated = (hat * gain).astype(bf16)
+    total[:, channels:] += tn(cotangent, gated)
     grad_gated = gg_ref[...].astype(f32)
     dprm_ref[taps + 2 : taps + 3, :] += jnp.sum(grad_gated * hat, axis=0, keepdims=True)
     grad_inner = inverse * (grad_gated * gain - hat * inner_mean)
-    dy = grad_inner * act
+    dy_ref[...] = grad_inner * act
     dgate = (grad_inner * y * sig_gate * (1.0 + gate_pre * (1.0 - sig_gate))).astype(bf16)
     dgate_ref[...] = dgate
-    dy_ref[...] = dy
-    total[:, :channels] += tn(normed_ref[...], dgate)
-    cotangent = take_rows(part_refs, place_ref[place_at + step_id], cot_buf)
-    total[:, channels:] += tn(cotangent, gated)
+    total[:, :channels] += tn(normed, dgate)
 
     @pl.when(step_id == pl.num_programs(0) - 1)
     def _():
@@ -409,7 +460,7 @@
         st_ref,
     ) = refs[:20]
     half_refs = refs[20 : 20 + halves]
-    out_ref, small_ref, dprm_ref, dprs_ref, dprh_ref, dbuf, dsbuf, carry, ending, gb_ref, total = refs[20 + halves :]
+    out_ref, small_ref, dprm_ref, dprs_ref, dprh_ref, dbuf, dsbuf, carry, ending, total = refs[20 + halves :]
     rows, channels = dgate_ref.shape
     step_id = pl.program_id(0)
     base = (pl.num_programs(0) - 1 - step_id) * rows
@@ -511,37 +562,34 @@
     draw = (by_head[rows : 2 * rows] - decay * dlog) * jax.nn.sigmoid(raw)
     add_row(dprh_ref, 0, draw)
     add_row(dprh_ref, 1, dlog * step * -decay)
-    du = (step_w * dstepped + skip * dy) * sig_u * (1.0 + u * (1.0 - sig_u))
-    dus = dmap * sig_us * (1.0 + us * (1.0 - sig_us))
-    dbuf[0:rows, :] = du
-    dsbuf[0:rows, :] = dus
-    v = v_ref[...].astype(f32)
-    vs = vs_ref[...].astype(f32)
     places = base + lax.broadcasted_iota(jnp.int32, (rows, 1), 0)
     segment = segment_of(places, ends)
-    dv = prm_ref[taps - 1 : taps, :] * du
-    dvs = prs_ref[taps - 1 : taps, :] * dus
-    add_row(dprm_ref, taps - 1, du * v)
-    add_row(dprs_ref, taps - 1, dus * vs)
-    add_row(dprm_ref, taps, du)
-    add_row(dprs_ref, taps, dus)
-    for lag in range(1, taps):
-        usable = segment_of(places + lag, ends) == segment
-        tap = taps - 1 - lag
-        later = jnp.where(usable, dbuf[lag : lag + rows, :], 0.0)
-        later_s = jnp.where(usable, dsbuf[lag : lag + rows, :], 0.0)
-        dv = dv + prm_ref[tap : tap + 1, :] * later
-        dvs = dvs + prs_ref[tap : tap + 1, :] * later_s
-        add_row(dprm_ref, tap, later * v)
-        add_row(dprs_ref, tap, later_s * vs)
-    dbuf[rows : rows + 8, :] = dbuf[0:8, :]
-    dsbuf[rows : rows + 8, :] = dsbuf[0:8, :]
-    gb_ref[:, :channels] = dv.astype(bf16)
-    gb_ref[:, channels : channels + 2 * STATE] = dvs.astype(bf16)
-    gb_ref[:, channels + 2 * STATE :] = pltpu.roll(draw, first_ref[0], 1).astype(bf16)
-    product = nt(dgate_ref[...], w_ref[:, :channels]) + nt(gb_ref[...], w_ref[:, channels:])
+    usable = [None] + [segment_of(places + lag, ends) == segment for lag in range(1, taps)]
+    normed = normed_ref[...]
+
+    def conv_back(du, v, weight_ref, buffer, sums_ref):
+        buffer[0:rows, :] = du
+        dv = weight_ref[taps - 1 : taps, :] * du
+        lines = [jnp.sum(du * v, axis=0, keepdims=True), jnp.sum(du, axis=0, keepdims=True)]
+        for lag in range(1, taps):
+            later = jnp.where(usable[lag], buffer[lag : lag + rows, :], 0.0)
+            dv = dv + weight_ref[taps - 1 - lag : taps - lag, :] * later
+            lines.insert(0, jnp.sum(later * v, axis=0, keepdims=True))
+        buffer[rows : rows + 8, :] = buffer[0:8, :]
+        sums_ref[0 : taps + 1, :] += jnp.concatenate(lines, axis=0)
+        return dv.astype(bf16)
+
+    product = nt(dgate_ref[...], w_ref[:, :channels])
+    du = (step_w * dstepped + skip * dy) * sig_u * (1.0 + u * (1.0 - sig_u))
+    dv = conv_back(du, v_ref[...].astype(f32), prm_ref, dbuf, dprm_ref)
+    product = product + nt(dv, w_ref[:, channels : 2 * channels])
+    total[:, :channels] += tn(normed, dv)
+    dus = dmap * sig_us * (1.0 + us * (1.0 - sig_us))
+    dvs = conv_back(dus, vs_ref[...].astype(f32), prs_ref, dsbuf, dprs_ref)
+    state_part = jnp.concatenate([dvs, pltpu.roll(draw, first_ref[0], 1).astype(bf16)], axis=1)
+    product = product + nt(state_part, w_ref[:, 2 * channels :])
+    total[:, channels:] += tn(normed, state_part)
     put_halves(half_refs, place_ref[place_at + step_id], product.astype(bf16))
-    total[...] += tn(normed_ref[...], gb_ref[...])
 
     @pl.when(step_id == pl.num_programs(0) - 1)
     def _():
@@ -630,7 +678,7 @@
     left, right = halves[1][:rows].astype(f32), halves[3][:rows].astype(f32)
     left = left + from_x[:rows].astype(f32) + far_left.astype(f32)
     right = right + from_y[:rows].astype(f32) + far_right.astype(f32)
-    return jnp.concatenate([left, right], axis=1)
+    return left, right
 
 
 def sum_over_tensor(z):
@@ -679,7 +727,7 @@
     def at(self, block, backwards, line):
         return (self.kinds[(block, backwards)] * self.lines + line) * self.steps
 
-    def call(self, kernel, scalars, steps, ins, outs, scratch, aliases=None):
+    def call(self, kernel, scalars, steps, ins, outs, scratch, aliases=None, flops=1000):
         specs, arrays = zip(*ins)
         out_specs, out_shapes = zip(*outs)
         return pl.pallas_call(
@@ -694,7 +742,7 @@
             out_shape=list(out_shapes),
             input_output_aliases=aliases or {},
             compiler_params=pltpu.CompilerParams(vmem_limit_bytes=56 * 2**20),
-            cost_estimate=pl.CostEstimate(flops=1000, bytes_accessed=1000, transcendentals=0),
+            cost_estimate=pl.CostEstimate(flops=flops, bytes_accessed=1000, transcendentals=0),
             name=getattr(kernel, "func", kernel).__name__,
         )(*scalars, *arrays)
 
@@ -744,6 +792,25 @@
             )
             for k in lines
         ]
+
+    def parameters(self, packed, cut, state_cut, head_cut, depth):
+        shapes = ((PARAMS, self.channels), (PARAMS, 2 * STATE), (PARAMS, LANES), (1, self.width))
+        return self.call(
+            functools.partial(
+                parameter_kernel,
+                taps=self.taps,
+                heads_here=self.head_count,
+                cut=cut,
+                state_cut=state_cut,
+                head_cut=head_cut,
+                depth=depth,
+            ),
+            (self.first,),
+            1,
+            [self.whole(packed)],
+            [self.whole(jax.ShapeDtypeStruct(shape, f32)) for shape in shapes],
+            [],
+        )
 
     def scan(self, low, high, hidden, weights, gain, prm, prs, prh, carried, before=()):
         channels, count = self.channels, self.group_rows
@@ -838,6 +905,7 @@
                 self.whole(jax.ShapeDtypeStruct((8, self.width), f32)),
             ],
             [pltpu.VMEM((WIDE_ROWS, self.width), bf16), pltpu.VMEM((self.width, 2 * channels), f32)],
+            flops=8 * self.group_rows * self.width * channels * 4,
         )
 
     def backward(self, weights, gain, terms, dprm_gate, prm, prs, prh, saved):
@@ -870,7 +938,6 @@
                 pltpu.VMEM((ROWS + 8, 2 * STATE), f32),
                 pltpu.VMEM((STATE, channels), f32),
                 pltpu.VMEM((8, channels), f32),
-                pltpu.VMEM((ROWS, gradients), bf16),
                 pltpu.VMEM((self.width, gradients), f32),
             ],
         )
@@ -917,48 +984,29 @@
     if square_mesh:
         from_x, from_y = gather_start(hidden_in)
 
-    small = [
-        norm_gain,
-        conv_kernel,
-        conv_offset,
-        state_kernel,
-        state_offset,
-        step_bias,
-        decay_log,
-        skip_gain,
-        gate_gain,
-    ]
-    flat = jnp.concatenate([z.reshape(-1) for z in small])
-    flat = jnp.pad(flat, (0, -flat.shape[0] % 1024)).reshape(-1, LANES)
-    small_all = lax.all_gather(flat, "dp", axis=0)
+    def padded(z):
+        return jnp.pad(z, ((0, 0), (0, LANES - z.shape[1])))
+
+    packed = jnp.concatenate(
+        [
+            padded(jnp.concatenate([conv_kernel.reshape(taps, -1), state_kernel], axis=1)),
+            padded(jnp.concatenate([conv_offset.reshape(1, -1), state_offset[None]], axis=1)),
+            padded(
+                jnp.concatenate(
+                    [gate_gain.reshape(1, -1), step_bias[None], decay_log[None], skip_gain[None]], axis=1
+                )
+            ),
+            padded(norm_gain[None]),
+        ],
+        axis=0,
+    )
+    packed = jnp.pad(packed, ((0, PARAMS - packed.shape[0]), (0, 0)))
+    packed = lax.all_gather(packed, "dp", axis=1, tiled=True)
     if square_mesh:
-        from_x, from_y, small_all = lax.optimization_barrier((from_x, from_y, small_all))
+        from_x, from_y, packed = lax.optimization_barrier((from_x, from_y, packed))
         hidden_all, _ = gather_end(hidden_in, from_x, from_y)
-        hidden_all, cot = lax.optimization_barrier((hidden_all, out_cotangent))
     else:
         hidden_all = [lax.all_gather(hidden_in, "tensor", axis=0, tiled=True)]
-    small_all = small_all.reshape(dp_count, -1).astype(f32)
-    shares, at = [], 0
-    for z in small:
-        shares.append(small_all[:, at : at + z.size].reshape((dp_count,) + z.shape))
-        at += z.size
-    gain_in = shares[0].reshape(1, width)
-    taps_conv = shares[1].transpose(1, 2, 0, 3).reshape(taps, channels)
-    off_conv = shares[2].transpose(1, 0, 2).reshape(1, channels)
-    taps_state = shares[3].transpose(1, 0, 2).reshape(taps, 2 * STATE)
-    off_state = shares[4].reshape(1, 2 * STATE)
-    gain_gate = shares[8].transpose(1, 0, 2).reshape(1, channels)
-
-    def own_heads(z):
-        return lax.dynamic_slice_in_dim(z.reshape(-1), first_head, heads_here, 0)
-
-    skip = jnp.repeat(own_heads(shares[7]), HEADDIM).reshape(1, channels)
-    prm = jnp.concatenate([taps_conv, off_conv, skip, gain_gate], axis=0)
-    prm = jnp.pad(prm, ((0, -prm.shape[0] % 8), (0, 0)))
-    prs = jnp.concatenate([taps_state, off_state], axis=0)
-    prs = jnp.pad(prs, ((0, -prs.shape[0] % 8), (0, 0)))
-    prh = jnp.stack([own_heads(shares[5]), jnp.exp(own_heads(shares[6]))])
-    prh = jnp.pad(prh, ((0, 6), (0, LANES - heads_here)))
 
     kernels = Kernels(
         seq_lengths,
@@ -971,6 +1019,12 @@
         taps,
         heads_here,
     )
+
+    prm, prs, prh, gain_in = kernels.parameters(packed, cut, state_cut, head_cut, depth)
+    if square_mesh:
+        hidden_all, prm, kernels.place, cot = lax.optimization_barrier(
+            (hidden_all, prm, kernels.place, out_cotangent)
+        )
 
     blocks = group_rows // ROWS
     common = (hidden_all, weights, gain_in, prm, prs, prh)
@@ -992,7 +1046,6 @@
         sums = sums + over_x(sums)
         sums, out_halves = lax.optimization_barrier((sums, out_halves))
         sums = sums + over_y(sums)
-        sums, out_halves = lax.optimization_barrier((sums, out_halves))
         moving = scatter_start(out_halves)
     else:
         sums = lax.psum(sums, "tensor")
@@ -1034,12 +1087,14 @@
     small_shared = sum_over_tensor(small_sum) if square_mesh else lax.psum(small_sum, "tensor")
 
     if square_mesh:
+        far, own_last, small_shared = lax.optimization_barrier((far, own_last, small_shared))
         own_state = own_last[:, channels:].astype(f32)
         own_state = (own_state + over_x(own_last[:, channels:]).astype(f32)).astype(bf16)
-        far, own_state, small_shared = lax.optimization_barrier((far, own_state, small_shared))
+        grad_normed = scatter_end(gn_halves, *moving, *far)
+        grad_normed, own_state = lax.optimization_barrier((grad_normed, own_state))
         own_state = own_state.astype(f32) + over_y(own_state).astype(f32)
-        grad_normed = scatter_end(gn_halves, *moving, *far)
-        branch = scatter_end(out_halves, *out_moving)
+        grad_normed = jnp.concatenate(grad_normed, axis=1)
+        branch = jnp.concatenate(scatter_end(out_halves, *out_moving), axis=1)
     else:
         grad_normed = own_sum(gn_halves)
         own_state = lax.psum(own_last[:, channels:].astype(f32), "tensor")

time: 260 us -> 247 us (0.950)
  local copies, waits for them, and re-layouts: 24.3 us -> 17 us
  Pallas kernels: 119 us -> 112 us
    ppermute x11, waiting for transfers between devices: 23.6 us -> 16.6 us  [over_y(): return lax.ppermute(z, 'tensor', [(0, 2), (2, 0), (1, 3), (3, 1)])]
    pallas_call x6 -> x7, Pallas kernels: 119 us -> 112 us  [call(): pl.pallas_call(kernel, grid_spec=pltpu.PrefetchScalarGridSpec(num_scalar_...]
    ppermute x11, waiting for transfers between devices: 6.42 us -> 11.9 us  [over_x(): return lax.ppermute(z, 'tensor', [(0, 1), (1, 0), (2, 3), (3, 2)])]
    concatenate x1 -> x0, local copies, waits for them, and re-layouts: 3.42 us -> none  [per_device(): flat = jnp.concatenate([z.reshape(-1) for z in small])]
  transfers between devices with their start and end apart: 29 -> 29, of which waited for: 13 -> 14; matrix products, arithmetic and copies ran while one was open for 15% -> 12% of each run, Pallas kernels for 43% -> 42%
where the time goes in v3:
time: 247 us; the launch traced here: 246 us
  Pallas kernels  112 us (45%)
  waiting for transfers between devices  37.2 us (15%)
  starting transfers between devices  28.8 us (12%)
  other arithmetic  22.2 us (9%)
  local copies, waits for them, and re-layouts  17 us (7%)
  between operations  14.9 us (6%)
  blocking collectives  14 us (6%)
    pallas_call x7, Pallas kernels, call(): pl.pallas_call(kernel, grid_spec=pltpu.PrefetchScalarGridSpec(num_scalar_...  112 us
    ppermute x11, waiting for transfers between devices, over_y(): return lax.ppermute(z, 'tensor', [(0, 2), (2, 0), (1, 3), (3, 1)])  16.6 us
    all_gather x1, blocking collectives, per_device(): packed = lax.all_gather(packed, 'dp', axis=1, tiled=True)  14 us
    ppermute x11, starting transfers between devices, over_x(): return lax.ppermute(z, 'tensor', [(0, 1), (1, 0), (2, 3), (3, 2)])  13 us
    ppermute x11, waiting for transfers between devices, over_x(): return lax.ppermute(z, 'tensor', [(0, 1), (1, 0), (2, 3), (3, 2)])  11.9 us
    ppermute x11, starting transfers between devices, over_y(): return lax.ppermute(z, 'tensor', [(0, 2), (2, 0), (1, 3), (3, 1)])  11.4 us
    ppermute x3, waiting for transfers between devices, sum_over_dp(): z = z + lax.ppermute(z, 'dp', [(i, i ^ bit) for i in range(count)])  8.56 us
    convert_element_type x4, other arithmetic, scatter_middle(): far = (left_far.astype(bf16), right_far.astype(bf16))  5.25 us
  transfers between devices with their start and end apart: 29, of which 14 were waited for; matrix products, arithmetic and copies ran while one was open for 12% of the time, Pallas kernels for 42%

profile of v3, /device:TPU:0, one launch (start us, length us, event | category | flops | bytes accessed | tf_op | source)
XLA Modules:
  0.0 246.4 jit_solution(8064959981625487430)
XLA Ops:
  7.2 1.1 copy.48
  8.3 1.7 fusion.9
  10.2 3.0 %collective-permute-start = (bf16[512,1024]{1,0:T(8,128)(2,1)}, bf16[512,1024]{1,0:T(8,128)(2,1)S(1)}, u32[]{:S(2)}, u32[]{:S(2)}) collective-permute-start(bf16[512,1024]{1,0:T(8,128)(2,1)} %refs_0_.1), channel_id=1, source_target_pairs={{0,1},{1,0},{2,3},{3,2},{4,5},{5,4},{6,7},{7,6},{8,9},{9,8},{10,11... | collective-permute-start | bytes 3145736 | tf_op jit(solution)/shard_map/ppermute | solution.py:644
  13.2 1.5 collective-permute-start.1
  14.7 0.8 reshape.72
  15.4 0.8 reshape.73
  16.2 0.8 reshape.71
  17.8 0.8 fusion.23
  19.2 14.0 %all_gather.9.packed_ref = bf16[8,1024]{1,0:T(8,128)(2,1)} all-gather(bf16[8,128]{1,0:T(8,128)(2,1)S(1)} %fusion.18), channel_id=1, replica_groups=mesh['dp'=8,'tensor'=4] {'dp'}, dimensions={1}, use_global_device_ids=true | all-gather | bytes 18432 | tf_op jit(solution)/shard_map/all_gather | solution.py:1004
  33.2 3.3 %collective-permute-done.refs_1_ = bf16[512,1024]{1,0:T(8,128)(2,1)S(1)} collective-permute-done((bf16[512,1024]{1,0:T(8,128)(2,1)}, bf16[512,1024]{1,0:T(8,128)(2,1)S(1)}, u32[]{:S(2)}, u32[]{:S(2)}) %collective-permute-start) | collective-permute-done | bytes 1048608 | tf_op jit(solution)/shard_map/ppermute | solution.py:644
  36.5 1.5 collective-permute-done.1.refs_2_
  38.0 0.9 slice.115
  38.9 0.8 slice.116
  39.7 1.5 collective-permute-start.2
  41.9 0.8 copy.49
  42.7 1.3 constant_dynamic-slice_fusion.5
  44.0 2.1 parameter_kernel.1
  46.1 6.5 %collective-permute-done.2.refs_3_ = bf16[512,512]{1,0:T(8,128)(2,1)} collective-permute-done((bf16[512,512]{1,0:T(8,128)(2,1)}, bf16[512,512]{1,0:T(8,128)(2,1)}, u32[]{:S(2)}, u32[]{:S(2)}) %collective-permute-start.2) | collective-permute-done | bytes 524320 | tf_op jit(solution)/shard_map/ppermute | solution.py:648
  52.6 1.3 collective-permute-done.3.refs_4_
  55.9 22.9 %scan_kernel.2 = (bf16[2048,1024]{1,0:T(8,128)(2,1)}, bf16[2048,512]{1,0:T(8,128)(2,1)}, f32[2048,512]{1,0:T(8,128)}, bf16[2048,256]{1,0:T(8,128)(2,1)}, f32[204...) custom-call(s32[1,1]{1,0:T(1,128)S(6)} %copy.63.len_ref, ...), custom_call_target="tpu_custom_call" | custom-call | flops 1000 | bytes 1000 | tf_op jit(solution)/shard_map/scan_kernel/pallas_call | solution.py:733
  78.8 1.1 slice.117
  79.9 1.1 slice.118
  80.9 1.4 collective-permute-start.6
  82.3 1.5 collective-permute-start.7
  83.8 11.1 %scan_kernel.3 = (bf16[2048,1024]{1,0:T(8,128)(2,1)}, bf16[2048,512]{1,0:T(8,128)(2,1)}, f32[2048,512]{1,0:T(8,128)}, bf16[2048,256]{1,0:T(8,128)(2,1)}, f32[204...) custom-call(s32[1,1]{1,0:T(1,128)S(6)} %copy.63.len_ref, ...), custom_call_target="tpu_custom_call", output_to_operand_aliasing={{0}: (18, {}), {1}: (19, {}), {2}: (20, {}), {3}: (21, {}),... | custom-call | flops 1000 | bytes 1000 | tf_op jit(solution)/shard_map/scan_kernel/pallas_call | solution.py:733
  95.0 0.8 copy-done.13
  96.0 8.3 %cotangent_kernel.1 = (bf16[2048,512]{1,0:T(8,128)(2,1)}, f32[8,2048]{1,0:T(8,128)}) custom-call(s32[216]{0:T(256)} %bitcast.31, bf16[512,1024]{1,0:T(8,128)(2,1)} %refs_0_.3, bf16[512,1024]{1,0:T(8,128)(2,1)} %collective-permute-done.4.refs_1_, bf16[512,1024]{1,0:T(8,128)(2,1)} %collective-permute-done.5.refs_2_, bf16[512,512]{1,0:T(8,128)(2,1)} %copy-done.13, ...), custom_call_target="tpu_custom_call" | custom-call | flops 1000 | bytes 1000 | tf_op jit(solution)/shard_map/cotangent_kernel/pallas_call | solution.py:733
  104.8 7.4 %product_kernel.1 = (bf16[1024,512]{1,0:T(8,128)(2,1)}, bf16[1024,512]{1,0:T(8,128)(2,1)}, bf16[1024,512]{1,0:T(8,128)(2,1)}, bf16[1024,512]{1,0:T(8,128)(2,1)}) custom-call(s32[216]{0:T(256)} %bitcast.32, bf16[2048,512]{1,0:T(8,128)(2,1)} %get-tuple-element.170.refs_6_.ga_ref, bf16[1024,512]{1,0:T(8,128)(2,1)} %all-gather.5.cloned.1.call-done.refs_5_.w_ref), custom_call_target="tpu_custom_call" | custom-call | flops 1000 | bytes 1000 | tf_op jit(solution)/shard_map/product_kernel/pallas_call | solution.py:733
  112.2 0.8 collective-permute-start.9
  112.9 1.5 collective-permute-start.10
  114.4 1.4 collective-permute-start.11
  115.8 1.5 collective-permute-done.9
  117.9 17.0 %gate_kernel.1 = (bf16[2048,512]{1,0:T(8,128)(2,1)}, f32[2048,512]{1,0:T(8,128)}, f32[8,512]{1,0:T(8,128)}, bf16[1024,1024]{1,0:T(8,128)(2,1)}, f32[8,1024]{1,0:T(8,128)}) custom-call(s32[216]{0:T(256)} %bitcast.33, bf16[512,1024]{1,0:T(8,128)(2,1)} %refs_0_.3, bf16[512,1024]{1,0:T(8,128)(2,1)} %collective-permute-done.4.refs_1_, ...), custom_call_target="tpu_custom_call" | custom-call | flops 34359738368 | bytes 1000 | tf_op jit(solution)/shard_map/gate_kernel/pallas_call | solution.py:733
  134.9 1.4 collective-permute-done.11
  136.8 1.2 add_convert_fusion.3
  138.0 1.4 collective-permute-start.12
  139.3 0.9 collective-permute-start.13
  140.2 43.6 %backward_kernel.1 = (bf16[1024,512]{1,0:T(8,128)(2,1)}, bf16[1024,512]{1,0:T(8,128)(2,1)}, bf16[1024,512]{1,0:T(8,128)(2,1)}, bf16[1024,512]{1,0:T(8,128)(2,1)}...) custom-call(s32[1,1]{1,0:T(1,128)S(6)} %copy.63.len_ref, ...), custom_call_target="tpu_custom_call" | custom-call | flops 1000 | bytes 1000 | tf_op jit(solution)/shard_map/backward_kernel/pallas_call | solution.py:733
  183.9 1.2 collective-permute-start.17
  186.2 1.2 collective-permute-done.14
  187.5 1.7 collective-permute-start.15
  189.1 3.1 %collective-permute-done.15 = f32[16,1024]{1,0:T(8,128)S(1)} collective-permute-done((f32[16,1024]{1,0:T(8,128)S(1)}, f32[16,1024]{1,0:T(8,128)S(1)}, u32[]{:S(2)}, u32[]{:S(2)}) %collective-permute-start.15) | collective-permute-done | bytes 65568 | tf_op jit(solution)/shard_map/ppermute | solution.py:693
  192.2 2.5 %collective-permute-start.16 = (f32[16,1024]{1,0:T(8,128)S(1)}, f32[16,1024]{1,0:T(8,128)S(1)}, u32[]{:S(2)}, u32[]{:S(2)}) collective-permute-start(f32[16,1024]{1,0:T(8,128)S(1)} %add.146), channel_id=1, source_target_pairs={{0,16},{4,20},{8,24},{12,28},{16,0},{20,4},{24,8},{28,12},{1,17},{... | collective-permute-start | bytes 196616 | tf_op jit(solution)/shard_map/ppermute | solution.py:693
  194.7 1.6 convert_add_fusion.4
  196.4 4.3 %collective-permute-done.16 = f32[16,1024]{1,0:T(8,128)S(1)} collective-permute-done((f32[16,1024]{1,0:T(8,128)S(1)}, f32[16,1024]{1,0:T(8,128)S(1)}, u32[]{:S(2)}, u32[]{:S(2)}) %collective-permute-start.16) | collective-permute-done | bytes 65568 | tf_op jit(solution)/shard_map/ppermute | solution.py:693
  200.7 2.2 collective-permute-done.17
  202.9 1.3 collective-permute-done.18
  204.1 2.0 add_convert_fusion
  206.1 2.0 add_convert_fusion.1
  208.1 0.9 collective-permute-start.19
  209.0 1.1 collective-permute-start.20
  210.8 0.8 copy.50
  211.6 1.6 convert_add_fusion.3
  213.2 1.0 collective-permute-start.21
  215.0 5.1 %collective-permute-done.21 = f32[16,1024]{1,0:T(8,128)S(1)} collective-permute-done((f32[16,1024]{1,0:T(8,128)S(1)}, f32[16,1024]{1,0:T(8,128)S(1)}, u32[]{:S(2)}, u32[]{:S(2)}) %collective-permute-start.21) | collective-permute-done | bytes 65568 | tf_op jit(solution)/shard_map/ppermute | solution.py:644
  221.1 3.3 %collective-permute-done.22 = f32[16,1024]{1,0:T(8,128)S(1)} collective-permute-done((f32[16,1024]{1,0:T(8,128)S(1)}, f32[16,1024]{1,0:T(8,128)S(1)}, u32[]{:S(2)}, u32[]{:S(2)}) %collective-permute-start.22) | collective-permute-done | bytes 65568 | tf_op jit(solution)/shard_map/ppermute | solution.py:648
  224.5 1.0 slice.136
  225.5 1.6 slice_convert_fusion
  228.3 1.1 collective-permute-start.23
  229.4 1.5 convert_add_fusion.1
  231.0 1.4 convert_add_fusion.2
  233.6 0.9 add_convert_fusion.4
  235.8 2.2 fusion.5
  238.0 1.2 collective-permute-done.24
  (102 shorter events, 13.4 us)
Async XLA Ops:
  7.2 34.7 %copy-start.15 = (bf16[512,128]{1,0:T(8,128)(2,1)S(1)}, bf16[512,128]{1,0:T(8,128)(2,1)}, u32[]{:S(2)}) copy-start(bf16[512,128]{1,0:T(8,128)(2,1)} %param.34) | copy-start | bytes 393220
  7.2 46.7 %copy-start.3 = (bf16[512,1024]{1,0:T(8,128)(2,1)S(1)}, bf16[512,1024]{1,0:T(8,128)(2,1)}, u32[]{:S(2)}) copy-start(bf16[512,1024]{1,0:T(8,128)(2,1)} %refs_0_.3) | copy-start | bytes 3145732
  7.2 48.7 %all-gather.3.cloned.1.call-start = ((), (), s32[]{:S(2)}) async-start(), calls=%async_computation.2 | async-start | bytes 3244032 | tf_op jit(solution)/shard_map/all_gather | solution.py:980
  10.1 84.9 %all-gather.5.cloned.1.call-start = ((), (), s32[]{:S(2)}) async-start(), calls=%async_computation.3 | async-start | bytes 1179648 | tf_op jit(solution)/shard_map/all_gather | solution.py:983
  10.2 26.4 %collective-permute-start = (bf16[512,1024]{1,0:T(8,128)(2,1)}, bf16[512,1024]{1,0:T(8,128)(2,1)S(1)}, u32[]{:S(2)}, u32[]{:S(2)}) collective-permute-start(bf16[512,1024]{1,0:T(8,128)(2,1)} %refs_0_.1), channel_id=1, source_target_pairs={{0,1},{1,0},{2,3},{3,2},{4,5},{5,4},{6,7},{7,6},{8,9},{9,8},{10,11... | collective-permute-start | bytes 3145736 | tf_op jit(solution)/shard_map/ppermute | solution.py:644
  13.2 24.8 %collective-permute-start.1 = (bf16[512,1024]{1,0:T(8,128)(2,1)}, bf16[512,1024]{1,0:T(8,128)(2,1)S(1)}, u32[]{:S(2)}, u32[]{:S(2)}) collective-permute-start(bf16[512,1024]{1,0:T(8,128)(2,1)} %refs_0_.1), channel_id=1, source_target_pairs={{0,2},{2,0},{1,3},{3,1},{4,6},{6,4},{5,7},{7,5},{8,10},{10,8},{9,1... | collective-permute-start | bytes 3145736 | tf_op jit(solution)/shard_map/ppermute | solution.py:648
  36.5 19.4 %copy-start.1 = (bf16[512,1024]{1,0:T(8,128)(2,1)}, bf16[512,1024]{1,0:T(8,128)(2,1)S(1)}, u32[]{:S(2)}) copy-start(bf16[512,1024]{1,0:T(8,128)(2,1)S(1)} %collective-permute-done.refs_1_) | copy-start | bytes 3145732
  38.0 17.9 %copy-start.2 = (bf16[512,1024]{1,0:T(8,128)(2,1)}, bf16[512,1024]{1,0:T(8,128)(2,1)S(1)}, u32[]{:S(2)}) copy-start(bf16[512,1024]{1,0:T(8,128)(2,1)S(1)} %collective-permute-done.1.refs_2_) | copy-start | bytes 3145732
  39.7 12.9 %collective-permute-start.2 = (bf16[512,512]{1,0:T(8,128)(2,1)}, bf16[512,512]{1,0:T(8,128)(2,1)}, u32[]{:S(2)}, u32[]{:S(2)}) collective-permute-start(bf16[512,512]{1,0:T(8,128)(2,1)} %slice.115), channel_id=1, source_target_pairs={{0,2},{2,0},{1,3},{3,1},{4,6},{6,4},{5,7},{7,5},{8,10},{10,8},{9,1... | collective-permute-start | bytes 1572872 | tf_op jit(solution)/shard_map/ppermute | solution.py:648
  41.2 12.6 %collective-permute-start.3 = (bf16[512,512]{1,0:T(8,128)(2,1)}, bf16[512,512]{1,0:T(8,128)(2,1)}, u32[]{:S(2)}, u32[]{:S(2)}) collective-permute-start(bf16[512,512]{1,0:T(8,128)(2,1)} %slice.116), channel_id=1, source_target_pairs={{0,1},{1,0},{2,3},{3,2},{4,5},{5,4},{6,7},{7,6},{8,9},{9,8},{10,11... | collective-permute-start | bytes 1572872 | tf_op jit(solution)/shard_map/ppermute | solution.py:644
  42.7 141.2 %reduce-scatter.3.cloned.1.call-start = ((), (), s32[]{:S(2)}) async-start(), calls=%async_computation.4 | async-start | bytes 2359296 | tf_op jit(solution)/shard_map/reduce_scatter | solution.py:1060
  53.9 24.9 %collective-permute-start.4 = (bf16[512,1024]{1,0:T(8,128)(2,1)S(1)}, bf16[512,1024]{1,0:T(8,128)(2,1)}, u32[]{:S(2)}, u32[]{:S(2)}) collective-permute-start(bf16[512,1024]{1,0:T(8,128)(2,1)S(1)} %copy-done.3), channel_id=1, source_target_pairs={{0,1},{1,0},{2,3},{3,2},{4,5},{5,4},{6,7},{7,6},{8,9},{9,8},{10,11... | collective-permute-start | bytes 3145736 | tf_op jit(solution)/shard_map/ppermute | solution.py:644
  54.5 24.3 %collective-permute-start.5 = (bf16[512,1024]{1,0:T(8,128)(2,1)S(1)}, bf16[512,1024]{1,0:T(8,128)(2,1)}, u32[]{:S(2)}, u32[]{:S(2)}) collective-permute-start(bf16[512,1024]{1,0:T(8,128)(2,1)S(1)} %copy-done.3), channel_id=1, source_target_pairs={{0,2},{2,0},{1,3},{3,1},{4,6},{6,4},{5,7},{7,5},{8,10},{10,8},{9,1... | collective-permute-start | bytes 3145736 | tf_op jit(solution)/shard_map/ppermute | solution.py:648
  80.9 14.0 %collective-permute-start.6 = (bf16[512,512]{1,0:T(8,128)(2,1)S(1)}, bf16[512,512]{1,0:T(8,128)(2,1)S(1)}, u32[]{:S(2)}, u32[]{:S(2)}) collective-permute-start(bf16[512,512]{1,0:T(8,128)(2,1)S(1)} %slice.117), channel_id=1, source_target_pairs={{0,2},{2,0},{1,3},{3,1},{4,6},{6,4},{5,7},{7,5},{8,10},{10,8},{9,1... | collective-permute-start | bytes 1572872 | tf_op jit(solution)/shard_map/ppermute | solution.py:648
  82.3 12.7 %collective-permute-start.7 = (bf16[512,512]{1,0:T(8,128)(2,1)S(1)}, bf16[512,512]{1,0:T(8,128)(2,1)S(1)}, u32[]{:S(2)}, u32[]{:S(2)}) collective-permute-start(bf16[512,512]{1,0:T(8,128)(2,1)S(1)} %slice.118), channel_id=1, source_target_pairs={{0,1},{1,0},{2,3},{3,2},{4,5},{5,4},{6,7},{7,6},{8,9},{9,8},{10,11... | collective-permute-start | bytes 1572872 | tf_op jit(solution)/shard_map/ppermute | solution.py:644
  95.0 0.8 copy-start.13
  95.0 0.9 copy-start.14
  104.3 7.9 %copy-start.18 = (f32[8,2048]{1,0:T(8,128)S(1)}, f32[8,2048]{1,0:T(8,128)}, u32[]{:S(2)}) copy-start(f32[8,2048]{1,0:T(8,128)} %get-tuple-element.168) | copy-start | bytes 196612
  104.3 7.9 %collective-permute-start.8 = (f32[8,2048]{1,0:T(8,128)}, f32[8,2048]{1,0:T(8,128)S(1)}, u32[]{:S(2)}, u32[]{:S(2)}) collective-permute-start(f32[8,2048]{1,0:T(8,128)} %get-tuple-element.168), channel_id=1, source_target_pairs={{0,1},{1,0},{2,3},{3,2},{4,5},{5,4},{6,7},{7,6},{8,9},{9,8},{10,11... | collective-permute-start | bytes 196616 | tf_op jit(solution)/shard_map/ppermute | solution.py:644
  112.2 5.1 %collective-permute-start.9 = (f32[8,2048]{1,0:T(8,128)S(1)}, f32[8,2048]{1,0:T(8,128)S(1)}, u32[]{:S(2)}, u32[]{:S(2)}) collective-permute-start(f32[8,2048]{1,0:T(8,128)S(1)} %add.131), channel_id=1, source_target_pairs={{0,2},{2,0},{1,3},{3,1},{4,6},{6,4},{5,7},{7,5},{8,10},{10,8},{9,1... | collective-permute-start | bytes 196616 | tf_op jit(solution)/shard_map/ppermute | solution.py:648
  112.9 22.0 %collective-permute-start.10 = (bf16[1024,512]{1,0:T(8,128)(2,1)}, bf16[1024,512]{1,0:T(8,128)(2,1)S(1)}, u32[]{:S(2)}, u32[]{:S(2)}) collective-permute-start(bf16[1024,512]{1,0:T(8,128)(2,1)} %get-tuple-element.186), channel_id=1, source_target_pairs={{0,1},{1,0},{2,3},{3,2},{4,5},{5,4},{6,7},{7,6},{8,9},{9,8},{10,11... | collective-permute-start | bytes 3145736 | tf_op jit(solution)/shard_map/ppermute | solution.py:644
  114.4 21.9 %collective-permute-start.11 = (bf16[1024,512]{1,0:T(8,128)(2,1)}, bf16[1024,512]{1,0:T(8,128)(2,1)S(1)}, u32[]{:S(2)}, u32[]{:S(2)}) collective-permute-start(bf16[1024,512]{1,0:T(8,128)(2,1)} %get-tuple-element.187), channel_id=1, source_target_pairs={{0,2},{2,0},{1,3},{3,1},{4,6},{6,4},{5,7},{7,5},{8,10},{10,8},{9,1... | collective-permute-start | bytes 3145736 | tf_op jit(solution)/shard_map/ppermute | solution.py:648
  134.9 1.6 copy-start.5
  134.9 1.9 copy-start.10
  134.9 1.4 copy-start.11
  136.3 1.7 copy-start.9
  136.3 88.2 %reduce-scatter.5.cloned.1.call-start = ((), (), s32[]{:S(2)}) async-start(), calls=%async_computation.5 | async-start | bytes 2064384 | tf_op jit(solution)/shard_map/reduce_scatter | solution.py:1082
  138.0 45.8 %collective-permute-start.12 = (bf16[512,512]{1,0:T(8,128)(2,1)S(1)}, bf16[512,512]{1,0:T(8,128)(2,1)}, u32[]{:S(2)}, u32[]{:S(2)}) collective-permute-start(bf16[512,512]{1,0:T(8,128)(2,1)S(1)} %add_convert_fusion.3), channel_id=1, source_target_pairs={{0,2},{2,0},{1,3},{3,1},{4,6},{6,4},{5,7},{7,5},{8,10},{10,8},{9,1... | collective-permute-start | bytes 1572872 | tf_op jit(solution)/shard_map/ppermute | solution.py:648
  139.3 44.5 %collective-permute-start.13 = (bf16[512,512]{1,0:T(8,128)(2,1)S(1)}, bf16[512,512]{1,0:T(8,128)(2,1)}, u32[]{:S(2)}, u32[]{:S(2)}) collective-permute-start(bf16[512,512]{1,0:T(8,128)(2,1)S(1)} %add_convert_fusion.2), channel_id=1, source_target_pairs={{0,1},{1,0},{2,3},{3,2},{4,5},{5,4},{6,7},{7,6},{8,9},{9,8},{10,11... | collective-permute-start | bytes 1572872 | tf_op jit(solution)/shard_map/ppermute | solution.py:644
  183.8 2.0 copy-start
  183.8 2.3 copy-start.17
  183.8 5.3 %slice-start = ((f32[8,2048]{1,0:T(8,128)}), f32[1,2048]{1,0:T(1,128)S(1)}, s32[]{:S(2)}) async-start(f32[8,2048]{1,0:T(8,128)} %add.132.refs_5_), calls=%async_computation.6 | async-start | bytes 16384 | tf_op jit(solution)/shard_map/slice | solution.py:1103
  183.9 12.4 %copy-start.12 = (bf16[128,1024]{1,0:T(8,128)(2,1)S(1)}, bf16[128,1024]{1,0:T(8,128)(2,1)}, u32[]{:S(2)}) copy-start(bf16[128,1024]{1,0:T(8,128)(2,1)} %reduce-scatter.3.cloned.1.call-done) | copy-start | bytes 786436
  183.9 19.0 %collective-permute-start.17 = (bf16[1024,512]{1,0:T(8,128)(2,1)}, bf16[1024,512]{1,0:T(8,128)(2,1)}, u32[]{:S(2)}, u32[]{:S(2)}) collective-permute-start(bf16[1024,512]{1,0:T(8,128)(2,1)} %get-tuple-element.215), channel_id=1, source_target_pairs={{0,1},{1,0},{2,3},{3,2},{4,5},{5,4},{6,7},{7,6},{8,9},{9,8},{10,11... | collective-permute-start | bytes 3145736 | tf_op jit(solution)/shard_map/ppermute | solution.py:644
  185.1 19.0 %collective-permute-start.18 = (bf16[1024,512]{1,0:T(8,128)(2,1)}, bf16[1024,512]{1,0:T(8,128)(2,1)}, u32[]{:S(2)}, u32[]{:S(2)}) collective-permute-start(bf16[1024,512]{1,0:T(8,128)(2,1)} %get-tuple-element.216), channel_id=1, source_target_pairs={{0,2},{2,0},{1,3},{3,1},{4,6},{6,4},{5,7},{7,5},{8,10},{10,8},{9,1... | collective-permute-start | bytes 3145736 | tf_op jit(solution)/shard_map/ppermute | solution.py:648
  186.1 18.0 %copy-start.8 = (bf16[1024,512]{1,0:T(8,128)(2,1)S(1)}, bf16[1024,512]{1,0:T(8,128)(2,1)}, u32[]{:S(2)}) copy-start(bf16[1024,512]{1,0:T(8,128)(2,1)} %get-tuple-element.218) | copy-start | bytes 3145732
  186.1 1.3 collective-permute-start.14
  187.5 4.7 %collective-permute-start.15 = (f32[16,1024]{1,0:T(8,128)S(1)}, f32[16,1024]{1,0:T(8,128)S(1)}, u32[]{:S(2)}, u32[]{:S(2)}) collective-permute-start(f32[16,1024]{1,0:T(8,128)S(1)} %add.145), channel_id=1, source_target_pairs={{0,8},{4,12},{8,0},{12,4},{16,24},{20,28},{24,16},{28,20},{1,9},{5... | collective-permute-start | bytes 196616 | tf_op jit(solution)/shard_map/ppermute | solution.py:693
  192.2 13.9 %copy-start.6 = (bf16[1024,512]{1,0:T(8,128)(2,1)S(1)}, bf16[1024,512]{1,0:T(8,128)(2,1)}, u32[]{:S(2)}) copy-start(bf16[1024,512]{1,0:T(8,128)(2,1)} %get-tuple-element.213) | copy-start | bytes 3145732
  192.2 8.4 %collective-permute-start.16 = (f32[16,1024]{1,0:T(8,128)S(1)}, f32[16,1024]{1,0:T(8,128)S(1)}, u32[]{:S(2)}, u32[]{:S(2)}) collective-permute-start(f32[16,1024]{1,0:T(8,128)S(1)} %add.146), channel_id=1, source_target_pairs={{0,16},{4,20},{8,24},{12,28},{16,0},{20,4},{24,8},{28,12},{1,17},{... | collective-permute-start | bytes 196616 | tf_op jit(solution)/shard_map/ppermute | solution.py:693
  208.1 16.4 %collective-permute-start.19 = (bf16[512,512]{1,0:T(8,128)(2,1)}, bf16[512,512]{1,0:T(8,128)(2,1)}, u32[]{:S(2)}, u32[]{:S(2)}) collective-permute-start(bf16[512,512]{1,0:T(8,128)(2,1)} %add_convert_fusion.1), channel_id=1, source_target_pairs={{0,2},{2,0},{1,3},{3,1},{4,6},{6,4},{5,7},{7,5},{8,10},{10,8},{9,1... | collective-permute-start | bytes 1572872 | tf_op jit(solution)/shard_map/ppermute | solution.py:648
  209.0 15.5 %collective-permute-start.20 = (bf16[512,512]{1,0:T(8,128)(2,1)}, bf16[512,512]{1,0:T(8,128)(2,1)}, u32[]{:S(2)}, u32[]{:S(2)}) collective-permute-start(bf16[512,512]{1,0:T(8,128)(2,1)} %add_convert_fusion), channel_id=1, source_target_pairs={{0,1},{1,0},{2,3},{3,2},{4,5},{5,4},{6,7},{7,6},{8,9},{9,8},{10,11... | collective-permute-start | bytes 1572872 | tf_op jit(solution)/shard_map/ppermute | solution.py:644
  213.2 6.9 %collective-permute-start.21 = (f32[16,1024]{1,0:T(8,128)S(1)}, f32[16,1024]{1,0:T(8,128)S(1)}, u32[]{:S(2)}, u32[]{:S(2)}) collective-permute-start(f32[16,1024]{1,0:T(8,128)S(1)} %add.147), channel_id=1, source_target_pairs={{0,1},{1,0},{2,3},{3,2},{4,5},{5,4},{6,7},{7,6},{8,9},{9,8},{10,11... | collective-permute-start | bytes 196616 | tf_op jit(solution)/shard_map/ppermute | solution.py:644
  220.1 4.3 %collective-permute-start.22 = (f32[16,1024]{1,0:T(8,128)S(1)}, f32[16,1024]{1,0:T(8,128)S(1)}, u32[]{:S(2)}, u32[]{:S(2)}) collective-permute-start(f32[16,1024]{1,0:T(8,128)S(1)} %add.151), channel_id=1, source_target_pairs={{0,2},{2,0},{1,3},{3,1},{4,6},{6,4},{5,7},{7,5},{8,10},{10,8},{9,1... | collective-permute-start | bytes 196616 | tf_op jit(solution)/shard_map/ppermute | solution.py:648
  224.5 6.5 %copy-start.7 = (bf16[1024,512]{1,0:T(8,128)(2,1)S(1)}, bf16[1024,512]{1,0:T(8,128)(2,1)}, u32[]{:S(2)}) copy-start(bf16[1024,512]{1,0:T(8,128)(2,1)} %get-tuple-element.213) | copy-start | bytes 3145732
  228.3 5.3 %collective-permute-start.23 = (bf16[128,384]{1,0:T(8,128)(2,1)S(1)}, bf16[128,384]{1,0:T(8,128)(2,1)S(1)}, u32[]{:S(2)}, u32[]{:S(2)}) collective-permute-start(bf16[128,384]{1,0:T(8,128)(2,1)S(1)} %slice.136), channel_id=1, source_target_pairs={{0,1},{1,0},{2,3},{3,2},{4,5},{5,4},{6,7},{7,6},{8,9},{9,8},{10,11... | collective-permute-start | bytes 294920 | tf_op jit(solution)/shard_map/ppermute | solution.py:644
  231.0 4.3 %copy-start.16 = (f32[1,1024]{1,0:T(1,128)S(1)}, f32[1,1024]{1,0:T(1,128)}, u32[]{:S(2)}) copy-start(f32[1,1024]{1,0:T(1,128)} %get-tuple-element.137.refs_6_.refs_1_) | copy-start | bytes 12292
  232.4 3.4 %copy-start.4 = (bf16[512,1024]{1,0:T(8,128)(2,1)S(1)}, bf16[512,1024]{1,0:T(8,128)(2,1)}, u32[]{:S(2)}) copy-start(bf16[512,1024]{1,0:T(8,128)(2,1)} %refs_0_.3) | copy-start | bytes 3145732
  234.5 4.7 %collective-permute-start.24 = (bf16[128,384]{1,0:T(8,128)(2,1)S(1)}, bf16[128,384]{1,0:T(8,128)(2,1)S(1)}, u32[]{:S(2)}, u32[]{:S(2)}) collective-permute-start(bf16[128,384]{1,0:T(8,128)(2,1)S(1)} %add_convert_fusion.4), channel_id=1, source_target_pairs={{0,2},{2,0},{1,3},{3,1},{4,6},{6,4},{5,7},{7,5},{8,10},{10,8},{9,1... | collective-permute-start | bytes 294920 | tf_op jit(solution)/shard_map/ppermute | solution.py:648
Sparse Core Ops, SparseCore 0:
  10.2 38.9 all-gather.2
  51.4 20.9 all-gather.4
  136.5 35.8 reduce-scatter.2
  184.0 34.9 reduce-scatter.4

commit v4 on v3

--- a/solution.py
+++ b/solution.py
@@ -15,7 +15,7 @@
 ROWS = 256
 WIDE_ROWS = 512
 FIELD = 32
-PARAMS = 8
+PARAMS = 16
 SUB = 128
 EPS = 1e-05
 LOG2E = 1.4426950408889634
@@ -315,6 +315,7 @@
 ):
     packed = packed_ref[...]
     total = packed.shape[1]
+    rows = prm_ref.shape[0]
     source = lax.broadcasted_iota(jnp.int32, (total, 1), 0)
     maps_at = heads_here * cut
 
@@ -323,7 +324,7 @@
 
     def moved(columns, lane_of):
         lane = lane_of(lax.broadcasted_iota(jnp.int32, (1, columns), 1))
-        return nn(packed, jnp.where(source == lane, 1.0, 0.0).astype(bf16))
+        return nn(packed, jnp.where(source == lane, 1.0, 0.0).astype(bf16))[:rows]
 
     def by_channel(c):
         head, inside = split(c, HEADDIM)
@@ -342,7 +343,7 @@
         return lambda h: jnp.where(h < heads_here, part(first_ref[0] + h), -1)
 
     channels = prm_ref.shape[1]
-    row = lax.broadcasted_iota(jnp.int32, (PARAMS, 1), 0)
+    row = lax.broadcasted_iota(jnp.int32, (rows, 1), 0)
     by_head = moved(channels, by_channel)
     skip = by_part(head_cut, maps_at + 2 * head_cut)
     skips = moved(channels, lambda c: skip(first_ref[0] + split(c, HEADDIM)[0]))
@@ -794,7 +795,7 @@
         ]
 
     def parameters(self, packed, cut, state_cut, head_cut, depth):
-        shapes = ((PARAMS, self.channels), (PARAMS, 2 * STATE), (PARAMS, LANES), (1, self.width))
+        shapes = ((8, self.channels), (8, 2 * STATE), (8, LANES), (1, self.width))
         return self.call(
             functools.partial(
                 parameter_kernel,
@@ -1082,12 +1083,15 @@
     own_last = lax.psum_scatter(grad_last, "dp", scatter_dimension=0, tiled=True)
     small_sum = sum_over_dp(small_sum)
     if square_mesh:
-        small_sum, moving = lax.optimization_barrier((small_sum, moving))
-        far, small_sum = scatter_middle(gn_halves, *moving, small_sum)
-    small_shared = sum_over_tensor(small_sum) if square_mesh else lax.psum(small_sum, "tensor")
+        small_x = small_sum + over_x(small_sum)
+        small_x, moving = lax.optimization_barrier((small_x, moving))
+        small_shared = small_x + over_y(small_x)
+        far, small_shared = scatter_middle(gn_halves, *moving, small_shared)
+    else:
+        small_shared = lax.psum(small_sum, "tensor")
 
     if square_mesh:
-        far, own_last, small_shared = lax.optimization_barrier((far, own_last, small_shared))
+        far, own_last = lax.optimization_barrier((far, own_last))
         own_state = own_last[:, channels:].astype(f32)
         own_state = (own_state + over_x(own_last[:, channels:]).astype(f32)).astype(bf16)
         grad_normed = scatter_end(gn_halves, *moving, *far)

time: 247 us -> 243 us (0.984)
  waiting for transfers between devices: 37.2 us -> 32.5 us
  other arithmetic: 22.2 us -> 18.8 us
  starting transfers between devices: 28.8 us -> 31.5 us
    ppermute x11, waiting for transfers between devices: 11.9 us -> 6.28 us  [over_x(): return lax.ppermute(z, 'tensor', [(0, 1), (1, 0), (2, 3), (3, 2)])]
    ppermute x11, waiting for transfers between devices: 16.6 us -> 20 us  [over_y(): return lax.ppermute(z, 'tensor', [(0, 2), (2, 0), (1, 3), (3, 1)])]
  transfers between devices with their start and end apart: 29 -> 29, of which waited for: 14 -> 13; matrix products, arithmetic and copies ran while one was open for 12% -> 12% of each run, Pallas kernels for 42% -> 43%
where the time goes in v4:
time: 243 us; the launch traced here: 242 us
  Pallas kernels  112 us (46%)
  waiting for transfers between devices  32.5 us (13%)
  starting transfers between devices  31.5 us (13%)
  other arithmetic  18.8 us (8%)
  local copies, waits for them, and re-layouts  18.1 us (7%)
  between operations  14.9 us (6%)
  blocking collectives  14.1 us (6%)
    pallas_call x7, Pallas kernels, call(): pl.pallas_call(kernel, grid_spec=pltpu.PrefetchScalarGridSpec(num_scalar_...  112 us
    ppermute x11, waiting for transfers between devices, over_y(): return lax.ppermute(z, 'tensor', [(0, 2), (2, 0), (1, 3), (3, 1)])  20 us
    all_gather x1, blocking collectives, per_device(): packed = lax.all_gather(packed, 'dp', axis=1, tiled=True)  14.1 us
    ppermute x11, starting transfers between devices, over_x(): return lax.ppermute(z, 'tensor', [(0, 1), (1, 0), (2, 3), (3, 2)])  13.9 us
    ppermute x11, starting transfers between devices, over_y(): return lax.ppermute(z, 'tensor', [(0, 2), (2, 0), (1, 3), (3, 1)])  12.4 us
    ppermute x11, waiting for transfers between devices, over_x(): return lax.ppermute(z, 'tensor', [(0, 1), (1, 0), (2, 3), (3, 2)])  6.28 us
    ppermute x3, waiting for transfers between devices, sum_over_dp(): z = z + lax.ppermute(z, 'dp', [(i, i ^ bit) for i in range(count)])  6.09 us
    unnamed x41, local copies, waits for them, and re-layouts  5.09 us
  transfers between devices with their start and end apart: 29, of which 13 were waited for; matrix products, arithmetic and copies ran while one was open for 12% of the time, Pallas kernels for 43%

profile of v4, /device:TPU:0, one launch (start us, length us, event | category | flops | bytes accessed | tf_op | source)
XLA Modules:
  0.0 242.3 jit_solution(1178456961256425705)
XLA Ops:
  7.2 1.1 copy.48
  8.3 1.8 fusion.9
  10.2 3.0 %collective-permute-start = (bf16[512,1024]{1,0:T(8,128)(2,1)}, bf16[512,1024]{1,0:T(8,128)(2,1)S(1)}, u32[]{:S(2)}, u32[]{:S(2)}) collective-permute-start(bf16[512,1024]{1,0:T(8,128)(2,1)} %refs_0_.1), channel_id=1, source_target_pairs={{0,1},{1,0},{2,3},{3,2},{4,5},{5,4},{6,7},{7,6},{8,9},{9,8},{10,11... | collective-permute-start | bytes 3145736 | tf_op jit(solution)/shard_map/ppermute | solution.py:645
  13.2 1.5 collective-permute-start.1
  14.7 0.8 reshape.72
  15.5 0.8 reshape.73
  16.2 0.8 reshape.71
  17.0 0.8 fusion.22
  17.8 0.8 fusion.23
  19.2 14.1 %all_gather.9.packed_ref = bf16[16,1024]{1,0:T(8,128)(2,1)} all-gather(bf16[16,128]{1,0:T(8,128)(2,1)S(1)} %fusion.16), channel_id=1, replica_groups=mesh['dp'=8,'tensor'=4] {'dp'}, dimensions={1}, use_global_device_ids=true | all-gather | bytes 36864 | tf_op jit(solution)/shard_map/all_gather | solution.py:1005
  33.3 3.2 %collective-permute-done.refs_1_ = bf16[512,1024]{1,0:T(8,128)(2,1)S(1)} collective-permute-done((bf16[512,1024]{1,0:T(8,128)(2,1)}, bf16[512,1024]{1,0:T(8,128)(2,1)S(1)}, u32[]{:S(2)}, u32[]{:S(2)}) %collective-permute-start) | collective-permute-done | bytes 1048608 | tf_op jit(solution)/shard_map/ppermute | solution.py:645
  36.5 1.5 collective-permute-done.1.refs_2_
  38.0 0.9 slice.115
  38.9 0.8 slice.116
  39.7 1.5 collective-permute-start.2
  41.9 0.8 copy.49
  42.7 1.3 constant_dynamic-slice_fusion.5
  44.0 2.2 parameter_kernel.1
  46.2 6.5 %collective-permute-done.2.refs_3_ = bf16[512,512]{1,0:T(8,128)(2,1)} collective-permute-done((bf16[512,512]{1,0:T(8,128)(2,1)}, bf16[512,512]{1,0:T(8,128)(2,1)}, u32[]{:S(2)}, u32[]{:S(2)}) %collective-permute-start.2) | collective-permute-done | bytes 524320 | tf_op jit(solution)/shard_map/ppermute | solution.py:649
  52.6 1.3 collective-permute-done.3.refs_4_
  55.9 22.9 %scan_kernel.2 = (bf16[2048,1024]{1,0:T(8,128)(2,1)}, bf16[2048,512]{1,0:T(8,128)(2,1)}, f32[2048,512]{1,0:T(8,128)}, bf16[2048,256]{1,0:T(8,128)(2,1)}, f32[204...) custom-call(s32[1,1]{1,0:T(1,128)S(6)} %copy.63.len_ref, ...), custom_call_target="tpu_custom_call" | custom-call | flops 1000 | bytes 1000 | tf_op jit(solution)/shard_map/scan_kernel/pallas_call | solution.py:734
  78.8 1.1 slice.117
  79.9 1.1 slice.118
  81.0 1.4 collective-permute-start.6
  82.4 1.5 collective-permute-start.7
  83.9 11.1 %scan_kernel.3 = (bf16[2048,1024]{1,0:T(8,128)(2,1)}, bf16[2048,512]{1,0:T(8,128)(2,1)}, f32[2048,512]{1,0:T(8,128)}, bf16[2048,256]{1,0:T(8,128)(2,1)}, f32[204...) custom-call(s32[1,1]{1,0:T(1,128)S(6)} %copy.63.len_ref, ...), custom_call_target="tpu_custom_call", output_to_operand_aliasing={{0}: (18, {}), {1}: (19, {}), {2}: (20, {}), {3}: (21, {}),... | custom-call | flops 1000 | bytes 1000 | tf_op jit(solution)/shard_map/scan_kernel/pallas_call | solution.py:734
  95.1 0.8 copy-done.12
  96.0 8.3 %cotangent_kernel.1 = (bf16[2048,512]{1,0:T(8,128)(2,1)}, f32[8,2048]{1,0:T(8,128)}) custom-call(s32[216]{0:T(256)} %bitcast.31, bf16[512,1024]{1,0:T(8,128)(2,1)} %refs_0_.3, bf16[512,1024]{1,0:T(8,128)(2,1)} %collective-permute-done.4.refs_1_, bf16[512,1024]{1,0:T(8,128)(2,1)} %collective-permute-done.5.refs_2_, bf16[512,512]{1,0:T(8,128)(2,1)} %copy-done.12, ...), custom_call_target="tpu_custom_call" | custom-call | flops 1000 | bytes 1000 | tf_op jit(solution)/shard_map/cotangent_kernel/pallas_call | solution.py:734
  104.8 7.4 %product_kernel.1 = (bf16[1024,512]{1,0:T(8,128)(2,1)}, bf16[1024,512]{1,0:T(8,128)(2,1)}, bf16[1024,512]{1,0:T(8,128)(2,1)}, bf16[1024,512]{1,0:T(8,128)(2,1)}) custom-call(s32[216]{0:T(256)} %bitcast.32, bf16[2048,512]{1,0:T(8,128)(2,1)} %get-tuple-element.169.refs_6_.ga_ref, bf16[1024,512]{1,0:T(8,128)(2,1)} %all-gather.5.cloned.1.call-done.refs_5_.w_ref), custom_call_target="tpu_custom_call" | custom-call | flops 1000 | bytes 1000 | tf_op jit(solution)/shard_map/product_kernel/pallas_call | solution.py:734
  112.2 0.8 collective-permute-start.9
  113.0 1.5 collective-permute-start.10
  114.4 1.4 collective-permute-start.11
  115.8 1.5 collective-permute-done.9
  117.9 17.0 %gate_kernel.1 = (bf16[2048,512]{1,0:T(8,128)(2,1)}, f32[2048,512]{1,0:T(8,128)}, f32[8,512]{1,0:T(8,128)}, bf16[1024,1024]{1,0:T(8,128)(2,1)}, f32[8,1024]{1,0:T(8,128)}) custom-call(s32[216]{0:T(256)} %bitcast.33, bf16[512,1024]{1,0:T(8,128)(2,1)} %refs_0_.3, bf16[512,1024]{1,0:T(8,128)(2,1)} %collective-permute-done.4.refs_1_, ...), custom_call_target="tpu_custom_call" | custom-call | flops 34359738368 | bytes 1000 | tf_op jit(solution)/shard_map/gate_kernel/pallas_call | solution.py:734
  135.0 1.4 collective-permute-done.11
  136.8 1.2 add_convert_fusion.3
  138.0 1.3 collective-permute-start.12
  139.4 0.9 collective-permute-start.13
  140.2 43.6 %backward_kernel.1 = (bf16[1024,512]{1,0:T(8,128)(2,1)}, bf16[1024,512]{1,0:T(8,128)(2,1)}, bf16[1024,512]{1,0:T(8,128)(2,1)}, bf16[1024,512]{1,0:T(8,128)(2,1)}...) custom-call(s32[1,1]{1,0:T(1,128)S(6)} %copy.63.len_ref, ...), custom_call_target="tpu_custom_call" | custom-call | flops 1000 | bytes 1000 | tf_op jit(solution)/shard_map/backward_kernel/pallas_call | solution.py:734
  183.9 1.1 copy-done
  185.3 1.2 collective-permute-start.18
  187.4 1.4 convert_add_fusion.4
  188.8 1.7 collective-permute-start.15
  190.5 1.6 convert_add_fusion.3
  192.1 1.9 collective-permute-done.15
  194.0 3.3 %collective-permute-start.16 = (f32[16,1024]{1,0:T(8,128)S(1)}, f32[16,1024]{1,0:T(8,128)S(1)}, u32[]{:S(2)}, u32[]{:S(2)}) collective-permute-start(f32[16,1024]{1,0:T(8,128)S(1)} %add.146), channel_id=1, source_target_pairs={{0,16},{4,20},{8,24},{12,28},{16,0},{20,4},{24,8},{28,12},{1,17},{... | collective-permute-start | bytes 196616 | tf_op jit(solution)/shard_map/ppermute | solution.py:694
  198.1 0.8 copy.50
  198.9 4.2 %collective-permute-done.16 = f32[16,1024]{1,0:T(8,128)S(1)} collective-permute-done((f32[16,1024]{1,0:T(8,128)S(1)}, f32[16,1024]{1,0:T(8,128)S(1)}, u32[]{:S(2)}, u32[]{:S(2)}) %collective-permute-start.16) | collective-permute-done | bytes 65568 | tf_op jit(solution)/shard_map/ppermute | solution.py:694
  203.1 1.6 collective-permute-start.17
  206.1 1.3 collective-permute-done.17
  207.4 0.9 collective-permute-start.20
  208.3 1.3 add_convert_fusion
  209.7 1.2 add_convert_fusion.1
  210.8 0.9 collective-permute-done.20
  211.8 0.9 collective-permute-start.21
  212.7 1.2 collective-permute-start.22
  216.2 7.7 %collective-permute-done.21 = bf16[512,512]{1,0:T(8,128)(2,1)} collective-permute-done((bf16[512,512]{1,0:T(8,128)(2,1)S(1)}, bf16[512,512]{1,0:T(8,128)(2,1)}, u32[]{:S(2)}, u32[]{:S(2)}) %collective-permute-start.21) | collective-permute-done | bytes 524320 | tf_op jit(solution)/shard_map/ppermute | solution.py:649
  224.4 1.0 slice.136
  225.4 1.3 collective-permute-start.23
  226.7 1.5 convert_add_fusion.1
  228.3 1.4 convert_add_fusion.2
  229.7 0.7 slice_convert_fusion
  230.5 1.3 collective-permute-start.24
  232.3 2.2 fusion.5
  (102 shorter events, 12.8 us)
Async XLA Ops:
  7.2 34.7 %copy-start.15 = (bf16[512,128]{1,0:T(8,128)(2,1)S(1)}, bf16[512,128]{1,0:T(8,128)(2,1)}, u32[]{:S(2)}) copy-start(bf16[512,128]{1,0:T(8,128)(2,1)} %param.34) | copy-start | bytes 393220
  7.2 46.7 %copy-start.3 = (bf16[512,1024]{1,0:T(8,128)(2,1)S(1)}, bf16[512,1024]{1,0:T(8,128)(2,1)}, u32[]{:S(2)}) copy-start(bf16[512,1024]{1,0:T(8,128)(2,1)} %refs_0_.3) | copy-start | bytes 3145732
  7.2 48.7 %all-gather.3.cloned.1.call-start = ((), (), s32[]{:S(2)}) async-start(), calls=%async_computation.2 | async-start | bytes 3244032 | tf_op jit(solution)/shard_map/all_gather | solution.py:981
  10.1 84.9 %all-gather.5.cloned.1.call-start = ((), (), s32[]{:S(2)}) async-start(), calls=%async_computation.3 | async-start | bytes 1179648 | tf_op jit(solution)/shard_map/all_gather | solution.py:984
  10.2 26.4 %collective-permute-start = (bf16[512,1024]{1,0:T(8,128)(2,1)}, bf16[512,1024]{1,0:T(8,128)(2,1)S(1)}, u32[]{:S(2)}, u32[]{:S(2)}) collective-permute-start(bf16[512,1024]{1,0:T(8,128)(2,1)} %refs_0_.1), channel_id=1, source_target_pairs={{0,1},{1,0},{2,3},{3,2},{4,5},{5,4},{6,7},{7,6},{8,9},{9,8},{10,11... | collective-permute-start | bytes 3145736 | tf_op jit(solution)/shard_map/ppermute | solution.py:645
  13.2 24.8 %collective-permute-start.1 = (bf16[512,1024]{1,0:T(8,128)(2,1)}, bf16[512,1024]{1,0:T(8,128)(2,1)S(1)}, u32[]{:S(2)}, u32[]{:S(2)}) collective-permute-start(bf16[512,1024]{1,0:T(8,128)(2,1)} %refs_0_.1), channel_id=1, source_target_pairs={{0,2},{2,0},{1,3},{3,1},{4,6},{6,4},{5,7},{7,5},{8,10},{10,8},{9,1... | collective-permute-start | bytes 3145736 | tf_op jit(solution)/shard_map/ppermute | solution.py:649
  36.5 19.4 %copy-start.1 = (bf16[512,1024]{1,0:T(8,128)(2,1)}, bf16[512,1024]{1,0:T(8,128)(2,1)S(1)}, u32[]{:S(2)}) copy-start(bf16[512,1024]{1,0:T(8,128)(2,1)S(1)} %collective-permute-done.refs_1_) | copy-start | bytes 3145732
  38.0 17.9 %copy-start.2 = (bf16[512,1024]{1,0:T(8,128)(2,1)}, bf16[512,1024]{1,0:T(8,128)(2,1)S(1)}, u32[]{:S(2)}) copy-start(bf16[512,1024]{1,0:T(8,128)(2,1)S(1)} %collective-permute-done.1.refs_2_) | copy-start | bytes 3145732
  39.7 12.9 %collective-permute-start.2 = (bf16[512,512]{1,0:T(8,128)(2,1)}, bf16[512,512]{1,0:T(8,128)(2,1)}, u32[]{:S(2)}, u32[]{:S(2)}) collective-permute-start(bf16[512,512]{1,0:T(8,128)(2,1)} %slice.115), channel_id=1, source_target_pairs={{0,2},{2,0},{1,3},{3,1},{4,6},{6,4},{5,7},{7,5},{8,10},{10,8},{9,1... | collective-permute-start | bytes 1572872 | tf_op jit(solution)/shard_map/ppermute | solution.py:649
  41.3 12.6 %collective-permute-start.3 = (bf16[512,512]{1,0:T(8,128)(2,1)}, bf16[512,512]{1,0:T(8,128)(2,1)}, u32[]{:S(2)}, u32[]{:S(2)}) collective-permute-start(bf16[512,512]{1,0:T(8,128)(2,1)} %slice.116), channel_id=1, source_target_pairs={{0,1},{1,0},{2,3},{3,2},{4,5},{5,4},{6,7},{7,6},{8,9},{9,8},{10,11... | collective-permute-start | bytes 1572872 | tf_op jit(solution)/shard_map/ppermute | solution.py:645
  42.7 141.2 %reduce-scatter.3.cloned.1.call-start = ((), (), s32[]{:S(2)}) async-start(), calls=%async_computation.4 | async-start | bytes 2359296 | tf_op jit(solution)/shard_map/reduce_scatter | solution.py:1061
  53.9 24.9 %collective-permute-start.4 = (bf16[512,1024]{1,0:T(8,128)(2,1)S(1)}, bf16[512,1024]{1,0:T(8,128)(2,1)}, u32[]{:S(2)}, u32[]{:S(2)}) collective-permute-start(bf16[512,1024]{1,0:T(8,128)(2,1)S(1)} %copy-done.3), channel_id=1, source_target_pairs={{0,1},{1,0},{2,3},{3,2},{4,5},{5,4},{6,7},{7,6},{8,9},{9,8},{10,11... | collective-permute-start | bytes 3145736 | tf_op jit(solution)/shard_map/ppermute | solution.py:645
  54.5 24.3 %collective-permute-start.5 = (bf16[512,1024]{1,0:T(8,128)(2,1)S(1)}, bf16[512,1024]{1,0:T(8,128)(2,1)}, u32[]{:S(2)}, u32[]{:S(2)}) collective-permute-start(bf16[512,1024]{1,0:T(8,128)(2,1)S(1)} %copy-done.3), channel_id=1, source_target_pairs={{0,2},{2,0},{1,3},{3,1},{4,6},{6,4},{5,7},{7,5},{8,10},{10,8},{9,1... | collective-permute-start | bytes 3145736 | tf_op jit(solution)/shard_map/ppermute | solution.py:649
  81.0 14.0 %collective-permute-start.6 = (bf16[512,512]{1,0:T(8,128)(2,1)S(1)}, bf16[512,512]{1,0:T(8,128)(2,1)S(1)}, u32[]{:S(2)}, u32[]{:S(2)}) collective-permute-start(bf16[512,512]{1,0:T(8,128)(2,1)S(1)} %slice.117), channel_id=1, source_target_pairs={{0,2},{2,0},{1,3},{3,1},{4,6},{6,4},{5,7},{7,5},{8,10},{10,8},{9,1... | collective-permute-start | bytes 1572872 | tf_op jit(solution)/shard_map/ppermute | solution.py:649
  82.4 12.7 %collective-permute-start.7 = (bf16[512,512]{1,0:T(8,128)(2,1)S(1)}, bf16[512,512]{1,0:T(8,128)(2,1)S(1)}, u32[]{:S(2)}, u32[]{:S(2)}) collective-permute-start(bf16[512,512]{1,0:T(8,128)(2,1)S(1)} %slice.118), channel_id=1, source_target_pairs={{0,1},{1,0},{2,3},{3,2},{4,5},{5,4},{6,7},{7,6},{8,9},{9,8},{10,11... | collective-permute-start | bytes 1572872 | tf_op jit(solution)/shard_map/ppermute | solution.py:645
  95.0 0.8 copy-start.12
  95.0 0.9 copy-start.13
  104.3 7.9 %copy-start.18 = (f32[8,2048]{1,0:T(8,128)S(1)}, f32[8,2048]{1,0:T(8,128)}, u32[]{:S(2)}) copy-start(f32[8,2048]{1,0:T(8,128)} %get-tuple-element.167) | copy-start | bytes 196612
  104.3 7.9 %collective-permute-start.8 = (f32[8,2048]{1,0:T(8,128)}, f32[8,2048]{1,0:T(8,128)S(1)}, u32[]{:S(2)}, u32[]{:S(2)}) collective-permute-start(f32[8,2048]{1,0:T(8,128)} %get-tuple-element.167), channel_id=1, source_target_pairs={{0,1},{1,0},{2,3},{3,2},{4,5},{5,4},{6,7},{7,6},{8,9},{9,8},{10,11... | collective-permute-start | bytes 196616 | tf_op jit(solution)/shard_map/ppermute | solution.py:645
  112.2 5.1 %collective-permute-start.9 = (f32[8,2048]{1,0:T(8,128)S(1)}, f32[8,2048]{1,0:T(8,128)S(1)}, u32[]{:S(2)}, u32[]{:S(2)}) collective-permute-start(f32[8,2048]{1,0:T(8,128)S(1)} %add.131), channel_id=1, source_target_pairs={{0,2},{2,0},{1,3},{3,1},{4,6},{6,4},{5,7},{7,5},{8,10},{10,8},{9,1... | collective-permute-start | bytes 196616 | tf_op jit(solution)/shard_map/ppermute | solution.py:649
  113.0 22.0 %collective-permute-start.10 = (bf16[1024,512]{1,0:T(8,128)(2,1)}, bf16[1024,512]{1,0:T(8,128)(2,1)S(1)}, u32[]{:S(2)}, u32[]{:S(2)}) collective-permute-start(bf16[1024,512]{1,0:T(8,128)(2,1)} %get-tuple-element.185), channel_id=1, source_target_pairs={{0,1},{1,0},{2,3},{3,2},{4,5},{5,4},{6,7},{7,6},{8,9},{9,8},{10,11... | collective-permute-start | bytes 3145736 | tf_op jit(solution)/shard_map/ppermute | solution.py:645
  114.4 21.9 %collective-permute-start.11 = (bf16[1024,512]{1,0:T(8,128)(2,1)}, bf16[1024,512]{1,0:T(8,128)(2,1)S(1)}, u32[]{:S(2)}, u32[]{:S(2)}) collective-permute-start(bf16[1024,512]{1,0:T(8,128)(2,1)} %get-tuple-element.186), channel_id=1, source_target_pairs={{0,2},{2,0},{1,3},{3,1},{4,6},{6,4},{5,7},{7,5},{8,10},{10,8},{9,1... | collective-permute-start | bytes 3145736 | tf_op jit(solution)/shard_map/ppermute | solution.py:649
  134.9 1.6 copy-start.7
  134.9 1.9 copy-start.8
  134.9 1.4 copy-start.10
  136.3 1.7 copy-start.9
  136.4 88.0 %reduce-scatter.5.cloned.1.call-start = ((), (), s32[]{:S(2)}) async-start(), calls=%async_computation.5 | async-start | bytes 2064384 | tf_op jit(solution)/shard_map/reduce_scatter | solution.py:1083
  138.0 45.8 %collective-permute-start.12 = (bf16[512,512]{1,0:T(8,128)(2,1)S(1)}, bf16[512,512]{1,0:T(8,128)(2,1)}, u32[]{:S(2)}, u32[]{:S(2)}) collective-permute-start(bf16[512,512]{1,0:T(8,128)(2,1)S(1)} %add_convert_fusion.3), channel_id=1, source_target_pairs={{0,2},{2,0},{1,3},{3,1},{4,6},{6,4},{5,7},{7,5},{8,10},{10,8},{9,1... | collective-permute-start | bytes 1572872 | tf_op jit(solution)/shard_map/ppermute | solution.py:649
  139.4 44.5 %collective-permute-start.13 = (bf16[512,512]{1,0:T(8,128)(2,1)S(1)}, bf16[512,512]{1,0:T(8,128)(2,1)}, u32[]{:S(2)}, u32[]{:S(2)}) collective-permute-start(bf16[512,512]{1,0:T(8,128)(2,1)S(1)} %add_convert_fusion.2), channel_id=1, source_target_pairs={{0,1},{1,0},{2,3},{3,2},{4,5},{5,4},{6,7},{7,6},{8,9},{9,8},{10,11... | collective-permute-start | bytes 1572872 | tf_op jit(solution)/shard_map/ppermute | solution.py:645
  183.8 1.2 copy-start
  183.8 3.4 %slice-start = ((f32[8,2048]{1,0:T(8,128)}), f32[1,2048]{1,0:T(1,128)S(1)}, s32[]{:S(2)}) async-start(f32[8,2048]{1,0:T(8,128)} %add.132.refs_5_), calls=%async_computation.6 | async-start | bytes 16384 | tf_op jit(solution)/shard_map/slice | solution.py:1107
  183.8 3.4 %copy-start.17 = (f32[16,1024]{1,0:T(8,128)S(1)}, f32[16,1024]{1,0:T(8,128)}, u32[]{:S(2)}) copy-start(f32[16,1024]{1,0:T(8,128)} %get-tuple-element.213) | copy-start | bytes 196612
  185.3 22.1 %collective-permute-start.18 = (bf16[1024,512]{1,0:T(8,128)(2,1)}, bf16[1024,512]{1,0:T(8,128)(2,1)}, u32[]{:S(2)}, u32[]{:S(2)}) collective-permute-start(bf16[1024,512]{1,0:T(8,128)(2,1)} %get-tuple-element.214), channel_id=1, source_target_pairs={{0,1},{1,0},{2,3},{3,2},{4,5},{5,4},{6,7},{7,6},{8,9},{9,8},{10,11... | collective-permute-start | bytes 3145736 | tf_op jit(solution)/shard_map/ppermute | solution.py:645
  186.5 20.9 %collective-permute-start.19 = (bf16[1024,512]{1,0:T(8,128)(2,1)}, bf16[1024,512]{1,0:T(8,128)(2,1)}, u32[]{:S(2)}, u32[]{:S(2)}) collective-permute-start(bf16[1024,512]{1,0:T(8,128)(2,1)} %get-tuple-element.215), channel_id=1, source_target_pairs={{0,2},{2,0},{1,3},{3,1},{4,6},{6,4},{5,7},{7,5},{8,10},{10,8},{9,1... | collective-permute-start | bytes 3145736 | tf_op jit(solution)/shard_map/ppermute | solution.py:649
  187.3 4.7 %copy-start.11 = (bf16[128,1024]{1,0:T(8,128)(2,1)S(1)}, bf16[128,1024]{1,0:T(8,128)(2,1)}, u32[]{:S(2)}) copy-start(bf16[128,1024]{1,0:T(8,128)(2,1)} %reduce-scatter.3.cloned.1.call-done) | copy-start | bytes 786436
  187.3 1.5 collective-permute-start.14
  188.8 5.2 %collective-permute-start.15 = (f32[16,1024]{1,0:T(8,128)S(1)}, f32[16,1024]{1,0:T(8,128)S(1)}, u32[]{:S(2)}, u32[]{:S(2)}) collective-permute-start(f32[16,1024]{1,0:T(8,128)S(1)} %add.145), channel_id=1, source_target_pairs={{0,8},{4,12},{8,0},{12,4},{16,24},{20,28},{24,16},{28,20},{1,9},{5... | collective-permute-start | bytes 196616 | tf_op jit(solution)/shard_map/ppermute | solution.py:694
  194.0 9.0 %collective-permute-start.16 = (f32[16,1024]{1,0:T(8,128)S(1)}, f32[16,1024]{1,0:T(8,128)S(1)}, u32[]{:S(2)}, u32[]{:S(2)}) collective-permute-start(f32[16,1024]{1,0:T(8,128)S(1)} %add.146), channel_id=1, source_target_pairs={{0,16},{4,20},{8,24},{12,28},{16,0},{20,4},{24,8},{28,12},{1,17},{... | collective-permute-start | bytes 196616 | tf_op jit(solution)/shard_map/ppermute | solution.py:694
  203.1 4.3 %collective-permute-start.17 = (f32[16,1024]{1,0:T(8,128)S(1)}, f32[16,1024]{1,0:T(8,128)S(1)}, u32[]{:S(2)}, u32[]{:S(2)}) collective-permute-start(f32[16,1024]{1,0:T(8,128)S(1)} %add.147), channel_id=1, source_target_pairs={{0,1},{1,0},{2,3},{3,2},{4,5},{5,4},{6,7},{7,6},{8,9},{9,8},{10,11... | collective-permute-start | bytes 196616 | tf_op jit(solution)/shard_map/ppermute | solution.py:645
  204.8 4.9 %copy-start.5 = (bf16[1024,512]{1,0:T(8,128)(2,1)S(1)}, bf16[1024,512]{1,0:T(8,128)(2,1)}, u32[]{:S(2)}) copy-start(bf16[1024,512]{1,0:T(8,128)(2,1)} %get-tuple-element.212) | copy-start | bytes 3145732
  207.4 4.3 %collective-permute-start.20 = (f32[16,1024]{1,0:T(8,128)S(1)}, f32[16,1024]{1,0:T(8,128)S(1)}, u32[]{:S(2)}, u32[]{:S(2)}) collective-permute-start(f32[16,1024]{1,0:T(8,128)S(1)} %add.148), channel_id=1, source_target_pairs={{0,2},{2,0},{1,3},{3,1},{4,6},{6,4},{5,7},{7,5},{8,10},{10,8},{9,1... | collective-permute-start | bytes 196616 | tf_op jit(solution)/shard_map/ppermute | solution.py:649
  211.8 12.1 %collective-permute-start.21 = (bf16[512,512]{1,0:T(8,128)(2,1)S(1)}, bf16[512,512]{1,0:T(8,128)(2,1)}, u32[]{:S(2)}, u32[]{:S(2)}) collective-permute-start(bf16[512,512]{1,0:T(8,128)(2,1)S(1)} %add_convert_fusion.1), channel_id=1, source_target_pairs={{0,2},{2,0},{1,3},{3,1},{4,6},{6,4},{5,7},{7,5},{8,10},{10,8},{9,1... | collective-permute-start | bytes 1572872 | tf_op jit(solution)/shard_map/ppermute | solution.py:649
  212.7 11.7 %collective-permute-start.22 = (bf16[512,512]{1,0:T(8,128)(2,1)S(1)}, bf16[512,512]{1,0:T(8,128)(2,1)}, u32[]{:S(2)}, u32[]{:S(2)}) collective-permute-start(bf16[512,512]{1,0:T(8,128)(2,1)S(1)} %add_convert_fusion), channel_id=1, source_target_pairs={{0,1},{1,0},{2,3},{3,2},{4,5},{5,4},{6,7},{7,6},{8,9},{9,8},{10,11... | collective-permute-start | bytes 1572872 | tf_op jit(solution)/shard_map/ppermute | solution.py:645
  224.4 3.9 %copy-start.6 = (bf16[1024,512]{1,0:T(8,128)(2,1)S(1)}, bf16[1024,512]{1,0:T(8,128)(2,1)}, u32[]{:S(2)}) copy-start(bf16[1024,512]{1,0:T(8,128)(2,1)} %get-tuple-element.212) | copy-start | bytes 3145732
  225.4 4.3 %copy-start.14 = (bf16[128,896]{1,0:T(8,128)(2,1)S(1)}, bf16[128,896]{1,0:T(8,128)(2,1)}, u32[]{:S(2)}) copy-start(bf16[128,896]{1,0:T(8,128)(2,1)} %reduce-scatter.5.cloned.1.call-done) | copy-start | bytes 688132
  225.4 5.1 %collective-permute-start.23 = (bf16[128,384]{1,0:T(8,128)(2,1)S(1)}, bf16[128,384]{1,0:T(8,128)(2,1)S(1)}, u32[]{:S(2)}, u32[]{:S(2)}) collective-permute-start(bf16[128,384]{1,0:T(8,128)(2,1)S(1)} %slice.136), channel_id=1, source_target_pairs={{0,1},{1,0},{2,3},{3,2},{4,5},{5,4},{6,7},{7,6},{8,9},{9,8},{10,11... | collective-permute-start | bytes 294920 | tf_op jit(solution)/shard_map/ppermute | solution.py:645
  228.3 3.5 %copy-start.16 = (f32[1,1024]{1,0:T(1,128)S(1)}, f32[1,1024]{1,0:T(1,128)}, u32[]{:S(2)}) copy-start(f32[1,1024]{1,0:T(1,128)} %get-tuple-element.136.refs_6_.refs_1_) | copy-start | bytes 12292
  229.7 2.6 %copy-start.4 = (bf16[512,1024]{1,0:T(8,128)(2,1)S(1)}, bf16[512,1024]{1,0:T(8,128)(2,1)}, u32[]{:S(2)}) copy-start(bf16[512,1024]{1,0:T(8,128)(2,1)} %refs_0_.3) | copy-start | bytes 3145732
  230.5 4.7 %collective-permute-start.24 = (bf16[128,384]{1,0:T(8,128)(2,1)S(1)}, bf16[128,384]{1,0:T(8,128)(2,1)S(1)}, u32[]{:S(2)}, u32[]{:S(2)}) collective-permute-start(bf16[128,384]{1,0:T(8,128)(2,1)S(1)} %add_convert_fusion.4), channel_id=1, source_target_pairs={{0,2},{2,0},{1,3},{3,1},{4,6},{6,4},{5,7},{7,5},{8,10},{10,8},{9,1... | collective-permute-start | bytes 294920 | tf_op jit(solution)/shard_map/ppermute | solution.py:649
Sparse Core Ops, SparseCore 0:
  10.2 39.0 all-gather.2
  51.5 20.8 all-gather.4
  136.5 35.7 reduce-scatter.2
  184.0 36.8 reduce-scatter.4

commit v5 on v4

--- a/solution.py
+++ b/solution.py
@@ -152,17 +152,21 @@
 def take_rows(refs, which, buffer):
     if len(refs) == 1:
         return refs[0][...]
-    half = refs[3].shape[1]
-    for k in range(3):
+    half = buffer.shape[1] // 2
+    slots, at = [], 0
+    while at < len(refs):
+        count = 1 if refs[at].shape[1] == 2 * half else 2
+        slots.append(refs[at : at + count])
+        at += count
+    for k, slot in enumerate(slots):
 
         @pl.when(which == k)
-        def _(k=k):
-            buffer[...] = refs[k][...]
-
-    @pl.when(which == 3)
-    def _():
-        buffer[:, :half] = refs[3][...]
-        buffer[:, half:] = refs[4][...]
+        def _(slot=slot):
+            if len(slot) == 1:
+                buffer[...] = slot[0][...]
+            else:
+                buffer[:, :half] = slot[0][...]
+                buffer[:, half:] = slot[1][...]
 
     return buffer[...]
 
@@ -778,7 +782,7 @@
                 ),
                 z,
             )
-            for k, z in zip((1, 2, 3, 4, 4), arrays)
+            for k, z in zip((1, 2, 3, 4, 4) if len(arrays) == 5 else (1, 2, 2, 3, 3, 4, 4), arrays)
         ]
 
     def halves(self, block, backwards=False):
@@ -983,7 +987,10 @@
     )
     out_weights = lax.all_gather(proj_out.T, "dp", axis=0, tiled=True)
     if square_mesh:
-        from_x, from_y = gather_start(hidden_in)
+        half = width // 2
+        left, right = hidden_in[:, :half], hidden_in[:, half:]
+        x_left, y_right = over_x(left), over_y(right)
+        x_right, y_left = over_x(right), over_y(left)
 
     def padded(z):
         return jnp.pad(z, ((0, 0), (0, LANES - z.shape[1])))
@@ -1004,8 +1011,9 @@
     packed = jnp.pad(packed, ((0, PARAMS - packed.shape[0]), (0, 0)))
     packed = lax.all_gather(packed, "dp", axis=1, tiled=True)
     if square_mesh:
-        from_x, from_y, packed = lax.optimization_barrier((from_x, from_y, packed))
-        hidden_all, _ = gather_end(hidden_in, from_x, from_y)
+        x_left, y_right, packed = lax.optimization_barrier((x_left, y_right, packed))
+        far_left, far_right = over_y(x_left), over_x(y_right)
+        hidden_all = [hidden_in, x_left, x_right, y_left, y_right, far_left, far_right]
     else:
         hidden_all = [lax.all_gather(hidden_in, "tensor", axis=0, tiled=True)]
 

time: 243 us -> 242 us (level)
  waiting for transfers between devices: 32.5 us -> 36 us
    ppermute x11 -> x12, waiting for transfers between devices: 20 us -> 25 us  [over_y(): return lax.ppermute(z, 'tensor', [(0, 2), (2, 0), (1, 3), (3, 1)])]
    ppermute x11 -> x12, waiting for transfers between devices: 6.28 us -> 4.84 us  [over_x(): return lax.ppermute(z, 'tensor', [(0, 1), (1, 0), (2, 3), (3, 2)])]
    ppermute x11 -> x12, starting transfers between devices: 12.4 us -> 11.3 us  [over_y(): return lax.ppermute(z, 'tensor', [(0, 2), (2, 0), (1, 3), (3, 1)])]
    ppermute x11 -> x12, starting transfers between devices: 13.9 us -> 14.1 us  [over_x(): return lax.ppermute(z, 'tensor', [(0, 1), (1, 0), (2, 3), (3, 2)])]
    unnamed x41 -> x67, local copies, waits for them, and re-layouts: 5.09 us -> 4.91 us
  transfers between devices with their start and end apart: 29 -> 31, of which waited for: 13 -> 13; matrix products, arithmetic and copies ran while one was open for 12% -> 11% of each run, Pallas kernels for 43% -> 43%
where the time goes in v5:
time: 242 us
  Pallas kernels  112 us (46%)
  waiting for transfers between devices  36 us (15%)
  starting transfers between devices  31.1 us (13%)
  other arithmetic  16.8 us (7%)
  local copies, waits for them, and re-layouts  15.9 us (7%)
  between operations  15.1 us (6%)
  blocking collectives  14.2 us (6%)
    pallas_call x7, Pallas kernels, call(): pl.pallas_call(kernel, grid_spec=pltpu.PrefetchScalarGridSpec(num_scalar_...  112 us
    ppermute x12, waiting for transfers between devices, over_y(): return lax.ppermute(z, 'tensor', [(0, 2), (2, 0), (1, 3), (3, 1)])  25 us
    all_gather x1, blocking collectives, per_device(): packed = lax.all_gather(packed, 'dp', axis=1, tiled=True)  14.2 us
    ppermute x12, starting transfers between devices, over_x(): return lax.ppermute(z, 'tensor', [(0, 1), (1, 0), (2, 3), (3, 2)])  14.1 us
    ppermute x12, starting transfers between devices, over_y(): return lax.ppermute(z, 'tensor', [(0, 2), (2, 0), (1, 3), (3, 1)])  11.3 us
    ppermute x3, waiting for transfers between devices, sum_over_dp(): z = z + lax.ppermute(z, 'dp', [(i, i ^ bit) for i in range(count)])  6.04 us
    ppermute x3, starting transfers between devices, sum_over_dp(): z = z + lax.ppermute(z, 'dp', [(i, i ^ bit) for i in range(count)])  5.22 us
    unnamed x67, local copies, waits for them, and re-layouts  4.91 us
  transfers between devices with their start and end apart: 31, of which 13 were waited for; matrix products, arithmetic and copies ran while one was open for 11% of the time, Pallas kernels for 43%

profile of v5, /device:TPU:0, one launch (start us, length us, event | category | flops | bytes accessed | tf_op | source)
XLA Modules:
  0.0 241.6 jit_solution(1714823983409021354)
XLA Ops:
  7.3 1.1 copy.48
  8.5 1.7 fusion.9
  10.3 2.2 fusion.25
  12.5 2.9 %collective-permute-start = (bf16[512,512]{1,0:T(8,128)(2,1)}, bf16[512,512]{1,0:T(8,128)(2,1)S(1)}, u32[]{:S(2)}, u32[]{:S(2)}) collective-permute-start(bf16[512,512]{1,0:T(8,128)(2,1)} %get-tuple-element.249), channel_id=1, source_target_pairs={{0,1},{1,0},{2,3},{3,2},{4,5},{5,4},{6,7},{7,6},{8,9},{9,8},{10,11... | collective-permute-start | bytes 1572872 | tf_op jit(solution)/shard_map/ppermute | solution.py:649
  15.5 1.5 collective-permute-start.1
  17.0 0.5 collective-permute-start.2
  18.0 14.2 %all_gather.9.packed_ref = bf16[16,1024]{1,0:T(8,128)(2,1)} all-gather(bf16[16,128]{1,0:T(8,128)(2,1)S(1)} %fusion.16), channel_id=1, replica_groups=mesh['dp'=8,'tensor'=4] {'dp'}, dimensions={1}, use_global_device_ids=true | all-gather | bytes 36864 | tf_op jit(solution)/shard_map/all_gather | solution.py:1012
  32.2 1.4 collective-permute-start.4
  33.6 1.5 collective-permute-start.5
  35.2 0.8 copy.49
  36.0 1.3 constant_dynamic-slice_fusion.5
  37.3 2.2 parameter_kernel.1
  39.6 2.1 collective-permute-done.3.refs_3_
  41.7 9.9 %collective-permute-done.4.refs_5_ = bf16[512,512]{1,0:T(8,128)(2,1)} collective-permute-done((bf16[512,512]{1,0:T(8,128)(2,1)S(1)}, bf16[512,512]{1,0:T(8,128)(2,1)}, u32[]{:S(2)}, u32[]{:S(2)}) %collective-permute-start.4) | collective-permute-done | bytes 524320 | tf_op jit(solution)/shard_map/ppermute | solution.py:653
  52.0 1.7 collective-permute-start.7
  54.5 23.2 %scan_kernel.2 = (bf16[2048,1024]{1,0:T(8,128)(2,1)}, bf16[2048,512]{1,0:T(8,128)(2,1)}, f32[2048,512]{1,0:T(8,128)}, bf16[2048,256]{1,0:T(8,128)(2,1)}, f32[204...) custom-call(s32[1,1]{1,0:T(1,128)S(6)} %copy.63.len_ref, ...), custom_call_target="tpu_custom_call" | custom-call | flops 1000 | bytes 1000 | tf_op jit(solution)/shard_map/scan_kernel/pallas_call | solution.py:738
  77.8 0.9 slice.117
  78.7 0.8 slice.118
  79.8 1.7 collective-permute-start.9
  81.5 11.2 %scan_kernel.3 = (bf16[2048,1024]{1,0:T(8,128)(2,1)}, bf16[2048,512]{1,0:T(8,128)(2,1)}, f32[2048,512]{1,0:T(8,128)}, bf16[2048,256]{1,0:T(8,128)(2,1)}, f32[204...) custom-call(s32[1,1]{1,0:T(1,128)S(6)} %copy.63.len_ref, ...), custom_call_target="tpu_custom_call", output_to_operand_aliasing={{0}: (20, {}), {1}: (21, {}), {2}: (22, {}), {3}: (23, {}),... | custom-call | flops 1000 | bytes 1000 | tf_op jit(solution)/shard_map/scan_kernel/pallas_call | solution.py:738
  92.8 0.8 copy-done.16
  93.7 8.3 %cotangent_kernel.1 = (bf16[2048,512]{1,0:T(8,128)(2,1)}, f32[8,2048]{1,0:T(8,128)}) custom-call(s32[216]{0:T(256)} %bitcast.31, bf16[512,1024]{1,0:T(8,128)(2,1)} %refs_0_.3, bf16[512,1024]{1,0:T(8,128)(2,1)} %copy-done.3, bf16[512,1024]{1,0:T(8,128)(2,1)} %copy-done.4, bf16[512,512]{1,0:T(8,128)(2,1)} %copy-done.16, bf16[512,512]{1,0:T(8,128)(2,1)} %copy-done.17, ...), custom_call_target="tpu_custom_call" | custom-call | flops 1000 | bytes 1000 | tf_op jit(solution)/shard_map/cotangent_kernel/pallas_call | solution.py:738
  102.5 7.4 %product_kernel.1 = (bf16[1024,512]{1,0:T(8,128)(2,1)}, bf16[1024,512]{1,0:T(8,128)(2,1)}, bf16[1024,512]{1,0:T(8,128)(2,1)}, bf16[1024,512]{1,0:T(8,128)(2,1)}) custom-call(s32[216]{0:T(256)} %bitcast.32, bf16[2048,512]{1,0:T(8,128)(2,1)} %get-tuple-element.169.refs_6_.ga_ref, bf16[1024,512]{1,0:T(8,128)(2,1)} %all-gather.5.cloned.1.call-done.refs_5_.w_ref), custom_call_target="tpu_custom_call" | custom-call | flops 1000 | bytes 1000 | tf_op jit(solution)/shard_map/product_kernel/pallas_call | solution.py:738
  109.9 1.6 collective-permute-start.11
  111.6 1.6 collective-permute-start.12
  113.7 1.3 collective-permute-done.11
  115.0 0.6 add.132.refs_5_
  115.6 16.9 %gate_kernel.1 = (bf16[2048,512]{1,0:T(8,128)(2,1)}, f32[2048,512]{1,0:T(8,128)}, f32[8,512]{1,0:T(8,128)}, bf16[1024,1024]{1,0:T(8,128)(2,1)}, f32[8,1024]{1,0:T(8,128)}) custom-call(s32[216]{0:T(256)} %bitcast.33, bf16[512,1024]{1,0:T(8,128)(2,1)} %refs_0_.3, bf16[512,1024]{1,0:T(8,128)(2,1)} %copy-done.3, bf16[512,1024]{1,0:T(8,128)(2,1)} %copy-done.4, ...), custom_call_target="tpu_custom_call" | custom-call | flops 34359738368 | bytes 1000 | tf_op jit(solution)/shard_map/gate_kernel/pallas_call | solution.py:738
  132.5 1.3 collective-permute-done.12
  133.8 2.1 collective-permute-done.13
  136.3 1.2 add_convert_fusion.3
  137.5 0.5 collective-permute-start.14
  138.0 0.9 collective-permute-start.15
  138.9 43.3 %backward_kernel.1 = (bf16[1024,512]{1,0:T(8,128)(2,1)}, bf16[1024,512]{1,0:T(8,128)(2,1)}, bf16[1024,512]{1,0:T(8,128)(2,1)}, bf16[1024,512]{1,0:T(8,128)(2,1)}...) custom-call(s32[1,1]{1,0:T(1,128)S(6)} %copy.63.len_ref, ...), custom_call_target="tpu_custom_call" | custom-call | flops 1000 | bytes 1000 | tf_op jit(solution)/shard_map/backward_kernel/pallas_call | solution.py:738
  182.4 1.1 copy-done
  183.8 1.2 collective-permute-start.20
  185.0 1.5 collective-permute-start.21
  186.7 1.4 convert_add_fusion.4
  188.1 1.7 collective-permute-start.17
  189.8 1.6 convert_add_fusion.3
  191.4 1.9 collective-permute-done.17
  193.3 3.5 %collective-permute-start.18 = (f32[16,1024]{1,0:T(8,128)S(1)}, f32[16,1024]{1,0:T(8,128)S(1)}, u32[]{:S(2)}, u32[]{:S(2)}) collective-permute-start(f32[16,1024]{1,0:T(8,128)S(1)} %add.146), channel_id=1, source_target_pairs={{0,16},{4,20},{8,24},{12,28},{16,0},{20,4},{24,8},{28,12},{1,17},{... | collective-permute-start | bytes 196616 | tf_op jit(solution)/shard_map/ppermute | solution.py:698
  196.8 0.7 slice.154
  197.5 0.8 copy.50
  198.4 4.1 %collective-permute-done.18 = f32[16,1024]{1,0:T(8,128)S(1)} collective-permute-done((f32[16,1024]{1,0:T(8,128)S(1)}, f32[16,1024]{1,0:T(8,128)S(1)}, u32[]{:S(2)}, u32[]{:S(2)}) %collective-permute-start.18) | collective-permute-done | bytes 65568 | tf_op jit(solution)/shard_map/ppermute | solution.py:698
  202.7 0.7 constant_dynamic-slice_fusion
  203.3 0.7 dynamic-slice_bitcast_fusion
  204.0 2.8 %collective-permute-done.19 = f32[16,1024]{1,0:T(8,128)S(1)} collective-permute-done((f32[16,1024]{1,0:T(8,128)S(1)}, f32[16,1024]{1,0:T(8,128)S(1)}, u32[]{:S(2)}, u32[]{:S(2)}) %collective-permute-start.19) | collective-permute-done | bytes 65568 | tf_op jit(solution)/shard_map/ppermute | solution.py:649
  207.3 1.3 add_convert_fusion
  208.7 1.2 add_convert_fusion.1
  209.9 1.3 collective-permute-done.22
  211.7 1.7 collective-permute-start.24
  213.4 0.6 slice.146
  214.1 0.6 fusion.24
  215.7 7.7 %collective-permute-done.23 = bf16[512,512]{1,0:T(8,128)(2,1)} collective-permute-done((bf16[512,512]{1,0:T(8,128)(2,1)S(1)}, bf16[512,512]{1,0:T(8,128)(2,1)}, u32[]{:S(2)}, u32[]{:S(2)}) %collective-permute-start.23) | collective-permute-done | bytes 524320 | tf_op jit(solution)/shard_map/ppermute | solution.py:653
  223.9 1.0 slice.136
  224.9 1.1 collective-permute-start.25
  226.0 1.5 convert_add_fusion.1
  227.6 1.4 convert_add_fusion.2
  229.0 0.7 slice_convert_fusion
  229.8 1.3 collective-permute-start.26
  231.6 2.2 fusion.5
  233.8 0.7 collective-permute-done.26
  234.4 0.6 convert_add_fusion.5
  (131 shorter events, 7.0 us)
Async XLA Ops:
  7.2 10.3 %copy-start.24 = (bf16[8,8]{1,0:T(8,128)(2,1)S(1)}, bf16[8,8]{1,0:T(8,128)(2,1)}, u32[]{:S(2)}) copy-start(bf16[8,8]{1,0:T(8,128)(2,1)} %param.27) | copy-start | bytes 388
  7.2 10.4 %copy-start.25 = (bf16[8,8]{1,0:T(8,128)(2,1)S(1)}, bf16[8,8]{1,0:T(8,128)(2,1)}, u32[]{:S(2)}) copy-start(bf16[8,8]{1,0:T(8,128)(2,1)} %param.33) | copy-start | bytes 388
  7.2 10.5 %copy-start.23 = (bf16[4,8,8]{2,1,0:T(8,128)(2,1)S(1)}, bf16[4,8,8]{2,1,0:T(8,128)(2,1)}, u32[]{:S(2)}) copy-start(bf16[4,8,8]{2,1,0:T(8,128)(2,1)} %param.26) | copy-start | bytes 1540
  7.2 10.6 %copy-start.26 = (bf16[4,32]{1,0:T(4,128)(2,1)S(1)}, bf16[4,32]{1,0:T(4,128)(2,1)}, u32[]{:S(2)}) copy-start(bf16[4,32]{1,0:T(4,128)(2,1)} %param.28) | copy-start | bytes 772
  7.2 10.6 %copy-start.27 = (bf16[32]{0:T(256)(128)(2,1)S(1)}, bf16[32]{0:T(256)(128)(2,1)}, u32[]{:S(2)}) copy-start(bf16[32]{0:T(256)(128)(2,1)} %param.29) | copy-start | bytes 196
  7.2 10.6 %copy-start.30 = (bf16[4]{0:T(256)(128)(2,1)S(1)}, bf16[4]{0:T(256)(128)(2,1)}, u32[]{:S(2)}) copy-start(bf16[4]{0:T(256)(128)(2,1)} %param.30) | copy-start | bytes 28
  7.2 10.6 %copy-start.29 = (bf16[4]{0:T(256)(128)(2,1)S(1)}, bf16[4]{0:T(256)(128)(2,1)}, u32[]{:S(2)}) copy-start(bf16[4]{0:T(256)(128)(2,1)} %param.31) | copy-start | bytes 28
  7.3 10.6 %copy-start.28 = (bf16[4]{0:T(256)(128)(2,1)S(1)}, bf16[4]{0:T(256)(128)(2,1)}, u32[]{:S(2)}) copy-start(bf16[4]{0:T(256)(128)(2,1)} %param.32) | copy-start | bytes 28
  7.3 10.7 %copy-start.31 = (bf16[128]{0:T(256)(128)(2,1)S(1)}, bf16[128]{0:T(256)(128)(2,1)}, u32[]{:S(2)}) copy-start(bf16[128]{0:T(256)(128)(2,1)} %param.22) | copy-start | bytes 772
  7.3 27.9 %copy-start.19 = (bf16[512,128]{1,0:T(8,128)(2,1)S(1)}, bf16[512,128]{1,0:T(8,128)(2,1)}, u32[]{:S(2)}) copy-start(bf16[512,128]{1,0:T(8,128)(2,1)} %param.34) | copy-start | bytes 393220
  7.3 44.4 %copy-start.1 = (bf16[512,1024]{1,0:T(8,128)(2,1)S(1)}, bf16[512,1024]{1,0:T(8,128)(2,1)}, u32[]{:S(2)}) copy-start(bf16[512,1024]{1,0:T(8,128)(2,1)} %refs_0_.3) | copy-start | bytes 3145732
  7.3 47.2 %all-gather.3.cloned.1.call-start = ((), (), s32[]{:S(2)}) async-start(), calls=%async_computation.2 | async-start | bytes 3244032 | tf_op jit(solution)/shard_map/all_gather | solution.py:985
  10.2 82.5 %all-gather.5.cloned.1.call-start = ((), (), s32[]{:S(2)}) async-start(), calls=%async_computation.3 | async-start | bytes 1179648 | tf_op jit(solution)/shard_map/all_gather | solution.py:988
  12.5 19.7 %collective-permute-start = (bf16[512,512]{1,0:T(8,128)(2,1)}, bf16[512,512]{1,0:T(8,128)(2,1)S(1)}, u32[]{:S(2)}, u32[]{:S(2)}) collective-permute-start(bf16[512,512]{1,0:T(8,128)(2,1)} %get-tuple-element.249), channel_id=1, source_target_pairs={{0,1},{1,0},{2,3},{3,2},{4,5},{5,4},{6,7},{7,6},{8,9},{9,8},{10,11... | collective-permute-start | bytes 1572872 | tf_op jit(solution)/shard_map/ppermute | solution.py:649
  15.5 16.8 %collective-permute-start.1 = (bf16[512,512]{1,0:T(8,128)(2,1)}, bf16[512,512]{1,0:T(8,128)(2,1)S(1)}, u32[]{:S(2)}, u32[]{:S(2)}) collective-permute-start(bf16[512,512]{1,0:T(8,128)(2,1)} %get-tuple-element.248), channel_id=1, source_target_pairs={{0,2},{2,0},{1,3},{3,1},{4,6},{6,4},{5,7},{7,5},{8,10},{10,8},{9,1... | collective-permute-start | bytes 1572872 | tf_op jit(solution)/shard_map/ppermute | solution.py:653
  17.0 22.7 %collective-permute-start.2 = (bf16[512,512]{1,0:T(8,128)(2,1)}, bf16[512,512]{1,0:T(8,128)(2,1)S(1)}, u32[]{:S(2)}, u32[]{:S(2)}) collective-permute-start(bf16[512,512]{1,0:T(8,128)(2,1)} %get-tuple-element.248), channel_id=1, source_target_pairs={{0,1},{1,0},{2,3},{3,2},{4,5},{5,4},{6,7},{7,6},{8,9},{9,8},{10,11... | collective-permute-start | bytes 1572872 | tf_op jit(solution)/shard_map/ppermute | solution.py:649
  17.5 24.2 %collective-permute-start.3 = (bf16[512,512]{1,0:T(8,128)(2,1)}, bf16[512,512]{1,0:T(8,128)(2,1)S(1)}, u32[]{:S(2)}, u32[]{:S(2)}) collective-permute-start(bf16[512,512]{1,0:T(8,128)(2,1)} %get-tuple-element.249), channel_id=1, source_target_pairs={{0,2},{2,0},{1,3},{3,1},{4,6},{6,4},{5,7},{7,5},{8,10},{10,8},{9,1... | collective-permute-start | bytes 1572872 | tf_op jit(solution)/shard_map/ppermute | solution.py:653
  32.2 19.4 %copy-start.5 = (bf16[512,512]{1,0:T(8,128)(2,1)}, bf16[512,512]{1,0:T(8,128)(2,1)S(1)}, u32[]{:S(2)}) copy-start(bf16[512,512]{1,0:T(8,128)(2,1)S(1)} %collective-permute-done.refs_1_) | copy-start | bytes 1572868
  32.2 19.4 %copy-start.6 = (bf16[512,512]{1,0:T(8,128)(2,1)}, bf16[512,512]{1,0:T(8,128)(2,1)S(1)}, u32[]{:S(2)}) copy-start(bf16[512,512]{1,0:T(8,128)(2,1)S(1)} %collective-permute-done.1.refs_4_) | copy-start | bytes 1572868
  32.2 19.4 %collective-permute-start.4 = (bf16[512,512]{1,0:T(8,128)(2,1)S(1)}, bf16[512,512]{1,0:T(8,128)(2,1)}, u32[]{:S(2)}, u32[]{:S(2)}) collective-permute-start(bf16[512,512]{1,0:T(8,128)(2,1)S(1)} %collective-permute-done.refs_1_), channel_id=1, source_target_pairs={{0,2},{2,0},{1,3},{3,1},{4,6},{6,4},{5,7},{7,5},{8,10},{10,8},{9,1... | collective-permute-start | bytes 1572872 | tf_op jit(solution)/shard_map/ppermute | solution.py:653
  33.6 18.0 %collective-permute-start.5 = (bf16[512,512]{1,0:T(8,128)(2,1)S(1)}, bf16[512,512]{1,0:T(8,128)(2,1)}, u32[]{:S(2)}, u32[]{:S(2)}) collective-permute-start(bf16[512,512]{1,0:T(8,128)(2,1)S(1)} %collective-permute-done.1.refs_4_), channel_id=1, source_target_pairs={{0,1},{1,0},{2,3},{3,2},{4,5},{5,4},{6,7},{7,6},{8,9},{9,8},{10,11... | collective-permute-start | bytes 1572872 | tf_op jit(solution)/shard_map/ppermute | solution.py:649
  36.0 146.4 %reduce-scatter.3.cloned.1.call-start = ((), (), s32[]{:S(2)}) async-start(), calls=%async_computation.4 | async-start | bytes 2359296 | tf_op jit(solution)/shard_map/reduce_scatter | solution.py:1069
  39.6 12.0 %copy-start.7 = (bf16[512,512]{1,0:T(8,128)(2,1)}, bf16[512,512]{1,0:T(8,128)(2,1)S(1)}, u32[]{:S(2)}) copy-start(bf16[512,512]{1,0:T(8,128)(2,1)S(1)} %collective-permute-done.2.refs_2_) | copy-start | bytes 1572868
  41.7 9.9 %copy-start.8 = (bf16[512,512]{1,0:T(8,128)(2,1)}, bf16[512,512]{1,0:T(8,128)(2,1)S(1)}, u32[]{:S(2)}) copy-start(bf16[512,512]{1,0:T(8,128)(2,1)S(1)} %collective-permute-done.3.refs_3_) | copy-start | bytes 1572868
  51.7 26.0 %collective-permute-start.6 = (bf16[512,1024]{1,0:T(8,128)(2,1)S(1)}, bf16[512,1024]{1,0:T(8,128)(2,1)S(1)}, u32[]{:S(2)}, u32[]{:S(2)}) collective-permute-start(bf16[512,1024]{1,0:T(8,128)(2,1)S(1)} %copy-done.1), channel_id=1, source_target_pairs={{0,1},{1,0},{2,3},{3,2},{4,5},{5,4},{6,7},{7,6},{8,9},{9,8},{10,11... | collective-permute-start | bytes 3145736 | tf_op jit(solution)/shard_map/ppermute | solution.py:649
  52.0 25.7 %collective-permute-start.7 = (bf16[512,1024]{1,0:T(8,128)(2,1)S(1)}, bf16[512,1024]{1,0:T(8,128)(2,1)S(1)}, u32[]{:S(2)}, u32[]{:S(2)}) collective-permute-start(bf16[512,1024]{1,0:T(8,128)(2,1)S(1)} %copy-done.1), channel_id=1, source_target_pairs={{0,2},{2,0},{1,3},{3,1},{4,6},{6,4},{5,7},{7,5},{8,10},{10,8},{9,1... | collective-permute-start | bytes 3145736 | tf_op jit(solution)/shard_map/ppermute | solution.py:653
  77.7 15.0 %copy-start.3 = (bf16[512,1024]{1,0:T(8,128)(2,1)}, bf16[512,1024]{1,0:T(8,128)(2,1)S(1)}, u32[]{:S(2)}) copy-start(bf16[512,1024]{1,0:T(8,128)(2,1)S(1)} %collective-permute-done.6.refs_1_) | copy-start | bytes 3145732
  77.7 15.0 %copy-start.4 = (bf16[512,1024]{1,0:T(8,128)(2,1)}, bf16[512,1024]{1,0:T(8,128)(2,1)S(1)}, u32[]{:S(2)}) copy-start(bf16[512,1024]{1,0:T(8,128)(2,1)S(1)} %collective-permute-done.7.refs_2_) | copy-start | bytes 3145732
  79.5 13.2 %collective-permute-start.8 = (bf16[512,512]{1,0:T(8,128)(2,1)}, bf16[512,512]{1,0:T(8,128)(2,1)S(1)}, u32[]{:S(2)}, u32[]{:S(2)}) collective-permute-start(bf16[512,512]{1,0:T(8,128)(2,1)} %slice.117), channel_id=1, source_target_pairs={{0,2},{2,0},{1,3},{3,1},{4,6},{6,4},{5,7},{7,5},{8,10},{10,8},{9,1... | collective-permute-start | bytes 1572872 | tf_op jit(solution)/shard_map/ppermute | solution.py:653
  79.8 13.0 %collective-permute-start.9 = (bf16[512,512]{1,0:T(8,128)(2,1)}, bf16[512,512]{1,0:T(8,128)(2,1)S(1)}, u32[]{:S(2)}, u32[]{:S(2)}) collective-permute-start(bf16[512,512]{1,0:T(8,128)(2,1)} %slice.118), channel_id=1, source_target_pairs={{0,1},{1,0},{2,3},{3,2},{4,5},{5,4},{6,7},{7,6},{8,9},{9,8},{10,11... | collective-permute-start | bytes 1572872 | tf_op jit(solution)/shard_map/ppermute | solution.py:649
  92.8 0.8 copy-start.16
  92.8 1.0 copy-start.17
  102.1 7.8 %copy-start.22 = (f32[8,2048]{1,0:T(8,128)S(1)}, f32[8,2048]{1,0:T(8,128)}, u32[]{:S(2)}) copy-start(f32[8,2048]{1,0:T(8,128)} %get-tuple-element.167) | copy-start | bytes 196612
  102.1 7.8 %collective-permute-start.10 = (f32[8,2048]{1,0:T(8,128)}, f32[8,2048]{1,0:T(8,128)S(1)}, u32[]{:S(2)}, u32[]{:S(2)}) collective-permute-start(f32[8,2048]{1,0:T(8,128)} %get-tuple-element.167), channel_id=1, source_target_pairs={{0,1},{1,0},{2,3},{3,2},{4,5},{5,4},{6,7},{7,6},{8,9},{9,8},{10,11... | collective-permute-start | bytes 196616 | tf_op jit(solution)/shard_map/ppermute | solution.py:649
  109.9 5.0 %collective-permute-start.11 = (f32[8,2048]{1,0:T(8,128)S(1)}, f32[8,2048]{1,0:T(8,128)S(1)}, u32[]{:S(2)}, u32[]{:S(2)}) collective-permute-start(f32[8,2048]{1,0:T(8,128)S(1)} %add.131), channel_id=1, source_target_pairs={{0,2},{2,0},{1,3},{3,1},{4,6},{6,4},{5,7},{7,5},{8,10},{10,8},{9,1... | collective-permute-start | bytes 196616 | tf_op jit(solution)/shard_map/ppermute | solution.py:653
  111.6 22.2 %collective-permute-start.12 = (bf16[1024,512]{1,0:T(8,128)(2,1)}, bf16[1024,512]{1,0:T(8,128)(2,1)S(1)}, u32[]{:S(2)}, u32[]{:S(2)}) collective-permute-start(bf16[1024,512]{1,0:T(8,128)(2,1)} %get-tuple-element.185), channel_id=1, source_target_pairs={{0,1},{1,0},{2,3},{3,2},{4,5},{5,4},{6,7},{7,6},{8,9},{9,8},{10,11... | collective-permute-start | bytes 3145736 | tf_op jit(solution)/shard_map/ppermute | solution.py:649
  113.2 22.6 %collective-permute-start.13 = (bf16[1024,512]{1,0:T(8,128)(2,1)}, bf16[1024,512]{1,0:T(8,128)(2,1)S(1)}, u32[]{:S(2)}, u32[]{:S(2)}) collective-permute-start(bf16[1024,512]{1,0:T(8,128)(2,1)} %get-tuple-element.186), channel_id=1, source_target_pairs={{0,2},{2,0},{1,3},{3,1},{4,6},{6,4},{5,7},{7,5},{8,10},{10,8},{9,1... | collective-permute-start | bytes 3145736 | tf_op jit(solution)/shard_map/ppermute | solution.py:653
  132.5 3.7 %copy-start.11 = (bf16[1024,512]{1,0:T(8,128)(2,1)S(1)}, bf16[1024,512]{1,0:T(8,128)(2,1)}, u32[]{:S(2)}) copy-start(bf16[1024,512]{1,0:T(8,128)(2,1)} %get-tuple-element.188) | copy-start | bytes 3145732
  132.5 3.8 %copy-start.12 = (bf16[1024,512]{1,0:T(8,128)(2,1)S(1)}, bf16[1024,512]{1,0:T(8,128)(2,1)}, u32[]{:S(2)}) copy-start(bf16[1024,512]{1,0:T(8,128)(2,1)} %get-tuple-element.174) | copy-start | bytes 3145732
  133.8 2.1 copy-start.14
  135.9 1.6 copy-start.13
  135.9 88.0 %reduce-scatter.5.cloned.1.call-start = ((), (), s32[]{:S(2)}) async-start(), calls=%async_computation.5 | async-start | bytes 2064384 | tf_op jit(solution)/shard_map/reduce_scatter | solution.py:1091
  137.5 44.8 %collective-permute-start.14 = (bf16[512,512]{1,0:T(8,128)(2,1)S(1)}, bf16[512,512]{1,0:T(8,128)(2,1)}, u32[]{:S(2)}, u32[]{:S(2)}) collective-permute-start(bf16[512,512]{1,0:T(8,128)(2,1)S(1)} %add_convert_fusion.3), channel_id=1, source_target_pairs={{0,2},{2,0},{1,3},{3,1},{4,6},{6,4},{5,7},{7,5},{8,10},{10,8},{9,1... | collective-permute-start | bytes 1572872 | tf_op jit(solution)/shard_map/ppermute | solution.py:653
  138.0 44.3 %collective-permute-start.15 = (bf16[512,512]{1,0:T(8,128)(2,1)S(1)}, bf16[512,512]{1,0:T(8,128)(2,1)}, u32[]{:S(2)}, u32[]{:S(2)}) collective-permute-start(bf16[512,512]{1,0:T(8,128)(2,1)S(1)} %add_convert_fusion.2), channel_id=1, source_target_pairs={{0,1},{1,0},{2,3},{3,2},{4,5},{5,4},{6,7},{7,6},{8,9},{9,8},{10,11... | collective-permute-start | bytes 1572872 | tf_op jit(solution)/shard_map/ppermute | solution.py:649
  182.3 1.2 copy-start
  182.3 4.2 %slice-start = ((f32[8,2048]{1,0:T(8,128)}), f32[1,2048]{1,0:T(1,128)S(1)}, s32[]{:S(2)}) async-start(f32[8,2048]{1,0:T(8,128)} %add.132.refs_5_), calls=%async_computation.6 | async-start | bytes 16384 | tf_op jit(solution)/shard_map/slice | solution.py:1115
  182.3 4.2 %copy-start.21 = (f32[16,1024]{1,0:T(8,128)S(1)}, f32[16,1024]{1,0:T(8,128)}, u32[]{:S(2)}) copy-start(f32[16,1024]{1,0:T(8,128)} %get-tuple-element.213) | copy-start | bytes 196612
  183.8 23.1 %collective-permute-start.20 = (bf16[1024,512]{1,0:T(8,128)(2,1)}, bf16[1024,512]{1,0:T(8,128)(2,1)}, u32[]{:S(2)}, u32[]{:S(2)}) collective-permute-start(bf16[1024,512]{1,0:T(8,128)(2,1)} %get-tuple-element.214), channel_id=1, source_target_pairs={{0,1},{1,0},{2,3},{3,2},{4,5},{5,4},{6,7},{7,6},{8,9},{9,8},{10,11... | collective-permute-start | bytes 3145736 | tf_op jit(solution)/shard_map/ppermute | solution.py:649
  185.0 21.9 %collective-permute-start.21 = (bf16[1024,512]{1,0:T(8,128)(2,1)}, bf16[1024,512]{1,0:T(8,128)(2,1)}, u32[]{:S(2)}, u32[]{:S(2)}) collective-permute-start(bf16[1024,512]{1,0:T(8,128)(2,1)} %get-tuple-element.215), channel_id=1, source_target_pairs={{0,2},{2,0},{1,3},{3,1},{4,6},{6,4},{5,7},{7,5},{8,10},{10,8},{9,1... | collective-permute-start | bytes 3145736 | tf_op jit(solution)/shard_map/ppermute | solution.py:653
  186.6 4.8 %copy-start.15 = (bf16[128,1024]{1,0:T(8,128)(2,1)S(1)}, bf16[128,1024]{1,0:T(8,128)(2,1)}, u32[]{:S(2)}) copy-start(bf16[128,1024]{1,0:T(8,128)(2,1)} %reduce-scatter.3.cloned.1.call-done) | copy-start | bytes 786436
  186.6 1.5 collective-permute-start.16
  188.1 5.2 %collective-permute-start.17 = (f32[16,1024]{1,0:T(8,128)S(1)}, f32[16,1024]{1,0:T(8,128)S(1)}, u32[]{:S(2)}, u32[]{:S(2)}) collective-permute-start(f32[16,1024]{1,0:T(8,128)S(1)} %add.145), channel_id=1, source_target_pairs={{0,8},{4,12},{8,0},{12,4},{16,24},{20,28},{24,16},{28,20},{1,9},{5... | collective-permute-start | bytes 196616 | tf_op jit(solution)/shard_map/ppermute | solution.py:698
  193.3 9.2 %collective-permute-start.18 = (f32[16,1024]{1,0:T(8,128)S(1)}, f32[16,1024]{1,0:T(8,128)S(1)}, u32[]{:S(2)}, u32[]{:S(2)}) collective-permute-start(f32[16,1024]{1,0:T(8,128)S(1)} %add.146), channel_id=1, source_target_pairs={{0,16},{4,20},{8,24},{12,28},{16,0},{20,4},{24,8},{28,12},{1,17},{... | collective-permute-start | bytes 196616 | tf_op jit(solution)/shard_map/ppermute | solution.py:698
  202.5 4.3 %collective-permute-start.19 = (f32[16,1024]{1,0:T(8,128)S(1)}, f32[16,1024]{1,0:T(8,128)S(1)}, u32[]{:S(2)}, u32[]{:S(2)}) collective-permute-start(f32[16,1024]{1,0:T(8,128)S(1)} %add.147), channel_id=1, source_target_pairs={{0,1},{1,0},{2,3},{3,2},{4,5},{5,4},{6,7},{7,6},{8,9},{9,8},{10,11... | collective-permute-start | bytes 196616 | tf_op jit(solution)/shard_map/ppermute | solution.py:649
  202.7 6.0 %copy-start.9 = (bf16[1024,512]{1,0:T(8,128)(2,1)S(1)}, bf16[1024,512]{1,0:T(8,128)(2,1)}, u32[]{:S(2)}) copy-start(bf16[1024,512]{1,0:T(8,128)(2,1)} %get-tuple-element.212) | copy-start | bytes 3145732
  206.9 4.3 %collective-permute-start.22 = (f32[16,1024]{1,0:T(8,128)S(1)}, f32[16,1024]{1,0:T(8,128)S(1)}, u32[]{:S(2)}, u32[]{:S(2)}) collective-permute-start(f32[16,1024]{1,0:T(8,128)S(1)} %add.148), channel_id=1, source_target_pairs={{0,2},{2,0},{1,3},{3,1},{4,6},{6,4},{5,7},{7,5},{8,10},{10,8},{9,1... | collective-permute-start | bytes 196616 | tf_op jit(solution)/shard_map/ppermute | solution.py:653
  211.2 12.1 %collective-permute-start.23 = (bf16[512,512]{1,0:T(8,128)(2,1)S(1)}, bf16[512,512]{1,0:T(8,128)(2,1)}, u32[]{:S(2)}, u32[]{:S(2)}) collective-permute-start(bf16[512,512]{1,0:T(8,128)(2,1)S(1)} %add_convert_fusion.1), channel_id=1, source_target_pairs={{0,2},{2,0},{1,3},{3,1},{4,6},{6,4},{5,7},{7,5},{8,10},{10,8},{9,1... | collective-permute-start | bytes 1572872 | tf_op jit(solution)/shard_map/ppermute | solution.py:653
  211.7 12.2 %collective-permute-start.24 = (bf16[512,512]{1,0:T(8,128)(2,1)S(1)}, bf16[512,512]{1,0:T(8,128)(2,1)}, u32[]{:S(2)}, u32[]{:S(2)}) collective-permute-start(bf16[512,512]{1,0:T(8,128)(2,1)S(1)} %add_convert_fusion), channel_id=1, source_target_pairs={{0,1},{1,0},{2,3},{3,2},{4,5},{5,4},{6,7},{7,6},{8,9},{9,8},{10,11... | collective-permute-start | bytes 1572872 | tf_op jit(solution)/shard_map/ppermute | solution.py:649
  223.9 3.7 %copy-start.10 = (bf16[1024,512]{1,0:T(8,128)(2,1)S(1)}, bf16[1024,512]{1,0:T(8,128)(2,1)}, u32[]{:S(2)}) copy-start(bf16[1024,512]{1,0:T(8,128)(2,1)} %get-tuple-element.212) | copy-start | bytes 3145732
  224.9 4.1 %copy-start.18 = (bf16[128,896]{1,0:T(8,128)(2,1)S(1)}, bf16[128,896]{1,0:T(8,128)(2,1)}, u32[]{:S(2)}) copy-start(bf16[128,896]{1,0:T(8,128)(2,1)} %reduce-scatter.5.cloned.1.call-done) | copy-start | bytes 688132
  224.9 4.8 %collective-permute-start.25 = (bf16[128,384]{1,0:T(8,128)(2,1)S(1)}, bf16[128,384]{1,0:T(8,128)(2,1)S(1)}, u32[]{:S(2)}, u32[]{:S(2)}) collective-permute-start(bf16[128,384]{1,0:T(8,128)(2,1)S(1)} %slice.136), channel_id=1, source_target_pairs={{0,1},{1,0},{2,3},{3,2},{4,5},{5,4},{6,7},{7,6},{8,9},{9,8},{10,11... | collective-permute-start | bytes 294920 | tf_op jit(solution)/shard_map/ppermute | solution.py:649
  227.6 3.5 %copy-start.20 = (f32[1,1024]{1,0:T(1,128)S(1)}, f32[1,1024]{1,0:T(1,128)}, u32[]{:S(2)}) copy-start(f32[1,1024]{1,0:T(1,128)} %get-tuple-element.136.refs_8_.refs_1_) | copy-start | bytes 12292
  229.0 2.6 %copy-start.2 = (bf16[512,1024]{1,0:T(8,128)(2,1)S(1)}, bf16[512,1024]{1,0:T(8,128)(2,1)}, u32[]{:S(2)}) copy-start(bf16[512,1024]{1,0:T(8,128)(2,1)} %refs_0_.3) | copy-start | bytes 3145732
  229.8 4.7 %collective-permute-start.26 = (bf16[128,384]{1,0:T(8,128)(2,1)S(1)}, bf16[128,384]{1,0:T(8,128)(2,1)S(1)}, u32[]{:S(2)}, u32[]{:S(2)}) collective-permute-start(bf16[128,384]{1,0:T(8,128)(2,1)S(1)} %add_convert_fusion.4), channel_id=1, source_target_pairs={{0,2},{2,0},{1,3},{3,1},{4,6},{6,4},{5,7},{7,5},{8,10},{10,8},{9,1... | collective-permute-start | bytes 294920 | tf_op jit(solution)/shard_map/ppermute | solution.py:653
Sparse Core Ops, SparseCore 0:
  10.3 39.0 all-gather.2
  51.6 20.9 all-gather.4
  136.0 34.8 reduce-scatter.2
  182.5 37.6 reduce-scatter.4

commit v6 on v5

--- a/solution.py
+++ b/solution.py
@@ -473,8 +473,8 @@
 
     @pl.when(step_id == 0)
     def _():
-        dbuf[rows : rows + 8, :] = jnp.zeros((8, channels), f32)
-        dsbuf[rows : rows + 8, :] = jnp.zeros((8, 2 * STATE), f32)
+        dbuf[...] = jnp.zeros_like(dbuf)
+        dsbuf[...] = jnp.zeros_like(dsbuf)
         carry[...] = jnp.zeros_like(carry)
         ending[...] = jnp.zeros_like(ending)
         dprm_ref[...] = jnp.zeros_like(dprm_ref)
@@ -572,17 +572,25 @@
     usable = [None] + [segment_of(places + lag, ends) == segment for lag in range(1, taps)]
     normed = normed_ref[...]
 
-    def conv_back(du, v, weight_ref, buffer, sums_ref):
-        buffer[0:rows, :] = du
+    line = lax.broadcasted_iota(jnp.int32, (rows, 1), 0)
+
+    def conv_back(du, v, weight_ref, tail_ref, sums_ref):
+        edge = jnp.concatenate([du[rows - 8 :], tail_ref[...]], axis=0)
         dv = weight_ref[taps - 1 : taps, :] * du
+        edge_dv = jnp.zeros((8, du.shape[1]), f32)
         lines = [jnp.sum(du * v, axis=0, keepdims=True), jnp.sum(du, axis=0, keepdims=True)]
         for lag in range(1, taps):
-            later = jnp.where(usable[lag], buffer[lag : lag + rows, :], 0.0)
-            dv = dv + weight_ref[taps - 1 - lag : taps - lag, :] * later
-            lines.insert(0, jnp.sum(later * v, axis=0, keepdims=True))
-        buffer[rows : rows + 8, :] = buffer[0:8, :]
+            weight = weight_ref[taps - 1 - lag : taps - lag, :]
+            later = jnp.where(usable[lag] & (line < rows - lag), pltpu.roll(du, rows - lag, 0), 0.0)
+            inside = usable[lag][rows - 8 :] & (line[:8] >= 8 - lag)
+            edge_later = jnp.where(inside, edge[lag : lag + 8], 0.0)
+            dv = dv + weight * later
+            edge_dv = edge_dv + weight * edge_later
+            total_line = jnp.sum(later * v, axis=0, keepdims=True)
+            lines.insert(0, total_line + jnp.sum(edge_later * v[rows - 8 :], axis=0, keepdims=True))
+        tail_ref[...] = du[0:8]
         sums_ref[0 : taps + 1, :] += jnp.concatenate(lines, axis=0)
-        return dv.astype(bf16)
+        return jnp.concatenate([dv[: rows - 8], dv[rows - 8 :] + edge_dv], axis=0).astype(bf16)
 
     product = nt(dgate_ref[...], w_ref[:, :channels])
     du = (step_w * dstepped + skip * dy) * sig_u * (1.0 + u * (1.0 - sig_u))
@@ -939,8 +947,8 @@
             + [self.rows(z, ROWS, True) for z in saved],
             halves + [self.whole(z) for z in shapes],
             [
-                pltpu.VMEM((ROWS + 8, channels), f32),
-                pltpu.VMEM((ROWS + 8, 2 * STATE), f32),
+                pltpu.VMEM((8, channels), f32),
+                pltpu.VMEM((8, 2 * STATE), f32),
                 pltpu.VMEM((STATE, channels), f32),
                 pltpu.VMEM((8, channels), f32),
                 pltpu.VMEM((self.width, gradients), f32),

time: 242 us -> 242 us (level)
  no operation moved by 1% of the time
where the time goes in v6:
time: 242 us; the launch traced here: 241 us
  Pallas kernels  112 us (46%)
  waiting for transfers between devices  35.6 us (15%)
  starting transfers between devices  31.2 us (13%)
  other arithmetic  16.8 us (7%)
  local copies, waits for them, and re-layouts  15.9 us (7%)
  between operations  15.1 us (6%)
  blocking collectives  14.2 us (6%)
    pallas_call x7, Pallas kernels, call(): pl.pallas_call(kernel, grid_spec=pltpu.PrefetchScalarGridSpec(num_scalar_...  112 us
    ppermute x12, waiting for transfers between devices, over_y(): return lax.ppermute(z, 'tensor', [(0, 2), (2, 0), (1, 3), (3, 1)])  24.6 us
    all_gather x1, blocking collectives, per_device(): packed = lax.all_gather(packed, 'dp', axis=1, tiled=True)  14.2 us
    ppermute x12, starting transfers between devices, over_x(): return lax.ppermute(z, 'tensor', [(0, 1), (1, 0), (2, 3), (3, 2)])  14.1 us
    ppermute x12, starting transfers between devices, over_y(): return lax.ppermute(z, 'tensor', [(0, 2), (2, 0), (1, 3), (3, 1)])  11.5 us
    ppermute x3, waiting for transfers between devices, sum_over_dp(): z = z + lax.ppermute(z, 'dp', [(i, i ^ bit) for i in range(count)])  6.02 us
    ppermute x3, starting transfers between devices, sum_over_dp(): z = z + lax.ppermute(z, 'dp', [(i, i ^ bit) for i in range(count)])  5.17 us
    unnamed x67, local copies, waits for them, and re-layouts  4.91 us
  transfers between devices with their start and end apart: 31, of which 13 were waited for; matrix products, arithmetic and copies ran while one was open for 11% of the time, Pallas kernels for 43%

profile of v6, /device:TPU:0, one launch (start us, length us, event | category | flops | bytes accessed | tf_op | source)
XLA Modules:
  0.0 241.0 jit_solution(6146852255434996150)
XLA Ops:
  7.3 1.1 copy.48
  8.5 1.7 fusion.9
  10.3 2.2 fusion.25
  12.5 2.9 %collective-permute-start = (bf16[512,512]{1,0:T(8,128)(2,1)}, bf16[512,512]{1,0:T(8,128)(2,1)S(1)}, u32[]{:S(2)}, u32[]{:S(2)}) collective-permute-start(bf16[512,512]{1,0:T(8,128)(2,1)} %get-tuple-element.249), channel_id=1, source_target_pairs={{0,1},{1,0},{2,3},{3,2},{4,5},{5,4},{6,7},{7,6},{8,9},{9,8},{10,11... | collective-permute-start | bytes 1572872 | tf_op jit(solution)/shard_map/ppermute | solution.py:657
  15.5 1.5 collective-permute-start.1
  17.0 0.5 collective-permute-start.2
  18.0 14.2 %all_gather.9.packed_ref = bf16[16,1024]{1,0:T(8,128)(2,1)} all-gather(bf16[16,128]{1,0:T(8,128)(2,1)S(1)} %fusion.16), channel_id=1, replica_groups=mesh['dp'=8,'tensor'=4] {'dp'}, dimensions={1}, use_global_device_ids=true | all-gather | bytes 36864 | tf_op jit(solution)/shard_map/all_gather | solution.py:1020
  32.2 1.4 collective-permute-start.4
  33.6 1.5 collective-permute-start.5
  35.2 0.8 copy.49
  36.0 1.3 constant_dynamic-slice_fusion.5
  37.3 2.2 parameter_kernel.1
  39.6 2.1 collective-permute-done.3.refs_3_
  41.7 9.9 %collective-permute-done.4.refs_5_ = bf16[512,512]{1,0:T(8,128)(2,1)} collective-permute-done((bf16[512,512]{1,0:T(8,128)(2,1)S(1)}, bf16[512,512]{1,0:T(8,128)(2,1)}, u32[]{:S(2)}, u32[]{:S(2)}) %collective-permute-start.4) | collective-permute-done | bytes 524320 | tf_op jit(solution)/shard_map/ppermute | solution.py:661
  52.0 1.7 collective-permute-start.7
  54.5 23.2 %scan_kernel.2 = (bf16[2048,1024]{1,0:T(8,128)(2,1)}, bf16[2048,512]{1,0:T(8,128)(2,1)}, f32[2048,512]{1,0:T(8,128)}, bf16[2048,256]{1,0:T(8,128)(2,1)}, f32[204...) custom-call(s32[1,1]{1,0:T(1,128)S(6)} %copy.63.len_ref, ...), custom_call_target="tpu_custom_call" | custom-call | flops 1000 | bytes 1000 | tf_op jit(solution)/shard_map/scan_kernel/pallas_call | solution.py:746
  77.8 0.9 slice.117
  78.7 0.8 slice.118
  79.8 1.7 collective-permute-start.9
  81.5 11.2 %scan_kernel.3 = (bf16[2048,1024]{1,0:T(8,128)(2,1)}, bf16[2048,512]{1,0:T(8,128)(2,1)}, f32[2048,512]{1,0:T(8,128)}, bf16[2048,256]{1,0:T(8,128)(2,1)}, f32[204...) custom-call(s32[1,1]{1,0:T(1,128)S(6)} %copy.63.len_ref, ...), custom_call_target="tpu_custom_call", output_to_operand_aliasing={{0}: (20, {}), {1}: (21, {}), {2}: (22, {}), {3}: (23, {}),... | custom-call | flops 1000 | bytes 1000 | tf_op jit(solution)/shard_map/scan_kernel/pallas_call | solution.py:746
  92.8 0.8 copy-done.16
  93.7 8.3 %cotangent_kernel.1 = (bf16[2048,512]{1,0:T(8,128)(2,1)}, f32[8,2048]{1,0:T(8,128)}) custom-call(s32[216]{0:T(256)} %bitcast.31, bf16[512,1024]{1,0:T(8,128)(2,1)} %refs_0_.3, bf16[512,1024]{1,0:T(8,128)(2,1)} %copy-done.3, bf16[512,1024]{1,0:T(8,128)(2,1)} %copy-done.4, bf16[512,512]{1,0:T(8,128)(2,1)} %copy-done.16, bf16[512,512]{1,0:T(8,128)(2,1)} %copy-done.17, ...), custom_call_target="tpu_custom_call" | custom-call | flops 1000 | bytes 1000 | tf_op jit(solution)/shard_map/cotangent_kernel/pallas_call | solution.py:746
  102.5 7.4 %product_kernel.1 = (bf16[1024,512]{1,0:T(8,128)(2,1)}, bf16[1024,512]{1,0:T(8,128)(2,1)}, bf16[1024,512]{1,0:T(8,128)(2,1)}, bf16[1024,512]{1,0:T(8,128)(2,1)}) custom-call(s32[216]{0:T(256)} %bitcast.32, bf16[2048,512]{1,0:T(8,128)(2,1)} %get-tuple-element.169.refs_6_.ga_ref, bf16[1024,512]{1,0:T(8,128)(2,1)} %all-gather.5.cloned.1.call-done.refs_5_.w_ref), custom_call_target="tpu_custom_call" | custom-call | flops 1000 | bytes 1000 | tf_op jit(solution)/shard_map/product_kernel/pallas_call | solution.py:746
  109.9 1.6 collective-permute-start.11
  111.6 1.6 collective-permute-start.12
  113.7 1.3 collective-permute-done.11
  115.0 0.6 add.132.refs_5_
  115.6 16.9 %gate_kernel.1 = (bf16[2048,512]{1,0:T(8,128)(2,1)}, f32[2048,512]{1,0:T(8,128)}, f32[8,512]{1,0:T(8,128)}, bf16[1024,1024]{1,0:T(8,128)(2,1)}, f32[8,1024]{1,0:T(8,128)}) custom-call(s32[216]{0:T(256)} %bitcast.33, bf16[512,1024]{1,0:T(8,128)(2,1)} %refs_0_.3, bf16[512,1024]{1,0:T(8,128)(2,1)} %copy-done.3, bf16[512,1024]{1,0:T(8,128)(2,1)} %copy-done.4, ...), custom_call_target="tpu_custom_call" | custom-call | flops 34359738368 | bytes 1000 | tf_op jit(solution)/shard_map/gate_kernel/pallas_call | solution.py:746
  132.5 1.3 collective-permute-done.12
  133.8 2.1 collective-permute-done.13
  136.3 1.2 add_convert_fusion.3
  137.5 0.5 collective-permute-start.14
  138.0 0.9 collective-permute-start.15
  138.9 43.1 %backward_kernel.1 = (bf16[1024,512]{1,0:T(8,128)(2,1)}, bf16[1024,512]{1,0:T(8,128)(2,1)}, bf16[1024,512]{1,0:T(8,128)(2,1)}, bf16[1024,512]{1,0:T(8,128)(2,1)}...) custom-call(s32[1,1]{1,0:T(1,128)S(6)} %copy.63.len_ref, ...), custom_call_target="tpu_custom_call" | custom-call | flops 1000 | bytes 1000 | tf_op jit(solution)/shard_map/backward_kernel/pallas_call | solution.py:746
  182.1 1.1 copy-done
  183.5 1.2 collective-permute-start.20
  184.7 1.5 collective-permute-start.21
  186.4 1.4 convert_add_fusion.4
  187.8 1.7 collective-permute-start.17
  189.5 1.6 convert_add_fusion.3
  191.1 1.9 collective-permute-done.17
  193.0 3.4 %collective-permute-start.18 = (f32[16,1024]{1,0:T(8,128)S(1)}, f32[16,1024]{1,0:T(8,128)S(1)}, u32[]{:S(2)}, u32[]{:S(2)}) collective-permute-start(f32[16,1024]{1,0:T(8,128)S(1)} %add.146), channel_id=1, source_target_pairs={{0,16},{4,20},{8,24},{12,28},{16,0},{20,4},{24,8},{28,12},{1,17},{... | collective-permute-start | bytes 196616 | tf_op jit(solution)/shard_map/ppermute | solution.py:706
  196.5 0.7 slice.154
  197.2 0.8 copy.50
  198.0 4.1 %collective-permute-done.18 = f32[16,1024]{1,0:T(8,128)S(1)} collective-permute-done((f32[16,1024]{1,0:T(8,128)S(1)}, f32[16,1024]{1,0:T(8,128)S(1)}, u32[]{:S(2)}, u32[]{:S(2)}) %collective-permute-start.18) | collective-permute-done | bytes 65568 | tf_op jit(solution)/shard_map/ppermute | solution.py:706
  202.3 0.7 constant_dynamic-slice_fusion
  203.0 0.7 dynamic-slice_bitcast_fusion
  203.7 2.8 %collective-permute-done.19 = f32[16,1024]{1,0:T(8,128)S(1)} collective-permute-done((f32[16,1024]{1,0:T(8,128)S(1)}, f32[16,1024]{1,0:T(8,128)S(1)}, u32[]{:S(2)}, u32[]{:S(2)}) %collective-permute-start.19) | collective-permute-done | bytes 65568 | tf_op jit(solution)/shard_map/ppermute | solution.py:657
  207.0 1.3 add_convert_fusion
  208.4 1.2 add_convert_fusion.1
  209.6 1.3 collective-permute-done.22
  211.4 1.7 collective-permute-start.24
  213.2 0.6 slice.146
  213.8 0.6 fusion.24
  215.4 7.3 %collective-permute-done.23 = bf16[512,512]{1,0:T(8,128)(2,1)} collective-permute-done((bf16[512,512]{1,0:T(8,128)(2,1)S(1)}, bf16[512,512]{1,0:T(8,128)(2,1)}, u32[]{:S(2)}, u32[]{:S(2)}) %collective-permute-start.23) | collective-permute-done | bytes 524320 | tf_op jit(solution)/shard_map/ppermute | solution.py:661
  223.3 1.0 slice.136
  224.3 1.1 collective-permute-start.25
  225.4 1.5 convert_add_fusion.1
  227.0 1.4 convert_add_fusion.2
  228.4 0.7 slice_convert_fusion
  229.2 1.3 collective-permute-start.26
  231.0 2.2 fusion.5
  233.2 0.7 collective-permute-done.26
  233.9 0.6 convert_add_fusion.5
  (131 shorter events, 7.1 us)
Async XLA Ops:
  7.2 10.3 %copy-start.24 = (bf16[8,8]{1,0:T(8,128)(2,1)S(1)}, bf16[8,8]{1,0:T(8,128)(2,1)}, u32[]{:S(2)}) copy-start(bf16[8,8]{1,0:T(8,128)(2,1)} %param.27) | copy-start | bytes 388
  7.2 10.4 %copy-start.25 = (bf16[8,8]{1,0:T(8,128)(2,1)S(1)}, bf16[8,8]{1,0:T(8,128)(2,1)}, u32[]{:S(2)}) copy-start(bf16[8,8]{1,0:T(8,128)(2,1)} %param.33) | copy-start | bytes 388
  7.2 10.5 %copy-start.23 = (bf16[4,8,8]{2,1,0:T(8,128)(2,1)S(1)}, bf16[4,8,8]{2,1,0:T(8,128)(2,1)}, u32[]{:S(2)}) copy-start(bf16[4,8,8]{2,1,0:T(8,128)(2,1)} %param.26) | copy-start | bytes 1540
  7.2 10.6 %copy-start.26 = (bf16[4,32]{1,0:T(4,128)(2,1)S(1)}, bf16[4,32]{1,0:T(4,128)(2,1)}, u32[]{:S(2)}) copy-start(bf16[4,32]{1,0:T(4,128)(2,1)} %param.28) | copy-start | bytes 772
  7.2 10.6 %copy-start.27 = (bf16[32]{0:T(256)(128)(2,1)S(1)}, bf16[32]{0:T(256)(128)(2,1)}, u32[]{:S(2)}) copy-start(bf16[32]{0:T(256)(128)(2,1)} %param.29) | copy-start | bytes 196
  7.2 10.6 %copy-start.30 = (bf16[4]{0:T(256)(128)(2,1)S(1)}, bf16[4]{0:T(256)(128)(2,1)}, u32[]{:S(2)}) copy-start(bf16[4]{0:T(256)(128)(2,1)} %param.30) | copy-start | bytes 28
  7.2 10.6 %copy-start.29 = (bf16[4]{0:T(256)(128)(2,1)S(1)}, bf16[4]{0:T(256)(128)(2,1)}, u32[]{:S(2)}) copy-start(bf16[4]{0:T(256)(128)(2,1)} %param.31) | copy-start | bytes 28
  7.3 10.6 %copy-start.28 = (bf16[4]{0:T(256)(128)(2,1)S(1)}, bf16[4]{0:T(256)(128)(2,1)}, u32[]{:S(2)}) copy-start(bf16[4]{0:T(256)(128)(2,1)} %param.32) | copy-start | bytes 28
  7.3 10.7 %copy-start.31 = (bf16[128]{0:T(256)(128)(2,1)S(1)}, bf16[128]{0:T(256)(128)(2,1)}, u32[]{:S(2)}) copy-start(bf16[128]{0:T(256)(128)(2,1)} %param.22) | copy-start | bytes 772
  7.3 27.9 %copy-start.19 = (bf16[512,128]{1,0:T(8,128)(2,1)S(1)}, bf16[512,128]{1,0:T(8,128)(2,1)}, u32[]{:S(2)}) copy-start(bf16[512,128]{1,0:T(8,128)(2,1)} %param.34) | copy-start | bytes 393220
  7.3 44.4 %copy-start.1 = (bf16[512,1024]{1,0:T(8,128)(2,1)S(1)}, bf16[512,1024]{1,0:T(8,128)(2,1)}, u32[]{:S(2)}) copy-start(bf16[512,1024]{1,0:T(8,128)(2,1)} %refs_0_.3) | copy-start | bytes 3145732
  7.3 47.2 %all-gather.3.cloned.1.call-start = ((), (), s32[]{:S(2)}) async-start(), calls=%async_computation.2 | async-start | bytes 3244032 | tf_op jit(solution)/shard_map/all_gather | solution.py:993
  10.2 82.5 %all-gather.5.cloned.1.call-start = ((), (), s32[]{:S(2)}) async-start(), calls=%async_computation.3 | async-start | bytes 1179648 | tf_op jit(solution)/shard_map/all_gather | solution.py:996
  12.5 19.7 %collective-permute-start = (bf16[512,512]{1,0:T(8,128)(2,1)}, bf16[512,512]{1,0:T(8,128)(2,1)S(1)}, u32[]{:S(2)}, u32[]{:S(2)}) collective-permute-start(bf16[512,512]{1,0:T(8,128)(2,1)} %get-tuple-element.249), channel_id=1, source_target_pairs={{0,1},{1,0},{2,3},{3,2},{4,5},{5,4},{6,7},{7,6},{8,9},{9,8},{10,11... | collective-permute-start | bytes 1572872 | tf_op jit(solution)/shard_map/ppermute | solution.py:657
  15.5 16.8 %collective-permute-start.1 = (bf16[512,512]{1,0:T(8,128)(2,1)}, bf16[512,512]{1,0:T(8,128)(2,1)S(1)}, u32[]{:S(2)}, u32[]{:S(2)}) collective-permute-start(bf16[512,512]{1,0:T(8,128)(2,1)} %get-tuple-element.248), channel_id=1, source_target_pairs={{0,2},{2,0},{1,3},{3,1},{4,6},{6,4},{5,7},{7,5},{8,10},{10,8},{9,1... | collective-permute-start | bytes 1572872 | tf_op jit(solution)/shard_map/ppermute | solution.py:661
  17.0 22.7 %collective-permute-start.2 = (bf16[512,512]{1,0:T(8,128)(2,1)}, bf16[512,512]{1,0:T(8,128)(2,1)S(1)}, u32[]{:S(2)}, u32[]{:S(2)}) collective-permute-start(bf16[512,512]{1,0:T(8,128)(2,1)} %get-tuple-element.248), channel_id=1, source_target_pairs={{0,1},{1,0},{2,3},{3,2},{4,5},{5,4},{6,7},{7,6},{8,9},{9,8},{10,11... | collective-permute-start | bytes 1572872 | tf_op jit(solution)/shard_map/ppermute | solution.py:657
  17.5 24.2 %collective-permute-start.3 = (bf16[512,512]{1,0:T(8,128)(2,1)}, bf16[512,512]{1,0:T(8,128)(2,1)S(1)}, u32[]{:S(2)}, u32[]{:S(2)}) collective-permute-start(bf16[512,512]{1,0:T(8,128)(2,1)} %get-tuple-element.249), channel_id=1, source_target_pairs={{0,2},{2,0},{1,3},{3,1},{4,6},{6,4},{5,7},{7,5},{8,10},{10,8},{9,1... | collective-permute-start | bytes 1572872 | tf_op jit(solution)/shard_map/ppermute | solution.py:661
  32.2 19.4 %copy-start.5 = (bf16[512,512]{1,0:T(8,128)(2,1)}, bf16[512,512]{1,0:T(8,128)(2,1)S(1)}, u32[]{:S(2)}) copy-start(bf16[512,512]{1,0:T(8,128)(2,1)S(1)} %collective-permute-done.refs_1_) | copy-start | bytes 1572868
  32.2 19.4 %copy-start.6 = (bf16[512,512]{1,0:T(8,128)(2,1)}, bf16[512,512]{1,0:T(8,128)(2,1)S(1)}, u32[]{:S(2)}) copy-start(bf16[512,512]{1,0:T(8,128)(2,1)S(1)} %collective-permute-done.1.refs_4_) | copy-start | bytes 1572868
  32.2 19.4 %collective-permute-start.4 = (bf16[512,512]{1,0:T(8,128)(2,1)S(1)}, bf16[512,512]{1,0:T(8,128)(2,1)}, u32[]{:S(2)}, u32[]{:S(2)}) collective-permute-start(bf16[512,512]{1,0:T(8,128)(2,1)S(1)} %collective-permute-done.refs_1_), channel_id=1, source_target_pairs={{0,2},{2,0},{1,3},{3,1},{4,6},{6,4},{5,7},{7,5},{8,10},{10,8},{9,1... | collective-permute-start | bytes 1572872 | tf_op jit(solution)/shard_map/ppermute | solution.py:661
  33.6 18.0 %collective-permute-start.5 = (bf16[512,512]{1,0:T(8,128)(2,1)S(1)}, bf16[512,512]{1,0:T(8,128)(2,1)}, u32[]{:S(2)}, u32[]{:S(2)}) collective-permute-start(bf16[512,512]{1,0:T(8,128)(2,1)S(1)} %collective-permute-done.1.refs_4_), channel_id=1, source_target_pairs={{0,1},{1,0},{2,3},{3,2},{4,5},{5,4},{6,7},{7,6},{8,9},{9,8},{10,11... | collective-permute-start | bytes 1572872 | tf_op jit(solution)/shard_map/ppermute | solution.py:657
  36.0 146.1 %reduce-scatter.3.cloned.1.call-start = ((), (), s32[]{:S(2)}) async-start(), calls=%async_computation.4 | async-start | bytes 2359296 | tf_op jit(solution)/shard_map/reduce_scatter | solution.py:1077
  39.6 12.0 %copy-start.7 = (bf16[512,512]{1,0:T(8,128)(2,1)}, bf16[512,512]{1,0:T(8,128)(2,1)S(1)}, u32[]{:S(2)}) copy-start(bf16[512,512]{1,0:T(8,128)(2,1)S(1)} %collective-permute-done.2.refs_2_) | copy-start | bytes 1572868
  41.7 9.9 %copy-start.8 = (bf16[512,512]{1,0:T(8,128)(2,1)}, bf16[512,512]{1,0:T(8,128)(2,1)S(1)}, u32[]{:S(2)}) copy-start(bf16[512,512]{1,0:T(8,128)(2,1)S(1)} %collective-permute-done.3.refs_3_) | copy-start | bytes 1572868
  51.7 26.0 %collective-permute-start.6 = (bf16[512,1024]{1,0:T(8,128)(2,1)S(1)}, bf16[512,1024]{1,0:T(8,128)(2,1)S(1)}, u32[]{:S(2)}, u32[]{:S(2)}) collective-permute-start(bf16[512,1024]{1,0:T(8,128)(2,1)S(1)} %copy-done.1), channel_id=1, source_target_pairs={{0,1},{1,0},{2,3},{3,2},{4,5},{5,4},{6,7},{7,6},{8,9},{9,8},{10,11... | collective-permute-start | bytes 3145736 | tf_op jit(solution)/shard_map/ppermute | solution.py:657
  52.0 25.7 %collective-permute-start.7 = (bf16[512,1024]{1,0:T(8,128)(2,1)S(1)}, bf16[512,1024]{1,0:T(8,128)(2,1)S(1)}, u32[]{:S(2)}, u32[]{:S(2)}) collective-permute-start(bf16[512,1024]{1,0:T(8,128)(2,1)S(1)} %copy-done.1), channel_id=1, source_target_pairs={{0,2},{2,0},{1,3},{3,1},{4,6},{6,4},{5,7},{7,5},{8,10},{10,8},{9,1... | collective-permute-start | bytes 3145736 | tf_op jit(solution)/shard_map/ppermute | solution.py:661
  77.7 15.0 %copy-start.3 = (bf16[512,1024]{1,0:T(8,128)(2,1)}, bf16[512,1024]{1,0:T(8,128)(2,1)S(1)}, u32[]{:S(2)}) copy-start(bf16[512,1024]{1,0:T(8,128)(2,1)S(1)} %collective-permute-done.6.refs_1_) | copy-start | bytes 3145732
  77.7 15.0 %copy-start.4 = (bf16[512,1024]{1,0:T(8,128)(2,1)}, bf16[512,1024]{1,0:T(8,128)(2,1)S(1)}, u32[]{:S(2)}) copy-start(bf16[512,1024]{1,0:T(8,128)(2,1)S(1)} %collective-permute-done.7.refs_2_) | copy-start | bytes 3145732
  79.5 13.2 %collective-permute-start.8 = (bf16[512,512]{1,0:T(8,128)(2,1)}, bf16[512,512]{1,0:T(8,128)(2,1)S(1)}, u32[]{:S(2)}, u32[]{:S(2)}) collective-permute-start(bf16[512,512]{1,0:T(8,128)(2,1)} %slice.117), channel_id=1, source_target_pairs={{0,2},{2,0},{1,3},{3,1},{4,6},{6,4},{5,7},{7,5},{8,10},{10,8},{9,1... | collective-permute-start | bytes 1572872 | tf_op jit(solution)/shard_map/ppermute | solution.py:661
  79.8 13.0 %collective-permute-start.9 = (bf16[512,512]{1,0:T(8,128)(2,1)}, bf16[512,512]{1,0:T(8,128)(2,1)S(1)}, u32[]{:S(2)}, u32[]{:S(2)}) collective-permute-start(bf16[512,512]{1,0:T(8,128)(2,1)} %slice.118), channel_id=1, source_target_pairs={{0,1},{1,0},{2,3},{3,2},{4,5},{5,4},{6,7},{7,6},{8,9},{9,8},{10,11... | collective-permute-start | bytes 1572872 | tf_op jit(solution)/shard_map/ppermute | solution.py:657
  92.8 0.8 copy-start.16
  92.8 1.0 copy-start.17
  102.1 7.8 %copy-start.22 = (f32[8,2048]{1,0:T(8,128)S(1)}, f32[8,2048]{1,0:T(8,128)}, u32[]{:S(2)}) copy-start(f32[8,2048]{1,0:T(8,128)} %get-tuple-element.167) | copy-start | bytes 196612
  102.1 7.8 %collective-permute-start.10 = (f32[8,2048]{1,0:T(8,128)}, f32[8,2048]{1,0:T(8,128)S(1)}, u32[]{:S(2)}, u32[]{:S(2)}) collective-permute-start(f32[8,2048]{1,0:T(8,128)} %get-tuple-element.167), channel_id=1, source_target_pairs={{0,1},{1,0},{2,3},{3,2},{4,5},{5,4},{6,7},{7,6},{8,9},{9,8},{10,11... | collective-permute-start | bytes 196616 | tf_op jit(solution)/shard_map/ppermute | solution.py:657
  109.9 5.0 %collective-permute-start.11 = (f32[8,2048]{1,0:T(8,128)S(1)}, f32[8,2048]{1,0:T(8,128)S(1)}, u32[]{:S(2)}, u32[]{:S(2)}) collective-permute-start(f32[8,2048]{1,0:T(8,128)S(1)} %add.131), channel_id=1, source_target_pairs={{0,2},{2,0},{1,3},{3,1},{4,6},{6,4},{5,7},{7,5},{8,10},{10,8},{9,1... | collective-permute-start | bytes 196616 | tf_op jit(solution)/shard_map/ppermute | solution.py:661
  111.6 22.2 %collective-permute-start.12 = (bf16[1024,512]{1,0:T(8,128)(2,1)}, bf16[1024,512]{1,0:T(8,128)(2,1)S(1)}, u32[]{:S(2)}, u32[]{:S(2)}) collective-permute-start(bf16[1024,512]{1,0:T(8,128)(2,1)} %get-tuple-element.185), channel_id=1, source_target_pairs={{0,1},{1,0},{2,3},{3,2},{4,5},{5,4},{6,7},{7,6},{8,9},{9,8},{10,11... | collective-permute-start | bytes 3145736 | tf_op jit(solution)/shard_map/ppermute | solution.py:657
  113.2 22.6 %collective-permute-start.13 = (bf16[1024,512]{1,0:T(8,128)(2,1)}, bf16[1024,512]{1,0:T(8,128)(2,1)S(1)}, u32[]{:S(2)}, u32[]{:S(2)}) collective-permute-start(bf16[1024,512]{1,0:T(8,128)(2,1)} %get-tuple-element.186), channel_id=1, source_target_pairs={{0,2},{2,0},{1,3},{3,1},{4,6},{6,4},{5,7},{7,5},{8,10},{10,8},{9,1... | collective-permute-start | bytes 3145736 | tf_op jit(solution)/shard_map/ppermute | solution.py:661
  132.5 3.7 %copy-start.11 = (bf16[1024,512]{1,0:T(8,128)(2,1)S(1)}, bf16[1024,512]{1,0:T(8,128)(2,1)}, u32[]{:S(2)}) copy-start(bf16[1024,512]{1,0:T(8,128)(2,1)} %get-tuple-element.188) | copy-start | bytes 3145732
  132.5 3.8 %copy-start.12 = (bf16[1024,512]{1,0:T(8,128)(2,1)S(1)}, bf16[1024,512]{1,0:T(8,128)(2,1)}, u32[]{:S(2)}) copy-start(bf16[1024,512]{1,0:T(8,128)(2,1)} %get-tuple-element.174) | copy-start | bytes 3145732
  133.8 2.1 copy-start.14
  135.9 1.6 copy-start.13
  135.9 87.4 %reduce-scatter.5.cloned.1.call-start = ((), (), s32[]{:S(2)}) async-start(), calls=%async_computation.5 | async-start | bytes 2064384 | tf_op jit(solution)/shard_map/reduce_scatter | solution.py:1099
  137.5 44.5 %collective-permute-start.14 = (bf16[512,512]{1,0:T(8,128)(2,1)S(1)}, bf16[512,512]{1,0:T(8,128)(2,1)}, u32[]{:S(2)}, u32[]{:S(2)}) collective-permute-start(bf16[512,512]{1,0:T(8,128)(2,1)S(1)} %add_convert_fusion.3), channel_id=1, source_target_pairs={{0,2},{2,0},{1,3},{3,1},{4,6},{6,4},{5,7},{7,5},{8,10},{10,8},{9,1... | collective-permute-start | bytes 1572872 | tf_op jit(solution)/shard_map/ppermute | solution.py:661
  138.0 44.0 %collective-permute-start.15 = (bf16[512,512]{1,0:T(8,128)(2,1)S(1)}, bf16[512,512]{1,0:T(8,128)(2,1)}, u32[]{:S(2)}, u32[]{:S(2)}) collective-permute-start(bf16[512,512]{1,0:T(8,128)(2,1)S(1)} %add_convert_fusion.2), channel_id=1, source_target_pairs={{0,1},{1,0},{2,3},{3,2},{4,5},{5,4},{6,7},{7,6},{8,9},{9,8},{10,11... | collective-permute-start | bytes 1572872 | tf_op jit(solution)/shard_map/ppermute | solution.py:657
  182.0 1.2 copy-start
  182.0 4.2 %slice-start = ((f32[8,2048]{1,0:T(8,128)}), f32[1,2048]{1,0:T(1,128)S(1)}, s32[]{:S(2)}) async-start(f32[8,2048]{1,0:T(8,128)} %add.132.refs_5_), calls=%async_computation.6 | async-start | bytes 16384 | tf_op jit(solution)/shard_map/slice | solution.py:1123
  182.0 4.2 %copy-start.21 = (f32[16,1024]{1,0:T(8,128)S(1)}, f32[16,1024]{1,0:T(8,128)}, u32[]{:S(2)}) copy-start(f32[16,1024]{1,0:T(8,128)} %get-tuple-element.213) | copy-start | bytes 196612
  183.5 23.0 %collective-permute-start.20 = (bf16[1024,512]{1,0:T(8,128)(2,1)}, bf16[1024,512]{1,0:T(8,128)(2,1)}, u32[]{:S(2)}, u32[]{:S(2)}) collective-permute-start(bf16[1024,512]{1,0:T(8,128)(2,1)} %get-tuple-element.214), channel_id=1, source_target_pairs={{0,1},{1,0},{2,3},{3,2},{4,5},{5,4},{6,7},{7,6},{8,9},{9,8},{10,11... | collective-permute-start | bytes 3145736 | tf_op jit(solution)/shard_map/ppermute | solution.py:657
  184.7 21.8 %collective-permute-start.21 = (bf16[1024,512]{1,0:T(8,128)(2,1)}, bf16[1024,512]{1,0:T(8,128)(2,1)}, u32[]{:S(2)}, u32[]{:S(2)}) collective-permute-start(bf16[1024,512]{1,0:T(8,128)(2,1)} %get-tuple-element.215), channel_id=1, source_target_pairs={{0,2},{2,0},{1,3},{3,1},{4,6},{6,4},{5,7},{7,5},{8,10},{10,8},{9,1... | collective-permute-start | bytes 3145736 | tf_op jit(solution)/shard_map/ppermute | solution.py:661
  186.3 4.8 %copy-start.15 = (bf16[128,1024]{1,0:T(8,128)(2,1)S(1)}, bf16[128,1024]{1,0:T(8,128)(2,1)}, u32[]{:S(2)}) copy-start(bf16[128,1024]{1,0:T(8,128)(2,1)} %reduce-scatter.3.cloned.1.call-done) | copy-start | bytes 786436
  186.3 1.5 collective-permute-start.16
  187.8 5.2 %collective-permute-start.17 = (f32[16,1024]{1,0:T(8,128)S(1)}, f32[16,1024]{1,0:T(8,128)S(1)}, u32[]{:S(2)}, u32[]{:S(2)}) collective-permute-start(f32[16,1024]{1,0:T(8,128)S(1)} %add.145), channel_id=1, source_target_pairs={{0,8},{4,12},{8,0},{12,4},{16,24},{20,28},{24,16},{28,20},{1,9},{5... | collective-permute-start | bytes 196616 | tf_op jit(solution)/shard_map/ppermute | solution.py:706
  193.0 9.1 %collective-permute-start.18 = (f32[16,1024]{1,0:T(8,128)S(1)}, f32[16,1024]{1,0:T(8,128)S(1)}, u32[]{:S(2)}, u32[]{:S(2)}) collective-permute-start(f32[16,1024]{1,0:T(8,128)S(1)} %add.146), channel_id=1, source_target_pairs={{0,16},{4,20},{8,24},{12,28},{16,0},{20,4},{24,8},{28,12},{1,17},{... | collective-permute-start | bytes 196616 | tf_op jit(solution)/shard_map/ppermute | solution.py:706
  202.2 4.3 %collective-permute-start.19 = (f32[16,1024]{1,0:T(8,128)S(1)}, f32[16,1024]{1,0:T(8,128)S(1)}, u32[]{:S(2)}, u32[]{:S(2)}) collective-permute-start(f32[16,1024]{1,0:T(8,128)S(1)} %add.147), channel_id=1, source_target_pairs={{0,1},{1,0},{2,3},{3,2},{4,5},{5,4},{6,7},{7,6},{8,9},{9,8},{10,11... | collective-permute-start | bytes 196616 | tf_op jit(solution)/shard_map/ppermute | solution.py:657
  202.3 6.1 %copy-start.9 = (bf16[1024,512]{1,0:T(8,128)(2,1)S(1)}, bf16[1024,512]{1,0:T(8,128)(2,1)}, u32[]{:S(2)}) copy-start(bf16[1024,512]{1,0:T(8,128)(2,1)} %get-tuple-element.212) | copy-start | bytes 3145732
  206.5 4.3 %collective-permute-start.22 = (f32[16,1024]{1,0:T(8,128)S(1)}, f32[16,1024]{1,0:T(8,128)S(1)}, u32[]{:S(2)}, u32[]{:S(2)}) collective-permute-start(f32[16,1024]{1,0:T(8,128)S(1)} %add.148), channel_id=1, source_target_pairs={{0,2},{2,0},{1,3},{3,1},{4,6},{6,4},{5,7},{7,5},{8,10},{10,8},{9,1... | collective-permute-start | bytes 196616 | tf_op jit(solution)/shard_map/ppermute | solution.py:661
  210.9 11.9 %collective-permute-start.23 = (bf16[512,512]{1,0:T(8,128)(2,1)S(1)}, bf16[512,512]{1,0:T(8,128)(2,1)}, u32[]{:S(2)}, u32[]{:S(2)}) collective-permute-start(bf16[512,512]{1,0:T(8,128)(2,1)S(1)} %add_convert_fusion.1), channel_id=1, source_target_pairs={{0,2},{2,0},{1,3},{3,1},{4,6},{6,4},{5,7},{7,5},{8,10},{10,8},{9,1... | collective-permute-start | bytes 1572872 | tf_op jit(solution)/shard_map/ppermute | solution.py:661
  211.4 11.9 %collective-permute-start.24 = (bf16[512,512]{1,0:T(8,128)(2,1)S(1)}, bf16[512,512]{1,0:T(8,128)(2,1)}, u32[]{:S(2)}, u32[]{:S(2)}) collective-permute-start(bf16[512,512]{1,0:T(8,128)(2,1)S(1)} %add_convert_fusion), channel_id=1, source_target_pairs={{0,1},{1,0},{2,3},{3,2},{4,5},{5,4},{6,7},{7,6},{8,9},{9,8},{10,11... | collective-permute-start | bytes 1572872 | tf_op jit(solution)/shard_map/ppermute | solution.py:657
  223.3 3.7 %copy-start.10 = (bf16[1024,512]{1,0:T(8,128)(2,1)S(1)}, bf16[1024,512]{1,0:T(8,128)(2,1)}, u32[]{:S(2)}) copy-start(bf16[1024,512]{1,0:T(8,128)(2,1)} %get-tuple-element.212) | copy-start | bytes 3145732
  224.3 4.1 %copy-start.18 = (bf16[128,896]{1,0:T(8,128)(2,1)S(1)}, bf16[128,896]{1,0:T(8,128)(2,1)}, u32[]{:S(2)}) copy-start(bf16[128,896]{1,0:T(8,128)(2,1)} %reduce-scatter.5.cloned.1.call-done) | copy-start | bytes 688132
  224.3 4.8 %collective-permute-start.25 = (bf16[128,384]{1,0:T(8,128)(2,1)S(1)}, bf16[128,384]{1,0:T(8,128)(2,1)S(1)}, u32[]{:S(2)}, u32[]{:S(2)}) collective-permute-start(bf16[128,384]{1,0:T(8,128)(2,1)S(1)} %slice.136), channel_id=1, source_target_pairs={{0,1},{1,0},{2,3},{3,2},{4,5},{5,4},{6,7},{7,6},{8,9},{9,8},{10,11... | collective-permute-start | bytes 294920 | tf_op jit(solution)/shard_map/ppermute | solution.py:657
  227.0 3.5 %copy-start.20 = (f32[1,1024]{1,0:T(1,128)S(1)}, f32[1,1024]{1,0:T(1,128)}, u32[]{:S(2)}) copy-start(f32[1,1024]{1,0:T(1,128)} %get-tuple-element.136.refs_8_.refs_1_) | copy-start | bytes 12292
  228.4 2.6 %copy-start.2 = (bf16[512,1024]{1,0:T(8,128)(2,1)S(1)}, bf16[512,1024]{1,0:T(8,128)(2,1)}, u32[]{:S(2)}) copy-start(bf16[512,1024]{1,0:T(8,128)(2,1)} %refs_0_.3) | copy-start | bytes 3145732
  229.2 4.7 %collective-permute-start.26 = (bf16[128,384]{1,0:T(8,128)(2,1)S(1)}, bf16[128,384]{1,0:T(8,128)(2,1)S(1)}, u32[]{:S(2)}, u32[]{:S(2)}) collective-permute-start(bf16[128,384]{1,0:T(8,128)(2,1)S(1)} %add_convert_fusion.4), channel_id=1, source_target_pairs={{0,2},{2,0},{1,3},{3,1},{4,6},{6,4},{5,7},{7,5},{8,10},{10,8},{9,1... | collective-permute-start | bytes 294920 | tf_op jit(solution)/shard_map/ppermute | solution.py:661
Sparse Core Ops, SparseCore 0:
  10.3 39.0 all-gather.2
  51.6 20.9 all-gather.4
  136.0 34.9 reduce-scatter.2
  182.2 37.7 reduce-scatter.4
